TPU v7x, 256 devices: a whole 4x4x8 slice. The times are simulated.
256 devices in a mesh: region: 8 (over x, y_hi), slab: 32 (over z, y_lo, core).
Axes of the slice: x: 4, y: 4 (y_hi: 2, y_lo: 2; y = y_hi * 2 + y_lo), z: 8, core: 2. Of those that a mesh axis runs over, the one named last changes fastest.
Arguments:
- nodes: bfloat16 [32768, 256], P(('region', 'slab')), may hold values from -6 to 6
- edge_feats: bfloat16 [163840, 256], P(('region', 'slab')), may hold values from -6 to 6
- cotangent: float32 [32768, 256], P(('region', 'slab')), may hold values from -6 to 6
- edge_w1: bfloat16 [768, 256], replicated, may hold values from -0.21875 to 0.21875
- edge_w2: bfloat16 [256, 256], replicated, may hold values from -0.375 to 0.375
- node_w1: bfloat16 [512, 256], replicated, may hold values from -0.25 to 0.25
- node_w2: bfloat16 [256, 256], replicated, may hold values from -0.375 to 0.375
- ln_gain: float32 [256], replicated, may hold values from 0.1 to 1.9
- senders: int32 [163840], P(('region', 'slab')), may hold values from 0 to 255
- receivers: int32 [163840], P(('region', 'slab')), may hold values from 0 to 127
- send_rows: int32 [1024, 32], P(('region', 'slab')), may hold values from 0 to 127
- edge_count: int32 [8, 32], P('region', 'slab'), may hold values from 160 to 640, as said below
Outputs:
- node_grad: float32 [32768, 256], P(('region', 'slab'))
- edge_grad: float32 [163840, 256], P(('region', 'slab'))
- grad_edge_in: float32 [768, 256], replicated
- grad_edge_out: float32 [256, 256], replicated
- grad_node_in: float32 [512, 256], replicated
- grad_node_out: float32 [256, 256], replicated
- grad_gain: float32 [256], replicated
Inputs may be any that keep to these rules, and one draw needn't show every extreme that they name: `senders`: index into the device's 128 own rows followed by its 128 halo rows. `receivers`: index into the device's own rows. `send_rows`: index into the device's own rows. `edge_count`: slots below it are live, the rest padding; some device has all 640 slots live.
All inputs are finite; a program needn't handle non-finite values.
Results may differ from a plain program's by a relative error of at most 0.019.
Values may be sent and summed in bfloat16 or wider, within the bound.
No kernel may reach another device: no remote copies, remote signals or barrier semaphores. Data moves between devices by JAX's collectives and lax.ppermute only.
A program may use at most 64 MiB of HBM per device.

v0:
```python
import jax
import jax.numpy as jnp
from jax import lax
from jax.sharding import PartitionSpec as P

STEPS = 4


EPS = 1e-05


def with_halo(value, sides, width):
    for axis, dim in sides:
        size, length = (lax.axis_size(axis), value.shape[dim])
        up = [(i, (i + 1) % size) for i in range(size)]
        down = [(j, i) for i, j in up]
        last = lax.slice_in_dim(value, length - width, length, axis=dim)
        first = lax.slice_in_dim(value, 0, width, axis=dim)
        before = lax.ppermute(last, axis, up)
        after = lax.ppermute(first, axis, down)
        value = jnp.concatenate([before, value, after], axis=dim)
    return value


def silu_slope(pre):
    sig = jax.nn.sigmoid(pre)
    return sig * (1.0 + pre * (1.0 - sig))


def edge_forward(extended, own_rows, edges, send_idx, recv_idx, live_mask, edge_w1, edge_w2):
    stacked = jnp.concatenate([extended[send_idx], own_rows[recv_idx], edges], axis=1)
    pre_edge = jnp.dot(stacked, edge_w1, preferred_element_type=jnp.float32)
    hidden_edge = jax.nn.silu(pre_edge).astype(jnp.bfloat16)
    message = jnp.dot(hidden_edge, edge_w2, preferred_element_type=jnp.float32) * live_mask[:, None]
    summed = jax.ops.segment_sum(message, recv_idx, num_segments=own_rows.shape[0])
    return (stacked, pre_edge, hidden_edge, summed)


def node_parts(own_rows, summed, node_w1, node_w2):
    joined = jnp.concatenate([own_rows, summed.astype(jnp.bfloat16)], axis=1)
    pre_node = jnp.dot(joined, node_w1, preferred_element_type=jnp.float32)
    hidden_node = jax.nn.silu(pre_node).astype(jnp.bfloat16)
    update = jnp.dot(hidden_node, node_w2, preferred_element_type=jnp.float32)
    centre = update - jnp.mean(update, axis=-1, keepdims=True)
    inv_dev = lax.rsqrt(jnp.mean(centre * centre, axis=-1, keepdims=True) + EPS)
    return (joined, pre_node, hidden_node, centre * inv_dev, inv_dev)


def node_forward(own_rows, summed, node_w1, node_w2, ln_gain):
    normed = node_parts(own_rows, summed, node_w1, node_w2)[3]
    return (own_rows.astype(jnp.float32) + normed * ln_gain).astype(jnp.bfloat16)


def local_backward(extended, edges, send_idx, recv_idx, live_mask, upstream, weights):
    edge_w1, edge_w2, node_w1, node_w2, ln_gain = weights
    own_count = upstream.shape[0]
    width = upstream.shape[1]
    own_rows = extended[:own_count]
    stacked, pre_edge, hidden_edge, summed = edge_forward(
        extended, own_rows, edges, send_idx, recv_idx, live_mask, edge_w1, edge_w2
    )
    joined, pre_node, hidden_node, normed, inv_dev = node_parts(own_rows, summed, node_w1, node_w2)
    gain_term = jnp.sum(upstream * normed, axis=0)
    scaled = upstream * ln_gain
    grad_update = inv_dev * (
        scaled
        - jnp.mean(scaled, axis=-1, keepdims=True)
        - normed * jnp.mean(scaled * normed, axis=-1, keepdims=True)
    )
    grad_update = grad_update.astype(jnp.bfloat16)
    node_out_term = jnp.dot(hidden_node.T, grad_update, preferred_element_type=jnp.float32)
    grad_hidden = jnp.dot(grad_update, node_w2.T, preferred_element_type=jnp.float32)
    grad_pre_node = (grad_hidden * silu_slope(pre_node)).astype(jnp.bfloat16)
    node_in_term = jnp.dot(joined.T, grad_pre_node, preferred_element_type=jnp.float32)
    grad_joined = jnp.dot(grad_pre_node, node_w1.T, preferred_element_type=jnp.float32)
    grad_message = (grad_joined[:, width:][recv_idx] * live_mask[:, None]).astype(jnp.bfloat16)
    edge_out_term = jnp.dot(hidden_edge.T, grad_message, preferred_element_type=jnp.float32)
    grad_hidden_edge = jnp.dot(grad_message, edge_w2.T, preferred_element_type=jnp.float32)
    grad_pre_edge = (grad_hidden_edge * silu_slope(pre_edge)).astype(jnp.bfloat16)
    edge_in_term = jnp.dot(stacked.T, grad_pre_edge, preferred_element_type=jnp.float32)
    grad_stacked = jnp.dot(grad_pre_edge, edge_w1.T, preferred_element_type=jnp.float32)
    grad_extended = jax.ops.segment_sum(
        grad_stacked[:, :width], send_idx, num_segments=extended.shape[0]
    )
    grad_own = upstream + grad_joined[:, :width] + grad_extended[:own_count]
    grad_own = grad_own + jax.ops.segment_sum(
        grad_stacked[:, width : 2 * width], recv_idx, num_segments=own_count
    )
    terms = (edge_in_term, edge_out_term, node_in_term, node_out_term, gain_term)
    return (grad_own, grad_extended[own_count:], grad_stacked[:, 2 * width :], terms)


def gather_rims(states, send_lists):
    slab_pair = jnp.stack([states[send_lists[0]], states[send_lists[1]]])
    region_pair = jnp.stack([states[send_lists[2]], states[send_lists[3]]])
    slab_padded = with_halo(slab_pair, (("slab", 0),), 1)
    region_padded = with_halo(region_pair, (("region", 0),), 1)
    return jnp.concatenate(
        [states, slab_padded[0], slab_padded[3], region_padded[0], region_padded[3]], axis=0
    )


def return_rims(target, grad_halo, send_lists):
    block_rows = send_lists.shape[1]
    slab_pair = jnp.stack([grad_halo[:block_rows], grad_halo[block_rows : 2 * block_rows]])
    region_pair = jnp.stack(
        [grad_halo[2 * block_rows : 3 * block_rows], grad_halo[3 * block_rows :]]
    )
    slab_back = with_halo(slab_pair.astype(jnp.bfloat16), (("slab", 0),), 1).astype(slab_pair.dtype)
    region_back = with_halo(region_pair.astype(jnp.bfloat16), (("region", 0),), 1).astype(
        region_pair.dtype
    )
    target = target.at[send_lists[0]].add(slab_back[0]).at[send_lists[1]].add(slab_back[3])
    return target.at[send_lists[2]].add(region_back[0]).at[send_lists[3]].add(region_back[3])


def local(
    nodes,
    edge_feats,
    cotangent,
    edge_w1,
    edge_w2,
    node_w1,
    node_w2,
    ln_gain,
    senders,
    receivers,
    send_rows,
    edge_count,
):
    own_count = nodes.shape[0]
    width = nodes.shape[1]
    live_mask = (jnp.arange(edge_feats.shape[0], dtype=jnp.int32) < edge_count[0, 0]).astype(
        jnp.float32
    )
    weights = (edge_w1, edge_w2, node_w1, node_w2, ln_gain)
    extended_list = []
    states = nodes
    for layer_index in range(STEPS):
        extended = gather_rims(states, send_rows)
        extended_list.append(extended)
        if layer_index + 1 < STEPS:
            summed = edge_forward(
                extended, states, edge_feats, senders, receivers, live_mask, edge_w1, edge_w2
            )[3]
            states = node_forward(states, summed, node_w1, node_w2, ln_gain)
    upstream = cotangent
    edge_total = jnp.zeros(edge_feats.shape, jnp.float32)
    totals = (
        jnp.zeros((3 * width, width), jnp.float32),
        jnp.zeros((width, width), jnp.float32),
        jnp.zeros((2 * width, width), jnp.float32),
        jnp.zeros((width, width), jnp.float32),
        jnp.zeros((width,), jnp.float32),
    )
    for layer_index in reversed(range(STEPS)):
        grad_own, grad_halo, grad_edge, terms = local_backward(
            extended_list[layer_index], edge_feats, senders, receivers, live_mask, upstream, weights
        )
        terms = lax.psum((terms[0], terms[1], terms[2], terms[3], terms[4]), ("region", "slab"))
        totals = tuple((c + t for c, t in zip(totals, terms)))
        upstream = return_rims(grad_own, grad_halo, send_rows)
        edge_total = edge_total + grad_edge
    factor = float(own_count * lax.axis_size("region") * lax.axis_size("slab")) ** (-0.5)
    return (
        upstream,
        edge_total,
        totals[0] * factor,
        totals[1] * factor,
        totals[2] * factor,
        totals[3] * factor,
        totals[4] * factor,
    )


def solution(mesh):
    placed = (
        P(("region", "slab"), None),
        P(("region", "slab"), None),
        P(("region", "slab"), None),
        P(),
        P(),
        P(),
        P(),
        P(),
        P(("region", "slab")),
        P(("region", "slab")),
        P(("region", "slab"), None),
        P("region", "slab"),
    )
    return jax.shard_map(
        local,
        mesh=mesh,
        in_specs=placed,
        out_specs=(
            P(("region", "slab"), None),
            P(("region", "slab"), None),
            P(),
            P(),
            P(),
            P(),
            P(),
        ),
        check_vma=False,
    )
```

profile of v0, /device:TPU:1, one launch (start us, length us, event | category | flops | bytes accessed | tf_op | source)
XLA Modules:
  0.0 584.7 jit_solution(1992018297700356619)
XLA Ops:
  9.6 3.8 collective-permute-start.2
  26.1 2.8 gather_fusion.5
  34.5 5.7 scatter_custom_fusion
  45.3 2.8 gather_fusion.11
  48.0 2.9 collective-permute-start.5
  51.7 4.6 collective-permute-start.7
  62.8 5.7 scatter_custom_fusion.1
  74.9 5.1 collective-permute-start.9
  81.7 4.0 collective-permute-start.11
  91.2 5.7 scatter_custom_fusion.2
  104.2 5.0 collective-permute-start.13
  110.9 3.9 collective-permute-start.15
  115.7 3.3 gather_fusion.22
  122.4 6.0 %scatter_custom_fusion.3 = f32[128,256]{1,0:T(8,128)S(1)} fusion(s32[640]{0:T(1024)} %param.21, f32[640,256]{1,0:T(8,128)} %convolution_multiply_fusion.4, f32[]{:T(128)} %constant.48.clone.1), kind=kCustom, calls=%fused_computation.211 | custom fusion | flops 163840 | bytes 131584 | tf_op jit(solution)/shard_map/scatter-add | solution.py:35
  138.9 7.0 %scatter_custom_fusion.4 = f32[256,256]{1,0:T(8,128)} fusion(s32[640]{0:T(1024)} %param.20, f32[640,768]{1,0:T(8,128)S(1)} %fusion.164, f32[]{:T(128)} %constant.48.clone.1), kind=kCustom, calls=%fused_computation.105 | custom fusion | flops 163840 | bytes 918016 | tf_op jit(solution)/shard_map/scatter-add | solution.py:82
  154.4 5.6 collective-permute-start.17
  161.9 7.3 %scatter_custom_fusion.5 = f32[128,256]{1,0:T(8,128)} fusion(f32[128,256]{1,0:T(8,128)} %slice_add_fusion.9, s32[640]{0:T(1024)} %param.21, f32[640,768]{1,0:T(8,128)S(1)} %fusion.164), kind=kCustom, calls=%fused_computation.103 | custom fusion | flops 163840 | bytes 786432 | tf_op jit(solution)/shard_map/scatter-add | solution.py:86
  186.3 2.9 gather_fusion.25
  195.3 6.4 %scatter_custom_fusion.10 = f32[256,256]{1,0:T(8,128)S(1)} fusion(s32[640]{0:T(1024)} %param.20, f32[640,768]{1,0:T(8,128)} %fusion.166, f32[]{:T(128)} %constant.48.clone.1), kind=kCustom, calls=%fused_computation.101 | custom fusion | flops 163840 | bytes 918016 | tf_op jit(solution)/shard_map/scatter-add | solution.py:82
  202.6 4.3 collective-permute-start.23
  210.4 8.1 %scatter_custom_fusion.11 = f32[128,256]{1,0:T(8,128)} fusion(f32[128,256]{1,0:T(8,128)} %slice_add_fusion.7, s32[640]{0:T(1024)} %param.21, f32[640,768]{1,0:T(8,128)} %fusion.166), kind=kCustom, calls=%fused_computation.99 | custom fusion | flops 163840 | bytes 786432 | tf_op jit(solution)/shard_map/scatter-add | solution.py:86
  242.9 7.0 %scatter_custom_fusion.16 = f32[256,256]{1,0:T(8,128)} fusion(s32[640]{0:T(1024)} %param.20, f32[640,768]{1,0:T(8,128)} %fusion.168, f32[]{:T(128)} %constant.48.clone.1), kind=kCustom, calls=%fused_computation.97 | custom fusion | flops 163840 | bytes 918016 | tf_op jit(solution)/shard_map/scatter-add | solution.py:82
  251.5 5.1 collective-permute-start.27
  256.6 3.0 collective-permute-start.25
  261.2 8.1 %scatter_custom_fusion.17 = f32[128,256]{1,0:T(8,128)} fusion(f32[128,256]{1,0:T(8,128)} %slice_add_fusion.5, s32[640]{0:T(1024)} %param.21, f32[640,768]{1,0:T(8,128)} %fusion.168), kind=kCustom, calls=%fused_computation.95 | custom fusion | flops 163840 | bytes 786432 | tf_op jit(solution)/shard_map/scatter-add | solution.py:86
  286.6 2.9 gather_fusion.27
  295.7 6.5 %scatter_custom_fusion.22 = f32[256,256]{1,0:T(8,128)S(1)} fusion(s32[640]{0:T(1024)} %param.20, f32[640,768]{1,0:T(8,128)} %fusion.170, f32[]{:T(128)} %constant.48.clone.1), kind=kCustom, calls=%fused_computation.93 | custom fusion | flops 163840 | bytes 918016 | tf_op jit(solution)/shard_map/scatter-add | solution.py:82
  302.3 5.3 collective-permute-start.31
  307.6 3.9 collective-permute-start.29
  311.6 79.2 %psum.174 = f32[256]{0:T(256)S(1)} all-reduce(f32[256]{0:T(256)S(1)} %add_add_fusion), channel_id=1, replica_groups=mesh['region'=8,'slab'=32] {'region','slab'}, use_global_device_ids=true, to_apply=%region_61.62 | all-reduce | flops 256 | bytes 2048 | tf_op jit(solution)/shard_map/psum | solution.py:160
  394.0 6.2 %scatter_custom_fusion.23 = f32[128,256]{1,0:T(8,128)S(1)} fusion(f32[128,256]{1,0:T(8,128)S(1)} %slice_add_fusion.3, s32[640]{0:T(1024)} %param.21, f32[640,768]{1,0:T(8,128)} %fusion.170), kind=kCustom, calls=%fused_computation.91 | custom fusion | flops 163840 | bytes 786432 | tf_op jit(solution)/shard_map/scatter-add | solution.py:86
  404.1 167.8 %all-reduce.3.cloned.1.call-done = (f32[768,256]{1,0:T(8,128)}, f32[256,256]{1,0:T(8,128)}, f32[512,256]{1,0:T(8,128)}, f32[256,256]{1,0:T(8,128)}) async-done(((f32[768,256]{1,0:T(8,128)}, f32[256,256]{1,0:T(8,128)}, f32[512,256]{1,0:T(8,128)}, f32[256,256]{1,0:T(8,128)}), (f32[768,256]{1,0:T(8,128)}, f32[256,256]{1,0:T(8,128)}, f32[512,256]{1,0:T(8,128)}, ...) | async-done | bytes 1835024 | tf_op jit(solution)/shard_map/psum | solution.py:160
  (387 shorter events, 170.3 us)
Async XLA Ops:
  7.2 564.8 %all-reduce.3.cloned.1.call-start = ((), (), s32[]{:S(2)}) async-start(), calls=%async_computation | async-start | bytes 3670016 | tf_op jit(solution)/shard_map/psum | solution.py:160
  9.6 19.4 %collective-permute-start.2 = (bf16[1,32,256]{2,1,0:T(8,128)(2,1)S(1)}, bf16[1,32,256]{2,1,0:T(8,128)(2,1)S(1)}, u32[]{:S(2)}, u32[]{:S(2)}) collective-permute-start(bf16[1,32,256]{2,1,0:T(8,128)(2,1)S(1)} %bitcast.213), channel_id=1, source_target_pairs={{0,32},{32,64},{64,96},{96,128},{128,160},{160,192},{192,224},{224... | collective-permute-start | bytes 49160 | tf_op jit(solution)/shard_map/ppermute | solution.py:19
  14.9 14.1 %collective-permute-start.3 = (bf16[1,32,256]{2,1,0:T(8,128)(2,1)S(1)}, bf16[1,32,256]{2,1,0:T(8,128)(2,1)S(1)}, u32[]{:S(2)}, u32[]{:S(2)}) collective-permute-start(bf16[1,32,256]{2,1,0:T(8,128)(2,1)S(1)} %bitcast.212), channel_id=1, source_target_pairs={{32,0},{64,32},{96,64},{128,96},{160,128},{192,160},{224,192},{0,2... | collective-permute-start | bytes 49160 | tf_op jit(solution)/shard_map/ppermute | solution.py:20
  18.6 10.3 %collective-permute-start = (bf16[1,32,256]{2,1,0:T(8,128)(2,1)S(1)}, bf16[1,32,256]{2,1,0:T(8,128)(2,1)S(1)}, u32[]{:S(2)}, u32[]{:S(2)}) collective-permute-start(bf16[1,32,256]{2,1,0:T(8,128)(2,1)S(1)} %bitcast.223), channel_id=1, source_target_pairs={{0,1},{1,2},{2,3},{3,4},{4,5},{5,6},{6,7},{7,8},{8,9},{9,10},{10,1... | collective-permute-start | bytes 49160 | tf_op jit(solution)/shard_map/ppermute | solution.py:19
  22.5 6.4 %collective-permute-start.1 = (bf16[1,32,256]{2,1,0:T(8,128)(2,1)S(1)}, bf16[1,32,256]{2,1,0:T(8,128)(2,1)S(1)}, u32[]{:S(2)}, u32[]{:S(2)}) collective-permute-start(bf16[1,32,256]{2,1,0:T(8,128)(2,1)S(1)} %bitcast.221), channel_id=1, source_target_pairs={{1,0},{2,1},{3,2},{4,3},{5,4},{6,5},{7,6},{8,7},{9,8},{10,9},{11,1... | collective-permute-start | bytes 49160 | tf_op jit(solution)/shard_map/ppermute | solution.py:20
  42.1 14.1 %collective-permute-start.4 = (bf16[1,32,256]{2,1,0:T(8,128)(2,1)S(1)}, bf16[1,32,256]{2,1,0:T(8,128)(2,1)S(1)}, u32[]{:S(2)}, u32[]{:S(2)}) collective-permute-start(bf16[1,32,256]{2,1,0:T(8,128)(2,1)S(1)} %bitcast.226), channel_id=1, source_target_pairs={{0,1},{1,2},{2,3},{3,4},{4,5},{5,6},{6,7},{7,8},{8,9},{9,10},{10,1... | collective-permute-start | bytes 49160 | tf_op jit(solution)/shard_map/ppermute | solution.py:19
  48.0 8.2 %collective-permute-start.5 = (bf16[1,32,256]{2,1,0:T(8,128)(2,1)S(1)}, bf16[1,32,256]{2,1,0:T(8,128)(2,1)S(1)}, u32[]{:S(2)}, u32[]{:S(2)}) collective-permute-start(bf16[1,32,256]{2,1,0:T(8,128)(2,1)S(1)} %bitcast.224), channel_id=1, source_target_pairs={{1,0},{2,1},{3,2},{4,3},{5,4},{6,5},{7,6},{8,7},{9,8},{10,9},{11,1... | collective-permute-start | bytes 49160 | tf_op jit(solution)/shard_map/ppermute | solution.py:20
  51.0 6.4 %collective-permute-start.6 = (bf16[1,32,256]{2,1,0:T(8,128)(2,1)S(1)}, bf16[1,32,256]{2,1,0:T(8,128)(2,1)S(1)}, u32[]{:S(2)}, u32[]{:S(2)}) collective-permute-start(bf16[1,32,256]{2,1,0:T(8,128)(2,1)S(1)} %bitcast.218), channel_id=1, source_target_pairs={{0,32},{32,64},{64,96},{96,128},{128,160},{160,192},{192,224},{224... | collective-permute-start | bytes 49160 | tf_op jit(solution)/shard_map/ppermute | solution.py:19
  51.7 5.7 collective-permute-start.7
  70.2 15.6 %collective-permute-start.8 = (bf16[1,32,256]{2,1,0:T(8,128)(2,1)S(1)}, bf16[1,32,256]{2,1,0:T(8,128)(2,1)S(1)}, u32[]{:S(2)}, u32[]{:S(2)}) collective-permute-start(bf16[1,32,256]{2,1,0:T(8,128)(2,1)S(1)} %bitcast.227), channel_id=1, source_target_pairs={{0,1},{1,2},{2,3},{3,4},{4,5},{5,6},{6,7},{7,8},{8,9},{9,10},{10,1... | collective-permute-start | bytes 49160 | tf_op jit(solution)/shard_map/ppermute | solution.py:19
  74.9 10.8 %collective-permute-start.9 = (bf16[1,32,256]{2,1,0:T(8,128)(2,1)S(1)}, bf16[1,32,256]{2,1,0:T(8,128)(2,1)S(1)}, u32[]{:S(2)}, u32[]{:S(2)}) collective-permute-start(bf16[1,32,256]{2,1,0:T(8,128)(2,1)S(1)} %bitcast.225), channel_id=1, source_target_pairs={{1,0},{2,1},{3,2},{4,3},{5,4},{6,5},{7,6},{8,7},{9,8},{10,9},{11,1... | collective-permute-start | bytes 49160 | tf_op jit(solution)/shard_map/ppermute | solution.py:20
  80.0 6.5 %collective-permute-start.10 = (bf16[1,32,256]{2,1,0:T(8,128)(2,1)S(1)}, bf16[1,32,256]{2,1,0:T(8,128)(2,1)S(1)}, u32[]{:S(2)}, u32[]{:S(2)}) collective-permute-start(bf16[1,32,256]{2,1,0:T(8,128)(2,1)S(1)} %bitcast.219), channel_id=1, source_target_pairs={{0,32},{32,64},{64,96},{96,128},{128,160},{160,192},{192,224},{224... | collective-permute-start | bytes 49160 | tf_op jit(solution)/shard_map/ppermute | solution.py:19
  99.2 15.6 %collective-permute-start.12 = (bf16[1,32,256]{2,1,0:T(8,128)(2,1)S(1)}, bf16[1,32,256]{2,1,0:T(8,128)(2,1)S(1)}, u32[]{:S(2)}, u32[]{:S(2)}) collective-permute-start(bf16[1,32,256]{2,1,0:T(8,128)(2,1)S(1)} %bitcast.220), channel_id=1, source_target_pairs={{0,1},{1,2},{2,3},{3,4},{4,5},{5,6},{6,7},{7,8},{8,9},{9,10},{10,1... | collective-permute-start | bytes 49160 | tf_op jit(solution)/shard_map/ppermute | solution.py:19
  104.2 10.6 %collective-permute-start.13 = (bf16[1,32,256]{2,1,0:T(8,128)(2,1)S(1)}, bf16[1,32,256]{2,1,0:T(8,128)(2,1)S(1)}, u32[]{:S(2)}, u32[]{:S(2)}) collective-permute-start(bf16[1,32,256]{2,1,0:T(8,128)(2,1)S(1)} %bitcast.222), channel_id=1, source_target_pairs={{1,0},{2,1},{3,2},{4,3},{5,4},{6,5},{7,6},{8,7},{9,8},{10,9},{11,1... | collective-permute-start | bytes 49160 | tf_op jit(solution)/shard_map/ppermute | solution.py:20
  109.2 6.6 %collective-permute-start.14 = (bf16[1,32,256]{2,1,0:T(8,128)(2,1)S(1)}, bf16[1,32,256]{2,1,0:T(8,128)(2,1)S(1)}, u32[]{:S(2)}, u32[]{:S(2)}) collective-permute-start(bf16[1,32,256]{2,1,0:T(8,128)(2,1)S(1)} %bitcast.217), channel_id=1, source_target_pairs={{0,32},{32,64},{64,96},{96,128},{128,160},{160,192},{192,224},{224... | collective-permute-start | bytes 49160 | tf_op jit(solution)/shard_map/ppermute | solution.py:19
  110.9 4.9 collective-permute-start.15
  149.2 24.9 %collective-permute-start.18 = (bf16[1,32,256]{2,1,0:T(8,128)(2,1)}, bf16[1,32,256]{2,1,0:T(8,128)(2,1)}, u32[]{:S(2)}, u32[]{:S(2)}) collective-permute-start(bf16[1,32,256]{2,1,0:T(8,128)(2,1)} %get-tuple-element.41), channel_id=1, source_target_pairs={{0,32},{32,64},{64,96},{96,128},{128,160},{160,192},{192,224},{224... | collective-permute-start | bytes 49160 | tf_op jit(solution)/shard_map/ppermute | solution.py:19
  151.6 22.5 %collective-permute-start.19 = (bf16[1,32,256]{2,1,0:T(8,128)(2,1)}, bf16[1,32,256]{2,1,0:T(8,128)(2,1)}, u32[]{:S(2)}, u32[]{:S(2)}) collective-permute-start(bf16[1,32,256]{2,1,0:T(8,128)(2,1)} %get-tuple-element.42), channel_id=1, source_target_pairs={{32,0},{64,32},{96,64},{128,96},{160,128},{192,160},{224,192},{0,2... | collective-permute-start | bytes 49160 | tf_op jit(solution)/shard_map/ppermute | solution.py:20
  154.4 14.8 %collective-permute-start.17 = (bf16[1,32,256]{2,1,0:T(8,128)(2,1)}, bf16[1,32,256]{2,1,0:T(8,128)(2,1)}, u32[]{:S(2)}, u32[]{:S(2)}) collective-permute-start(bf16[1,32,256]{2,1,0:T(8,128)(2,1)} %get-tuple-element.43), channel_id=1, source_target_pairs={{1,0},{2,1},{3,2},{4,3},{5,4},{6,5},{7,6},{8,7},{9,8},{10,9},{11,1... | collective-permute-start | bytes 49160 | tf_op jit(solution)/shard_map/ppermute | solution.py:20
  160.0 9.1 %collective-permute-start.16 = (bf16[1,32,256]{2,1,0:T(8,128)(2,1)}, bf16[1,32,256]{2,1,0:T(8,128)(2,1)}, u32[]{:S(2)}, u32[]{:S(2)}) collective-permute-start(bf16[1,32,256]{2,1,0:T(8,128)(2,1)} %get-tuple-element.44), channel_id=1, source_target_pairs={{0,1},{1,2},{2,3},{3,4},{4,5},{5,6},{6,7},{7,8},{8,9},{9,10},{10,1... | collective-permute-start | bytes 49160 | tf_op jit(solution)/shard_map/ppermute | solution.py:19
  201.8 21.7 %collective-permute-start.22 = (bf16[1,32,256]{2,1,0:T(8,128)(2,1)S(1)}, bf16[1,32,256]{2,1,0:T(8,128)(2,1)}, u32[]{:S(2)}, u32[]{:S(2)}) collective-permute-start(bf16[1,32,256]{2,1,0:T(8,128)(2,1)S(1)} %get-tuple-element.37), channel_id=1, source_target_pairs={{0,32},{32,64},{64,96},{96,128},{128,160},{160,192},{192,224},{224... | collective-permute-start | bytes 49160 | tf_op jit(solution)/shard_map/ppermute | solution.py:19
  202.6 20.9 %collective-permute-start.23 = (bf16[1,32,256]{2,1,0:T(8,128)(2,1)S(1)}, bf16[1,32,256]{2,1,0:T(8,128)(2,1)}, u32[]{:S(2)}, u32[]{:S(2)}) collective-permute-start(bf16[1,32,256]{2,1,0:T(8,128)(2,1)S(1)} %get-tuple-element.38), channel_id=1, source_target_pairs={{32,0},{64,32},{96,64},{128,96},{160,128},{192,160},{224,192},{0,2... | collective-permute-start | bytes 49160 | tf_op jit(solution)/shard_map/ppermute | solution.py:20
  206.9 11.6 %collective-permute-start.21 = (bf16[1,32,256]{2,1,0:T(8,128)(2,1)S(1)}, bf16[1,32,256]{2,1,0:T(8,128)(2,1)}, u32[]{:S(2)}, u32[]{:S(2)}) collective-permute-start(bf16[1,32,256]{2,1,0:T(8,128)(2,1)S(1)} %get-tuple-element.39), channel_id=1, source_target_pairs={{1,0},{2,1},{3,2},{4,3},{5,4},{6,5},{7,6},{8,7},{9,8},{10,9},{11,1... | collective-permute-start | bytes 49160 | tf_op jit(solution)/shard_map/ppermute | solution.py:20
  208.2 10.4 %collective-permute-start.20 = (bf16[1,32,256]{2,1,0:T(8,128)(2,1)S(1)}, bf16[1,32,256]{2,1,0:T(8,128)(2,1)}, u32[]{:S(2)}, u32[]{:S(2)}) collective-permute-start(bf16[1,32,256]{2,1,0:T(8,128)(2,1)S(1)} %get-tuple-element.40), channel_id=1, source_target_pairs={{0,1},{1,2},{2,3},{3,4},{4,5},{5,6},{6,7},{7,8},{8,9},{9,10},{10,1... | collective-permute-start | bytes 49160 | tf_op jit(solution)/shard_map/ppermute | solution.py:19
  251.5 22.8 %collective-permute-start.26 = (bf16[1,32,256]{2,1,0:T(8,128)(2,1)}, bf16[1,32,256]{2,1,0:T(8,128)(2,1)}, u32[]{:S(2)}, u32[]{:S(2)}) collective-permute-start(bf16[1,32,256]{2,1,0:T(8,128)(2,1)} %get-tuple-element.33), channel_id=1, source_target_pairs={{0,32},{32,64},{64,96},{96,128},{128,160},{160,192},{192,224},{224... | collective-permute-start | bytes 49160 | tf_op jit(solution)/shard_map/ppermute | solution.py:19
  251.5 22.8 %collective-permute-start.27 = (bf16[1,32,256]{2,1,0:T(8,128)(2,1)}, bf16[1,32,256]{2,1,0:T(8,128)(2,1)}, u32[]{:S(2)}, u32[]{:S(2)}) collective-permute-start(bf16[1,32,256]{2,1,0:T(8,128)(2,1)} %get-tuple-element.34), channel_id=1, source_target_pairs={{32,0},{64,32},{96,64},{128,96},{160,128},{192,160},{224,192},{0,2... | collective-permute-start | bytes 49160 | tf_op jit(solution)/shard_map/ppermute | solution.py:20
  256.6 12.8 %collective-permute-start.25 = (bf16[1,32,256]{2,1,0:T(8,128)(2,1)}, bf16[1,32,256]{2,1,0:T(8,128)(2,1)}, u32[]{:S(2)}, u32[]{:S(2)}) collective-permute-start(bf16[1,32,256]{2,1,0:T(8,128)(2,1)} %get-tuple-element.35), channel_id=1, source_target_pairs={{1,0},{2,1},{3,2},{4,3},{5,4},{6,5},{7,6},{8,7},{9,8},{10,9},{11,1... | collective-permute-start | bytes 49160 | tf_op jit(solution)/shard_map/ppermute | solution.py:20
  259.5 9.8 %collective-permute-start.24 = (bf16[1,32,256]{2,1,0:T(8,128)(2,1)}, bf16[1,32,256]{2,1,0:T(8,128)(2,1)}, u32[]{:S(2)}, u32[]{:S(2)}) collective-permute-start(bf16[1,32,256]{2,1,0:T(8,128)(2,1)} %get-tuple-element.36), channel_id=1, source_target_pairs={{0,1},{1,2},{2,3},{3,4},{4,5},{5,6},{6,7},{7,8},{8,9},{9,10},{10,1... | collective-permute-start | bytes 49160 | tf_op jit(solution)/shard_map/ppermute | solution.py:19
  302.2 99.9 %collective-permute-start.30 = (bf16[1,32,256]{2,1,0:T(8,128)(2,1)S(1)}, bf16[1,32,256]{2,1,0:T(8,128)(2,1)S(1)}, u32[]{:S(2)}, u32[]{:S(2)}) collective-permute-start(bf16[1,32,256]{2,1,0:T(8,128)(2,1)S(1)} %get-tuple-element.29), channel_id=1, source_target_pairs={{0,32},{32,64},{64,96},{96,128},{128,160},{160,192},{192,224},{224... | collective-permute-start | bytes 49160 | tf_op jit(solution)/shard_map/ppermute | solution.py:19
  302.3 99.8 %collective-permute-start.31 = (bf16[1,32,256]{2,1,0:T(8,128)(2,1)S(1)}, bf16[1,32,256]{2,1,0:T(8,128)(2,1)S(1)}, u32[]{:S(2)}, u32[]{:S(2)}) collective-permute-start(bf16[1,32,256]{2,1,0:T(8,128)(2,1)S(1)} %get-tuple-element.30), channel_id=1, source_target_pairs={{32,0},{64,32},{96,64},{128,96},{160,128},{192,160},{224,192},{0,2... | collective-permute-start | bytes 49160 | tf_op jit(solution)/shard_map/ppermute | solution.py:20
  307.6 92.5 %collective-permute-start.29 = (bf16[1,32,256]{2,1,0:T(8,128)(2,1)S(1)}, bf16[1,32,256]{2,1,0:T(8,128)(2,1)S(1)}, u32[]{:S(2)}, u32[]{:S(2)}) collective-permute-start(bf16[1,32,256]{2,1,0:T(8,128)(2,1)S(1)} %get-tuple-element.31), channel_id=1, source_target_pairs={{1,0},{2,1},{3,2},{4,3},{5,4},{6,5},{7,6},{8,7},{9,8},{10,9},{11,1... | collective-permute-start | bytes 49160 | tf_op jit(solution)/shard_map/ppermute | solution.py:20
  311.5 88.6 %collective-permute-start.28 = (bf16[1,32,256]{2,1,0:T(8,128)(2,1)S(1)}, bf16[1,32,256]{2,1,0:T(8,128)(2,1)S(1)}, u32[]{:S(2)}, u32[]{:S(2)}) collective-permute-start(bf16[1,32,256]{2,1,0:T(8,128)(2,1)S(1)} %get-tuple-element.32), channel_id=1, source_target_pairs={{0,1},{1,2},{2,3},{3,4},{4,5},{5,6},{6,7},{7,8},{8,9},{9,10},{10,1... | collective-permute-start | bytes 49160 | tf_op jit(solution)/shard_map/ppermute | solution.py:19
  (77 other events, 1002.4 us)
Sparse Core Ops, SparseCore 0:
  311.7 260.2 all-reduce.2
where the time goes:
time: 596 us; the launch traced here: 585 us
  waiting for transfers between devices  171 us (29%)
  other arithmetic  141 us (24%)
  blocking collectives  79.2 us (13%)
  starting transfers between devices  75.5 us (13%)
  local copies, waits for them, and re-layouts  56.4 us (9%)
  matrix products  44.8 us (8%)
  between operations  16.7 us (3%)
    psum x1, waiting for transfers between devices, local(): lax.psum((terms[0], terms[1], terms[2], terms[3], terms[4]), ('region', '...  168 us
    psum x1, blocking collectives, local(): lax.psum((terms[0], terms[1], terms[2], terms[3], terms[4]), ('region', '...  79.2 us
    ppermute x16, starting transfers between devices, with_halo(): after = lax.ppermute(first, axis, down)  59.6 us
    scatter-add x4, other arithmetic, local_backward(): jax.ops.segment_sum(grad_stacked[:, width:2 * width], recv_idx, num_segme...  29.7 us
    scatter-add x4, other arithmetic, local_backward(): jax.ops.segment_sum(grad_stacked[:, :width], send_idx, num_segments=exten...  26.9 us
    scatter-add x4, other arithmetic, edge_forward(): jax.ops.segment_sum(message, recv_idx, num_segments=own_rows.shape[0])  23.1 us
    scatter-add x8, other arithmetic, return_rims(): target.at[send_lists[0]].add(slab_back[0]).at[send_lists[1]]  16.7 us
    scatter-add x8, other arithmetic, return_rims(): target.at[send_lists[2]].add(region_back[0]).at[send_lists[3]]  16.6 us
  transfers between devices with their start and end apart: 33, of which 5 were waited for; matrix products, arithmetic and copies ran while one was open for 14% of the time, Pallas kernels for 0%

commit v1 on v0

v1 whole, which is shorter than its diff:
```python
import jax
import jax.numpy as jnp
from jax import lax
from jax.experimental import pallas as pl
from jax.experimental.pallas import tpu as pltpu
from jax.sharding import Mesh
from jax.sharding import PartitionSpec as P

STEPS = 4
EPS = 1e-05
L = 256
OWN = 128
HALO = 32
BF16 = jnp.bfloat16
F32 = jnp.float32
AXES = ("x", "yh", "z", "yl", "c")
REGION = ("x", "yh")
SLAB = ("z", "yl", "c")
PLANE = ("x", "yh", "yl")
CHUNKS = 16
CHUNK_ROWS = 64


def mm(a, b):
    return jnp.dot(a, b, preferred_element_type=F32)


def mm_t(a, b):
    return lax.dot_general(a, b, (((0,), (0,)), ((), ())), preferred_element_type=F32)


def split(v):
    high = v.astype(BF16)
    low = (v - high.astype(F32)).astype(BF16)
    return high, low


def mm_split(v, w):
    high, low = split(v)
    return mm(high, w) + mm(low, w)


def sigmoid(v):
    return 0.5 * jnp.tanh(0.5 * v) + 0.5


def call(kernel, outs, *args, smem=0, **kw):
    specs = [pl.BlockSpec(memory_space=pltpu.SMEM)] * smem
    specs += [pl.BlockSpec(memory_space=pltpu.VMEM)] * (len(args) - smem)
    return pl.pallas_call(
        kernel,
        out_shape=[jax.ShapeDtypeStruct(s, d) for s, d in outs],
        in_specs=specs,
        out_specs=[pl.BlockSpec(memory_space=pltpu.VMEM)] * len(outs),
        compiler_params=pltpu.CompilerParams(vmem_limit_bytes=32 * 1024 * 1024),
        **kw,
    )(*args)


def slot_lists(place, lists):
    slab_odd = place[1] % 2
    region_odd = place[0] % 2
    a, b, c, d = (lists[i : i + 1, :] for i in range(4))
    return (
        jnp.where(region_odd == 1, d, c),
        jnp.where(region_odd == 1, c, d),
        jnp.where(slab_odd == 1, b, a),
        jnp.where(slab_odd == 1, a, b),
    )


def first_kernel(place, nodes, lists, s0, s1, s2, s3, spread):
    h = nodes[...]
    row = lax.broadcasted_iota(jnp.int32, (OWN, HALO), 0)
    for i, (idx, out) in enumerate(zip(slot_lists(place, lists[...]), (s0, s1, s2, s3))):
        hot = (row == idx).astype(F32).astype(BF16)
        spread[:, i * HALO : (i + 1) * HALO] = hot
        out[...] = mm_t(hot, h).astype(BF16)


def prep_kernel(
    place, count, send_idx, recv_idx, feats, edge_w1, edge_w2, node_w1, node_w2,
    t_out, tt_out, s_out, st_out, fw_out, w1t_out, w2t_out, n1t_out, n2t_out,
):
    edges = feats.shape[0]
    lane = lax.broadcasted_iota(jnp.int32, (1, edges), 1)
    live = lane < count[0, 0]
    snd = send_idx[...]
    off = snd - OWN
    slab_swap = jnp.where(place[1] % 2 == 1, 3 * HALO, 2 * HALO)
    region_swap = jnp.where(place[0] % 2 == 1, 3 * HALO, 2 * HALO)
    flip = jnp.where(off < 2 * HALO, slab_swap, region_swap)
    snd = jnp.where(off >= 0, OWN + (off ^ flip), snd)
    snd = jnp.where(live, snd, -1)
    rcv = jnp.where(live, recv_idx[...], -1)
    tt = (lax.broadcasted_iota(jnp.int32, (2 * OWN, edges), 0) == snd).astype(F32)
    st = (lax.broadcasted_iota(jnp.int32, (OWN, edges), 0) == rcv).astype(F32)
    tt_out[...] = tt.astype(BF16)
    st_out[...] = st.astype(BF16)
    t_out[...] = tt.T.astype(BF16)
    s_out[...] = st.T.astype(BF16)
    w1 = edge_w1[...]
    fw_out[...] = mm(feats[...], w1[2 * L :])
    w1t_out[...] = w1.T
    w2t_out[...] = edge_w2[...].T
    n1t_out[...] = node_w1[...].T
    n2t_out[...] = node_w2[...].T


def forward_body(h, halo, t, s, st, fw, edge_w1, edge_w2, node_w1, node_w2):
    extended = jnp.concatenate([h] + halo, axis=0)
    from_send = mm(t, extended).astype(BF16)
    from_recv = mm(s, h).astype(BF16)
    pre = mm(from_send, edge_w1[:L]) + mm(from_recv, edge_w1[L : 2 * L]) + fw
    sig = sigmoid(pre)
    silu = pre * sig
    edge_slope = sig + silu * (1.0 - sig)
    hidden_sum = mm(st, silu.astype(BF16))
    summed = mm_split(hidden_sum, edge_w2).astype(BF16)
    pre_node = mm(h, node_w1[:L]) + mm(summed, node_w1[L:])
    sig_n = sigmoid(pre_node)
    silu_n = pre_node * sig_n
    node_slope = sig_n + silu_n * (1.0 - sig_n)
    hidden_node = silu_n.astype(BF16)
    update = mm(hidden_node, node_w2)
    centre = update - jnp.mean(update, axis=-1, keepdims=True)
    inv_dev = lax.rsqrt(jnp.mean(centre * centre, axis=-1, keepdims=True) + EPS)
    normed = centre * inv_dev
    return edge_slope, hidden_sum, summed, node_slope, hidden_node, normed, inv_dev


def forward_kernel(
    h_ref, p0, p1, p2, p3, t, s, st, fw, spread, edge_w1, edge_w2, node_w1, node_w2, gain,
    h_out, s0, s1, s2, s3, edge_slope_o, hidden_sum_o, summed_o, node_slope_o, hidden_node_o, normed_o, inv_dev_o,
):
    h = h_ref[...]
    parts = forward_body(
        h, [p0[...], p1[...], p2[...], p3[...]], t[...], s[...], st[...], fw[...],
        edge_w1, edge_w2[...], node_w1, node_w2[...],
    )
    edge_slope, hidden_sum, summed, node_slope, hidden_node, normed, inv_dev = parts
    nxt = (h.astype(F32) + normed * gain[...]).astype(BF16)
    h_out[...] = nxt
    sent = mm_t(spread[...], nxt).astype(BF16)
    for i, out in enumerate((s0, s1, s2, s3)):
        out[...] = sent[i * HALO : (i + 1) * HALO]
    edge_slope_o[...] = edge_slope
    hidden_sum_o[...] = hidden_sum
    summed_o[...] = summed
    node_slope_o[...] = node_slope
    hidden_node_o[...] = hidden_node
    normed_o[...] = normed
    inv_dev_o[...] = jnp.broadcast_to(inv_dev, inv_dev_o.shape)


def backward_body(
    up, parts, gain, s, st, tt, w1t, w2t, n1t, n2t,
    own_out, g0, g1, g2, g3, gpe_o, q_o, r_o, gpn_o, gu_o, gm_o, gain_o,
):
    edge_slope, node_slope, normed, inv_dev = parts
    gain_o[...] = jnp.sum(up * normed, axis=0, keepdims=True)
    scaled = up * gain
    gu = inv_dev * (
        scaled
        - jnp.mean(scaled, axis=-1, keepdims=True)
        - normed * jnp.mean(scaled * normed, axis=-1, keepdims=True)
    )
    gu = gu.astype(BF16)
    gpn = (mm(gu, n2t) * node_slope).astype(BF16)
    gj = mm(gpn, n1t)
    own_out[...] = up + gj[:, :L]
    gm = gj[:, L:].astype(BF16)
    high, low = split(mm(gm, w2t))
    s2 = jnp.concatenate([s, s], axis=1)
    ghe = mm(s2, jnp.concatenate([high, low], axis=0))
    gpe = (ghe * edge_slope).astype(BF16)
    q = mm(tt, gpe)
    r = mm(st, gpe)
    ge = mm_split(q, w1t[:, :L])
    own_out[...] = own_out[...] + ge[:OWN] + mm_split(r, w1t[:, L : 2 * L])
    for i, out in enumerate((g0, g1, g2, g3)):
        out[...] = ge[OWN + i * HALO : OWN + (i + 1) * HALO].astype(BF16)
    gpe_o[...] = gpe
    q_o[...] = q
    r_o[...] = r
    gpn_o[...] = gpn
    gu_o[...] = gu
    gm_o[...] = gm


def landed(own, spread, p0, p1, p2, p3):
    parts = jnp.concatenate([p0[...], p1[...], p2[...], p3[...]], axis=0)
    return own[...] + mm(spread[...], parts)


def turn_kernel(
    h_ref, p0, p1, p2, p3, t, s, st, fw, edge_w1, edge_w2, node_w1, node_w2, gain,
    cot, tt, w1t, w2t, n1t, n2t,
    own_out, g0, g1, g2, g3, gpe_o, q_o, r_o, gpn_o, gu_o, gm_o, gain_o, hidden_sum_o, summed_o, hidden_node_o,
):
    st_v, s_v = st[...], s[...]
    parts = forward_body(
        h_ref[...], [p0[...], p1[...], p2[...], p3[...]], t[...], s_v, st_v, fw[...],
        edge_w1, edge_w2[...], node_w1, node_w2[...],
    )
    edge_slope, hidden_sum, summed, node_slope, hidden_node, normed, inv_dev = parts
    hidden_sum_o[...] = hidden_sum
    summed_o[...] = summed
    hidden_node_o[...] = hidden_node
    backward_body(
        cot[...], (edge_slope, node_slope, normed, inv_dev), gain[...],
        s_v, st_v, tt[...], w1t, w2t[...], n1t[...], n2t[...],
        own_out, g0, g1, g2, g3, gpe_o, q_o, r_o, gpn_o, gu_o, gm_o, gain_o,
    )


def backward_kernel(
    own, p0, p1, p2, p3, spread, edge_slope, node_slope, normed, inv_dev, gain,
    s, st, tt, w1t, w2t, n1t, n2t,
    own_out, g0, g1, g2, g3, gpe_o, q_o, r_o, gpn_o, gu_o, gm_o, gain_o,
):
    up = landed(own, spread, p0, p1, p2, p3)
    backward_body(
        up, (edge_slope[...], node_slope[...], normed[...], inv_dev[:, :1]), gain[...],
        s[...], st[...], tt[...], w1t, w2t[...], n1t[...], n2t[...],
        own_out, g0, g1, g2, g3, gpe_o, q_o, r_o, gpn_o, gu_o, gm_o, gain_o,
    )


def weight_terms(h, halo, feats, hidden_sum, summed, hidden_node, gpe, q, r, gpn, gu, gm):
    extended = jnp.concatenate([h] + halo, axis=0)
    q_high, q_low = split(q)
    r_high, r_low = split(r)
    h_high, h_low = split(hidden_sum)
    return (
        mm_t(extended, q_high) + mm_t(extended, q_low),
        mm_t(h, r_high) + mm_t(h, r_low),
        mm_t(feats, gpe),
        mm_t(h_high, gm) + mm_t(h_low, gm),
        mm_t(h, gpn),
        mm_t(summed, gpn),
        mm_t(hidden_node, gu),
    )


def weight_args(refs):
    (h_ref, p0, p1, p2, p3, feats, hidden_sum, summed, hidden_node, gpe, q, r, gpn, gu, gm) = refs
    return weight_terms(
        h_ref[...], [p0[...], p1[...], p2[...], p3[...]], feats[...], hidden_sum[...], summed[...],
        hidden_node[...], gpe[...], q[...], r[...], gpn[...], gu[...], gm[...],
    )


def weight_first_kernel(*refs):
    w1t, gain_in, acc, edge_acc, gain_acc = refs[15:]
    for i, term in enumerate(weight_args(refs[:15])):
        acc[i] = term
    edge_acc[...] = mm(refs[9][...], w1t[:, 2 * L :])
    gain_acc[...] = gain_in[...]


def weight_kernel(*refs):
    w1t, gain_in, acc_in, edge_in, gain_acc_in, acc, edge_acc, gain_acc = refs[15:]
    for i, term in enumerate(weight_args(refs[:15])):
        acc[i] = acc_in[i] + term
    edge_acc[...] = edge_in[...] + mm(refs[9][...], w1t[:, 2 * L :])
    gain_acc[...] = gain_acc_in[...] + gain_in[...]


def weight_last_kernel(place, *refs):
    gain_in, acc_in, gain_acc_in, out = refs[15:]
    core = place[1] % 2
    terms = weight_args(refs[:15])
    for i, term in enumerate(terms):
        out[(i // 4) ^ core, (i % 4) * L : (i % 4 + 1) * L, :] = (acc_in[i] + term).astype(BF16)
    row = lax.broadcasted_iota(jnp.int32, (L, L), 0)
    gain = gain_acc_in[...] + gain_in[...]
    out[1 ^ core, 3 * L :, :] = jnp.where(row == 0, gain, 0.0).astype(BF16)


def edge_last_kernel(gpe, w1t, edge_in, out):
    out[...] = edge_in[...] + mm(gpe[...], w1t[:, 2 * L :])


def node_last_kernel(own, p0, p1, p2, p3, spread, out):
    out[...] = landed(own, spread, p0, p1, p2, p3)


def finish_kernel(factor, place, mine, other, edge_in, edge_out, node_in, node_out, gain):
    core = place[1] % 2

    def half(index, lo, hi):
        a = mine[lo:hi].astype(F32)
        b = other[lo:hi].astype(F32)
        return jnp.where(core == index, a, b) * factor

    edge_in[...] = half(0, 0, 3 * L)
    edge_out[...] = half(0, 3 * L, 4 * L)
    node_in[...] = half(1, 0, 2 * L)
    node_out[...] = half(1, 2 * L, 3 * L)
    gain[...] = half(1, 3 * L, 3 * L + 8)


def even_pairs(size):
    return [(i, i ^ 1) for i in range(size)]


def odd_pairs(size):
    up = [((i + 1) % size, (i + 2) % size) for i in range(0, size, 2)]
    return up + [(b, a) for a, b in up]


def exchange(parts):
    slabs = lax.axis_size(SLAB)
    regions = lax.axis_size(REGION)
    return [
        lax.ppermute(parts[0], REGION, odd_pairs(regions)),
        lax.ppermute(parts[1], REGION, even_pairs(regions)),
        lax.ppermute(parts[2], SLAB, odd_pairs(slabs)),
        lax.ppermute(parts[3], SLAB, even_pairs(slabs)),
    ]


def reduce_all(payload):
    keep = payload[0].astype(F32)
    got = lax.ppermute(payload[1], "c", [(0, 1), (1, 0)])
    part = (keep + got.astype(F32)).astype(BF16).reshape(CHUNKS, CHUNK_ROWS, L)
    part = lax.all_to_all(part, PLANE, 0, 0, tiled=True)
    part = jnp.sum(part.astype(F32), axis=0).astype(BF16)
    deep = lax.axis_size("z")
    part = lax.all_to_all(jnp.broadcast_to(part[None], (deep,) + part.shape), "z", 0, 0, tiled=True)
    part = jnp.sum(part.astype(F32), axis=0).astype(BF16)
    part = jnp.broadcast_to(part[None], (CHUNKS,) + part.shape)
    mine = lax.all_to_all(part, PLANE, 0, 0, tiled=True).reshape(CHUNKS * CHUNK_ROWS, L)
    other = lax.ppermute(mine, "c", [(0, 1), (1, 0)])
    return mine, other


def local(
    nodes, feats, cotangent, edge_w1, edge_w2, node_w1, node_w2, ln_gain, senders, receivers, send_rows, edge_count
):
    edges = feats.shape[0]
    place = jnp.stack([lax.axis_index(REGION), lax.axis_index(SLAB)]).astype(jnp.int32)
    gain = ln_gain.reshape(1, L)
    halo_outs = [((HALO, L), BF16)] * 4
    *sends, spread = call(
        first_kernel, halo_outs + [((OWN, 4 * HALO), BF16)], place, nodes, send_rows, smem=1
    )
    t, tt, s, st, fw, w1t, w2t, n1t, n2t = call(
        prep_kernel,
        [
            ((edges, 2 * OWN), BF16), ((2 * OWN, edges), BF16), ((edges, OWN), BF16), ((OWN, edges), BF16),
            ((edges, L), F32), ((L, 3 * L), BF16), ((L, L), BF16), ((L, 2 * L), BF16), ((L, L), BF16),
        ],
        place, edge_count, senders.reshape(1, edges), receivers.reshape(1, edges), feats, edge_w1, edge_w2, node_w1, node_w2,
        smem=2,
    )
    h = nodes
    saved = []
    for _ in range(STEPS - 1):
        halo = exchange(sends)
        nxt, *rest = call(
            forward_kernel,
            [((OWN, L), BF16)] + halo_outs + [
                ((edges, L), F32), ((OWN, L), F32), ((OWN, L), BF16), ((OWN, L), F32), ((OWN, L), BF16),
                ((OWN, L), F32), ((OWN, 128), F32),
            ],
            h, *halo, t, s, st, fw, spread, edge_w1, edge_w2, node_w1, node_w2, gain,
        )
        saved.append((h, halo, rest[4:]))
        sends = rest[:4]
        h = nxt
    halo = exchange(sends)
    back_outs = [((OWN, L), F32)] + halo_outs + [
        ((edges, L), BF16), ((2 * OWN, L), F32), ((OWN, L), F32), ((OWN, L), BF16), ((OWN, L), BF16), ((OWN, L), BF16), ((1, L), F32),
    ]
    own, g0, g1, g2, g3, *rest = call(
        turn_kernel,
        back_outs + [((OWN, L), F32), ((OWN, L), BF16), ((OWN, L), BF16)],
        h, *halo, t, s, st, fw, edge_w1, edge_w2, node_w1, node_w2, gain, cotangent, tt, w1t, w2t, n1t, n2t,
    )
    back = exchange([g0, g1, g2, g3])
    *terms, gain_term, hidden_sum, summed, hidden_node = rest
    acc_outs = [((7, L, L), F32), ((edges, L), F32), ((1, L), F32)]
    totals = call(
        weight_first_kernel, acc_outs, h, *halo, feats, hidden_sum, summed, hidden_node, *terms, w1t, gain_term
    )
    for layer in reversed(range(STEPS - 1)):
        h, halo, (edge_slope, hidden_sum, summed, node_slope, hidden_node, normed, inv_dev) = saved[layer]
        own, g0, g1, g2, g3, *rest = call(
            backward_kernel, back_outs,
            own, *back, spread, edge_slope, node_slope, normed, inv_dev, gain, s, st, tt, w1t, w2t, n1t, n2t,
        )
        back = exchange([g0, g1, g2, g3])
        *terms, gain_term = rest
        shared = (h, *halo, feats, hidden_sum, summed, hidden_node, *terms)
        if layer > 0:
            totals = call(weight_kernel, acc_outs, *shared, w1t, gain_term, *totals)
    (payload,) = call(
        weight_last_kernel, [((2, 4 * L, L), BF16)], place, *shared, gain_term, totals[0], totals[2], smem=1
    )
    mine, other = reduce_all(payload)
    (edge_grad,) = call(edge_last_kernel, [((edges, L), F32)], terms[0], w1t, totals[1])
    (node_grad,) = call(node_last_kernel, [((OWN, L), F32)], own, *back, spread)
    devices = lax.axis_size(REGION) * lax.axis_size(SLAB)
    factor = float(OWN * devices) ** (-0.5)

    def finish(*refs):
        finish_kernel(factor, *refs)

    edge_in, edge_out, node_in, node_out, gain_grad = call(
        finish, [((3 * L, L), F32), ((L, L), F32), ((2 * L, L), F32), ((L, L), F32), ((8, L), F32)], place, mine, other, smem=1
    )
    return node_grad, edge_grad, edge_in, edge_out, node_in, node_out, gain_grad[0]


def solution(mesh):
    fine = Mesh(mesh.devices.reshape(4, 2, 8, 2, 2), AXES)
    split_rows = P(AXES, None)
    placed = (
        split_rows, split_rows, split_rows, P(), P(), P(), P(), P(), P(AXES), P(AXES), split_rows, P(REGION, SLAB),
    )
    return jax.shard_map(
        local,
        mesh=fine,
        in_specs=placed,
        out_specs=(split_rows, split_rows, P(), P(), P(), P(), P()),
        check_vma=False,
    )
```

time: 596 us -> 158 us (0.27); the launches traced: 585 us -> 156 us
  waiting for transfers between devices: 171 us -> 10.9 us
  other arithmetic: 141 us -> 0.34 us
  matrix products: 44.8 us -> 0 us
  local copies, waits for them, and re-layouts: 56.4 us -> 12.7 us
  blocking collectives: 79.2 us -> 42.1 us
  Pallas kernels: 0 us -> 20.8 us
  between operations: 16.7 us -> 1.58 us
  starting transfers between devices: 75.5 us -> 67.6 us
    psum x1 -> x0, waiting for transfers between devices: 168 us -> none  [local(): lax.psum((terms[0], terms[1], terms[2], terms[3], terms[4]), ('region', '...]
    scatter-add x28 -> x0, other arithmetic: 113 us -> none  [the longest x4 29.7 us: local_backward(): jax.ops.segment_sum(grad_stacked[:, width:2 * width], recv_idx, num_segme...]
    psum x1 -> x0, blocking collectives: 79.2 us -> none  [local(): lax.psum((terms[0], terms[1], terms[2], terms[3], terms[4]), ('region', '...]
    gather x28 -> x0, local copies, waits for them, and re-layouts: 46.5 us -> none  [the longest x4 11.6 us: edge_forward(): extended[send_idx]]
    dot_general x48 -> x0, matrix products: 44.8 us -> none  [the longest x4 7.78 us: local_backward(): jnp.dot(hidden_node.T, grad_update, preferred_element_type=jnp.float32)]
    all_to_all x0 -> x3, blocking collectives: none -> 42.1 us  [the longest x1 16.3 us: reduce_all(): part = lax.all_to_all(part, PLANE, 0, 0, tiled=True)]
    pallas_call x0 -> x16, Pallas kernels: none -> 20.8 us  [call(): pl.pallas_call(kernel, out_shape=[jax.ShapeDtypeStruct(s, d) for s, d in...]
    ppermute x32 -> x34, waiting for transfers between devices: 2.96 us -> 10.9 us  [the longest x8 4.27 us: exchange(): lax.ppermute(parts[0], REGION, odd_pairs(regions))]
  transfers between devices with their start and end apart: 33 -> 34, of which waited for: 5 -> 10; matrix products, arithmetic and copies ran while one was open for 14% -> 1% of each run, Pallas kernels for 0% -> 3%
where the time goes in v1:
time: 158 us; the launch traced here: 156 us
  starting transfers between devices  67.6 us (43%)
  blocking collectives  42.1 us (27%)
  Pallas kernels  20.8 us (13%)
  local copies, waits for them, and re-layouts  12.7 us (8%)
  waiting for transfers between devices  10.9 us (7%)
  between operations  1.58 us (1%)
    ppermute x8, starting transfers between devices, exchange(): lax.ppermute(parts[0], REGION, odd_pairs(regions))  27.5 us
    ppermute x8, starting transfers between devices, exchange(): lax.ppermute(parts[3], SLAB, even_pairs(slabs))  25.6 us
    pallas_call x16, Pallas kernels, call(): pl.pallas_call(kernel, out_shape=[jax.ShapeDtypeStruct(s, d) for s, d in...  20.8 us
    all_to_all x1, blocking collectives, reduce_all(): part = lax.all_to_all(part, PLANE, 0, 0, tiled=True)  16.3 us
    all_to_all x1, blocking collectives, reduce_all(): lax.all_to_all(jnp.broadcast_to(part[None], (deep,) + part.shape), 'z', 0...  13.3 us
    all_to_all x1, blocking collectives, reduce_all(): lax.all_to_all(part, PLANE, 0, 0, tiled=True)  12.5 us
    unnamed x36, local copies, waits for them, and re-layouts  10.6 us
    ppermute x1, starting transfers between devices, reduce_all(): other = lax.ppermute(mine, 'c', [(0, 1), (1, 0)])  4.78 us
  transfers between devices with their start and end apart: 34, of which 10 were waited for; matrix products, arithmetic and copies ran while one was open for 1% of the time, Pallas kernels for 3%

profile of v1, /device:TPU:1, one launch (start us, length us, event | category | flops | bytes accessed | tf_op | source)
XLA Modules:
  0.0 156.0 jit_solution(15310778896297071229)
XLA Ops:
  3.0 6.0 %collective-permute-start = (bf16[32,256]{1,0:T(8,128)(2,1)S(1)}, bf16[32,256]{1,0:T(8,128)(2,1)S(1)}, u32[]{:S(2)}, u32[]{:S(2)}) collective-permute-start(bf16[32,256]{1,0:T(8,128)(2,1)S(1)} %get-tuple-element.122), channel_id=1, source_target_pairs={{32,64},{96,128},{160,192},{224,0},{64,32},{128,96},{192,160},{0,2... | collective-permute-start | bytes 49160 | tf_op jit(solution)/shard_map/ppermute | solution.py:317
  10.3 4.8 %collective-permute-start.3 = (bf16[32,256]{1,0:T(8,128)(2,1)S(1)}, bf16[32,256]{1,0:T(8,128)(2,1)S(1)}, u32[]{:S(2)}, u32[]{:S(2)}) collective-permute-start(bf16[32,256]{1,0:T(8,128)(2,1)S(1)} %get-tuple-element.125), channel_id=1, source_target_pairs={{0,1},{1,0},{2,3},{3,2},{4,5},{5,4},{6,7},{7,6},{8,9},{9,8},{10,11... | collective-permute-start | bytes 49160 | tf_op jit(solution)/shard_map/ppermute | solution.py:320
  27.3 1.6 %shard_map.173 = (bf16[128,256]{1,0:T(8,128)(2,1)S(1)}, bf16[32,256]{1,0:T(8,128)(2,1)S(1)}, bf16[32,256]{1,0:T(8,128)(2,1)S(1)}, bf16[32,256]{1,0:T(8,128)(2,1)...) custom-call(bf16[128,256]{1,0:T(8,128)(2,1)S(1)} %copy-done.12, ...), custom_call_target="tpu_custom_call" | custom-call | tf_op jit(solution)/shard_map/pallas_call | solution.py:50
  28.9 3.9 %collective-permute-start.4 = (bf16[32,256]{1,0:T(8,128)(2,1)S(1)}, bf16[32,256]{1,0:T(8,128)(2,1)S(1)}, u32[]{:S(2)}, u32[]{:S(2)}) collective-permute-start(bf16[32,256]{1,0:T(8,128)(2,1)S(1)} %get-tuple-element.132), channel_id=1, source_target_pairs={{32,64},{96,128},{160,192},{224,0},{64,32},{128,96},{192,160},{0,2... | collective-permute-start | bytes 49160 | tf_op jit(solution)/shard_map/ppermute | solution.py:317
  33.8 1.4 collective-permute-done.4.p0.refs_1_
  35.2 1.7 %collective-permute-done.5.p1.refs_2_ = bf16[32,256]{1,0:T(8,128)(2,1)S(1)} collective-permute-done((bf16[32,256]{1,0:T(8,128)(2,1)S(1)}, bf16[32,256]{1,0:T(8,128)(2,1)S(1)}, u32[]{:S(2)}, u32[]{:S(2)}) %collective-permute-start.5) | collective-permute-done | bytes 16416 | tf_op jit(solution)/shard_map/ppermute | solution.py:318
  37.0 1.6 %shard_map.174 = (bf16[128,256]{1,0:T(8,128)(2,1)S(1)}, bf16[32,256]{1,0:T(8,128)(2,1)S(1)}, bf16[32,256]{1,0:T(8,128)(2,1)S(1)}, bf16[32,256]{1,0:T(8,128)(2,1)...) custom-call(bf16[128,256]{1,0:T(8,128)(2,1)S(1)} %get-tuple-element., ...), custom_call_target="tpu_custom_call" | custom-call | tf_op jit(solution)/shard_map/pallas_call | solution.py:50
  38.6 2.4 %collective-permute-start.8 = (bf16[32,256]{1,0:T(8,128)(2,1)S(1)}, bf16[32,256]{1,0:T(8,128)(2,1)S(1)}, u32[]{:S(2)}, u32[]{:S(2)}) collective-permute-start(bf16[32,256]{1,0:T(8,128)(2,1)S(1)} %get-tuple-element.137), channel_id=1, source_target_pairs={{32,64},{96,128},{160,192},{224,0},{64,32},{128,96},{192,160},{0,2... | collective-permute-start | bytes 49160 | tf_op jit(solution)/shard_map/ppermute | solution.py:317
  42.3 2.1 %collective-permute-start.11 = (bf16[32,256]{1,0:T(8,128)(2,1)S(1)}, bf16[32,256]{1,0:T(8,128)(2,1)S(1)}, u32[]{:S(2)}, u32[]{:S(2)}) collective-permute-start(bf16[32,256]{1,0:T(8,128)(2,1)S(1)} %get-tuple-element.140), channel_id=1, source_target_pairs={{0,1},{1,0},{2,3},{3,2},{4,5},{5,4},{6,7},{7,6},{8,9},{9,8},{10,11... | collective-permute-start | bytes 49160 | tf_op jit(solution)/shard_map/ppermute | solution.py:320
  45.8 1.6 %shard_map.175 = (bf16[128,256]{1,0:T(8,128)(2,1)S(1)}, bf16[32,256]{1,0:T(8,128)(2,1)S(1)}, bf16[32,256]{1,0:T(8,128)(2,1)S(1)}, bf16[32,256]{1,0:T(8,128)(2,1)...) custom-call(bf16[128,256]{1,0:T(8,128)(2,1)S(1)} %get-tuple-element., ...), custom_call_target="tpu_custom_call" | custom-call | tf_op jit(solution)/shard_map/pallas_call | solution.py:50
  47.4 2.4 %collective-permute-start.12 = (bf16[32,256]{1,0:T(8,128)(2,1)S(1)}, bf16[32,256]{1,0:T(8,128)(2,1)S(1)}, u32[]{:S(2)}, u32[]{:S(2)}) collective-permute-start(bf16[32,256]{1,0:T(8,128)(2,1)S(1)} %get-tuple-element.142), channel_id=1, source_target_pairs={{32,64},{96,128},{160,192},{224,0},{64,32},{128,96},{192,160},{0,2... | collective-permute-start | bytes 49160 | tf_op jit(solution)/shard_map/ppermute | solution.py:317
  50.4 1.6 collective-permute-start.14
  52.0 3.1 %collective-permute-start.15 = (bf16[32,256]{1,0:T(8,128)(2,1)S(1)}, bf16[32,256]{1,0:T(8,128)(2,1)S(1)}, u32[]{:S(2)}, u32[]{:S(2)}) collective-permute-start(bf16[32,256]{1,0:T(8,128)(2,1)S(1)} %get-tuple-element.145), channel_id=1, source_target_pairs={{0,1},{1,0},{2,3},{3,2},{4,5},{5,4},{6,7},{7,6},{8,9},{9,8},{10,11... | collective-permute-start | bytes 49160 | tf_op jit(solution)/shard_map/ppermute | solution.py:320
  56.0 2.8 %shard_map.176 = (f32[128,256]{1,0:T(8,128)S(1)}, bf16[32,256]{1,0:T(8,128)(2,1)S(1)}, bf16[32,256]{1,0:T(8,128)(2,1)S(1)}, bf16[32,256]{1,0:T(8,128)(2,1)S(1)},...) custom-call(bf16[128,256]{1,0:T(8,128)(2,1)S(1)} %get-tuple-element., ...), custom_call_target="tpu_custom_call" | custom-call | tf_op jit(solution)/shard_map/pallas_call | solution.py:50
  58.7 4.7 %collective-permute-start.16 = (bf16[32,256]{1,0:T(8,128)(2,1)S(1)}, bf16[32,256]{1,0:T(8,128)(2,1)S(1)}, u32[]{:S(2)}, u32[]{:S(2)}) collective-permute-start(bf16[32,256]{1,0:T(8,128)(2,1)S(1)} %get-tuple-element.152), channel_id=1, source_target_pairs={{32,64},{96,128},{160,192},{224,0},{64,32},{128,96},{192,160},{0,2... | collective-permute-start | bytes 49160 | tf_op jit(solution)/shard_map/ppermute | solution.py:317
  63.4 4.7 %collective-permute-start.19 = (bf16[32,256]{1,0:T(8,128)(2,1)S(1)}, bf16[32,256]{1,0:T(8,128)(2,1)S(1)}, u32[]{:S(2)}, u32[]{:S(2)}) collective-permute-start(bf16[32,256]{1,0:T(8,128)(2,1)S(1)} %get-tuple-element.155), channel_id=1, source_target_pairs={{0,1},{1,0},{2,3},{3,2},{4,5},{5,4},{6,7},{7,6},{8,9},{9,8},{10,11... | collective-permute-start | bytes 49160 | tf_op jit(solution)/shard_map/ppermute | solution.py:320
  69.0 1.4 shard_map.177
  70.4 3.5 %collective-permute-start.20 = (bf16[32,256]{1,0:T(8,128)(2,1)S(1)}, bf16[32,256]{1,0:T(8,128)(2,1)S(1)}, u32[]{:S(2)}, u32[]{:S(2)}) collective-permute-start(bf16[32,256]{1,0:T(8,128)(2,1)S(1)} %get-tuple-element.161), channel_id=1, source_target_pairs={{32,64},{96,128},{160,192},{224,0},{64,32},{128,96},{192,160},{0,2... | collective-permute-start | bytes 49160 | tf_op jit(solution)/shard_map/ppermute | solution.py:317
  73.9 4.7 %collective-permute-start.23 = (bf16[32,256]{1,0:T(8,128)(2,1)S(1)}, bf16[32,256]{1,0:T(8,128)(2,1)S(1)}, u32[]{:S(2)}, u32[]{:S(2)}) collective-permute-start(bf16[32,256]{1,0:T(8,128)(2,1)S(1)} %get-tuple-element.164), channel_id=1, source_target_pairs={{0,1},{1,0},{2,3},{3,2},{4,5},{5,4},{6,7},{7,6},{8,9},{9,8},{10,11... | collective-permute-start | bytes 49160 | tf_op jit(solution)/shard_map/ppermute | solution.py:320
  79.5 1.4 shard_map.178
  80.9 3.3 %collective-permute-start.24 = (bf16[32,256]{1,0:T(8,128)(2,1)S(1)}, bf16[32,256]{1,0:T(8,128)(2,1)S(1)}, u32[]{:S(2)}, u32[]{:S(2)}) collective-permute-start(bf16[32,256]{1,0:T(8,128)(2,1)S(1)} %get-tuple-element.170), channel_id=1, source_target_pairs={{32,64},{96,128},{160,192},{224,0},{64,32},{128,96},{192,160},{0,2... | collective-permute-start | bytes 49160 | tf_op jit(solution)/shard_map/ppermute | solution.py:317
  84.7 5.0 %collective-permute-start.27 = (bf16[32,256]{1,0:T(8,128)(2,1)S(1)}, bf16[32,256]{1,0:T(8,128)(2,1)S(1)}, u32[]{:S(2)}, u32[]{:S(2)}) collective-permute-start(bf16[32,256]{1,0:T(8,128)(2,1)S(1)} %get-tuple-element.173), channel_id=1, source_target_pairs={{0,1},{1,0},{2,3},{3,2},{4,5},{5,4},{6,7},{7,6},{8,9},{9,8},{10,11... | collective-permute-start | bytes 49160 | tf_op jit(solution)/shard_map/ppermute | solution.py:320
  91.9 1.4 shard_map.179
  94.6 3.1 %collective-permute-start.32 = (bf16[1024,256]{1,0:T(8,128)(2,1)S(1)}, bf16[1024,256]{1,0:T(8,128)(2,1)S(1)}, u32[]{:S(2)}, u32[]{:S(2)}) collective-permute-start(bf16[1024,256]{1,0:T(8,128)(2,1)S(1)} %slice_bitcast_fusion), channel_id=1, source_target_pairs={{0,1},{1,0},{2,3},{3,2},{4,5},{5,4},{6,7},{7,6},{8,9},{9,8},{10,11... | collective-permute-start | bytes 1572872 | tf_op jit(solution)/shard_map/ppermute | solution.py:326
  97.7 1.5 collective-permute-done.32
  99.4 16.3 %all_to_all.15 = bf16[16,64,256]{2,1,0:T(8,128)(2,1)S(1)} all-to-all(bf16[16,64,256]{2,1,0:T(8,128)(2,1)S(1)} %bitcast.22), channel_id=1, replica_groups=mesh['x'=4,'yh'=2,'z'=8,'yl'=2,'c'=2] {'x','yh','yl'}, dimensions={0} | all-to-all | bytes 1048576 | tf_op jit(solution)/shard_map/all_to_all | solution.py:328
  115.8 13.3 %all_to_all.16 = bf16[8,64,256]{2,1,0:T(8,128)(2,1)S(1)} all-to-all(bf16[8,64,256]{2,1,0:T(8,128)(2,1)S(1)} %broadcast_in_dim.4), channel_id=1, replica_groups=mesh['x'=4,'yh'=2,'z'=8,'yl'=2,'c'=2] {'z'}, dimensions={0} | all-to-all | bytes 524288 | tf_op jit(solution)/shard_map/all_to_all | solution.py:331
  129.2 12.5 %all_to_all.17 = bf16[16,64,256]{2,1,0:T(8,128)(2,1)S(1)} all-to-all(bf16[16,64,256]{2,1,0:T(8,128)(2,1)S(1)} %broadcast_in_dim.5), channel_id=1, replica_groups=mesh['x'=4,'yh'=2,'z'=8,'yl'=2,'c'=2] {'x','yh','yl'}, dimensions={0} | all-to-all | bytes 1048576 | tf_op jit(solution)/shard_map/all_to_all | solution.py:334
  141.7 4.8 %collective-permute-start.33 = (bf16[1024,256]{1,0:T(8,128)(2,1)S(1)}, bf16[1024,256]{1,0:T(8,128)(2,1)S(1)}, u32[]{:S(2)}, u32[]{:S(2)}) collective-permute-start(bf16[1024,256]{1,0:T(8,128)(2,1)S(1)} %bitcast.13), channel_id=1, source_target_pairs={{0,1},{1,0},{2,3},{3,2},{4,5},{5,4},{6,7},{7,6},{8,9},{9,8},{10,11... | collective-permute-start | bytes 1572872 | tf_op jit(solution)/shard_map/ppermute | solution.py:335
  146.5 1.3 collective-permute-start.28
  150.3 2.4 %collective-permute-done.28.p0 = bf16[32,256]{1,0:T(8,128)(2,1)S(1)} collective-permute-done((bf16[32,256]{1,0:T(8,128)(2,1)S(1)}, bf16[32,256]{1,0:T(8,128)(2,1)S(1)}, u32[]{:S(2)}, u32[]{:S(2)}) %collective-permute-start.28) | collective-permute-done | bytes 16416 | tf_op jit(solution)/shard_map/ppermute | solution.py:317
  153.6 1.9 %shard_map.186 = (f32[768,256]{1,0:T(8,128)}, f32[256,256]{1,0:T(8,128)}, f32[512,256]{1,0:T(8,128)}, f32[256,256]{1,0:T(8,128)}, f32[8,256]{1,0:T(8,128)S(1)}) custom-call(s32[2]{0:T(128)S(1)} %pad_add_fusion.place.refs_0_, bf16[1024,256]{1,0:T(8,128)(2,1)S(1)} %bitcast.14, bf16[1024,256]{1,0:T(8,128)(2,1)S(1)} %collective-permute-done.33.refs_2_), custom_call_target="tpu_custom_call" | custom-call | tf_op jit(solution)/shard_map/pallas_call | solution.py:50
  (101 shorter events, 30.0 us)
Async XLA Ops:
  3.0 19.9 %collective-permute-start = (bf16[32,256]{1,0:T(8,128)(2,1)S(1)}, bf16[32,256]{1,0:T(8,128)(2,1)S(1)}, u32[]{:S(2)}, u32[]{:S(2)}) collective-permute-start(bf16[32,256]{1,0:T(8,128)(2,1)S(1)} %get-tuple-element.122), channel_id=1, source_target_pairs={{32,64},{96,128},{160,192},{224,0},{64,32},{128,96},{192,160},{0,2... | collective-permute-start | bytes 49160 | tf_op jit(solution)/shard_map/ppermute | solution.py:317
  9.0 13.9 %collective-permute-start.1 = (bf16[32,256]{1,0:T(8,128)(2,1)S(1)}, bf16[32,256]{1,0:T(8,128)(2,1)S(1)}, u32[]{:S(2)}, u32[]{:S(2)}) collective-permute-start(bf16[32,256]{1,0:T(8,128)(2,1)S(1)} %get-tuple-element.123), channel_id=1, source_target_pairs={{0,32},{32,0},{64,96},{96,64},{128,160},{160,128},{192,224},{224,1... | collective-permute-start | bytes 49160 | tf_op jit(solution)/shard_map/ppermute | solution.py:318
  9.0 13.9 %collective-permute-start.2 = (bf16[32,256]{1,0:T(8,128)(2,1)S(1)}, bf16[32,256]{1,0:T(8,128)(2,1)S(1)}, u32[]{:S(2)}, u32[]{:S(2)}) collective-permute-start(bf16[32,256]{1,0:T(8,128)(2,1)S(1)} %get-tuple-element.124), channel_id=1, source_target_pairs={{1,2},{3,4},{5,6},{7,8},{9,10},{11,12},{13,14},{15,16},{17,18},{19... | collective-permute-start | bytes 49160 | tf_op jit(solution)/shard_map/ppermute | solution.py:319
  10.3 12.7 %collective-permute-start.3 = (bf16[32,256]{1,0:T(8,128)(2,1)S(1)}, bf16[32,256]{1,0:T(8,128)(2,1)S(1)}, u32[]{:S(2)}, u32[]{:S(2)}) collective-permute-start(bf16[32,256]{1,0:T(8,128)(2,1)S(1)} %get-tuple-element.125), channel_id=1, source_target_pairs={{0,1},{1,0},{2,3},{3,2},{4,5},{5,4},{6,7},{7,6},{8,9},{9,8},{10,11... | collective-permute-start | bytes 49160 | tf_op jit(solution)/shard_map/ppermute | solution.py:320
  28.9 6.3 %collective-permute-start.4 = (bf16[32,256]{1,0:T(8,128)(2,1)S(1)}, bf16[32,256]{1,0:T(8,128)(2,1)S(1)}, u32[]{:S(2)}, u32[]{:S(2)}) collective-permute-start(bf16[32,256]{1,0:T(8,128)(2,1)S(1)} %get-tuple-element.132), channel_id=1, source_target_pairs={{32,64},{96,128},{160,192},{224,0},{64,32},{128,96},{192,160},{0,2... | collective-permute-start | bytes 49160 | tf_op jit(solution)/shard_map/ppermute | solution.py:317
  32.9 4.1 %collective-permute-start.5 = (bf16[32,256]{1,0:T(8,128)(2,1)S(1)}, bf16[32,256]{1,0:T(8,128)(2,1)S(1)}, u32[]{:S(2)}, u32[]{:S(2)}) collective-permute-start(bf16[32,256]{1,0:T(8,128)(2,1)S(1)} %get-tuple-element.133), channel_id=1, source_target_pairs={{0,32},{32,0},{64,96},{96,64},{128,160},{160,128},{192,224},{224,1... | collective-permute-start | bytes 49160 | tf_op jit(solution)/shard_map/ppermute | solution.py:318
  32.9 4.1 %collective-permute-start.6 = (bf16[32,256]{1,0:T(8,128)(2,1)S(1)}, bf16[32,256]{1,0:T(8,128)(2,1)S(1)}, u32[]{:S(2)}, u32[]{:S(2)}) collective-permute-start(bf16[32,256]{1,0:T(8,128)(2,1)S(1)} %get-tuple-element.134), channel_id=1, source_target_pairs={{1,2},{3,4},{5,6},{7,8},{9,10},{11,12},{13,14},{15,16},{17,18},{19... | collective-permute-start | bytes 49160 | tf_op jit(solution)/shard_map/ppermute | solution.py:319
  32.9 4.1 %collective-permute-start.7 = (bf16[32,256]{1,0:T(8,128)(2,1)S(1)}, bf16[32,256]{1,0:T(8,128)(2,1)S(1)}, u32[]{:S(2)}, u32[]{:S(2)}) collective-permute-start(bf16[32,256]{1,0:T(8,128)(2,1)S(1)} %get-tuple-element.135), channel_id=1, source_target_pairs={{0,1},{1,0},{2,3},{3,2},{4,5},{5,4},{6,7},{7,6},{8,9},{9,8},{10,11... | collective-permute-start | bytes 49160 | tf_op jit(solution)/shard_map/ppermute | solution.py:320
  38.6 6.3 %collective-permute-start.8 = (bf16[32,256]{1,0:T(8,128)(2,1)S(1)}, bf16[32,256]{1,0:T(8,128)(2,1)S(1)}, u32[]{:S(2)}, u32[]{:S(2)}) collective-permute-start(bf16[32,256]{1,0:T(8,128)(2,1)S(1)} %get-tuple-element.137), channel_id=1, source_target_pairs={{32,64},{96,128},{160,192},{224,0},{64,32},{128,96},{192,160},{0,2... | collective-permute-start | bytes 49160 | tf_op jit(solution)/shard_map/ppermute | solution.py:317
  41.0 4.1 %collective-permute-start.9 = (bf16[32,256]{1,0:T(8,128)(2,1)S(1)}, bf16[32,256]{1,0:T(8,128)(2,1)S(1)}, u32[]{:S(2)}, u32[]{:S(2)}) collective-permute-start(bf16[32,256]{1,0:T(8,128)(2,1)S(1)} %get-tuple-element.138), channel_id=1, source_target_pairs={{0,32},{32,0},{64,96},{96,64},{128,160},{160,128},{192,224},{224,1... | collective-permute-start | bytes 49160 | tf_op jit(solution)/shard_map/ppermute | solution.py:318
  47.4 7.7 %collective-permute-start.12 = (bf16[32,256]{1,0:T(8,128)(2,1)S(1)}, bf16[32,256]{1,0:T(8,128)(2,1)S(1)}, u32[]{:S(2)}, u32[]{:S(2)}) collective-permute-start(bf16[32,256]{1,0:T(8,128)(2,1)S(1)} %get-tuple-element.142), channel_id=1, source_target_pairs={{32,64},{96,128},{160,192},{224,0},{64,32},{128,96},{192,160},{0,2... | collective-permute-start | bytes 49160 | tf_op jit(solution)/shard_map/ppermute | solution.py:317
  49.8 5.3 %collective-permute-start.13 = (bf16[32,256]{1,0:T(8,128)(2,1)S(1)}, bf16[32,256]{1,0:T(8,128)(2,1)S(1)}, u32[]{:S(2)}, u32[]{:S(2)}) collective-permute-start(bf16[32,256]{1,0:T(8,128)(2,1)S(1)} %get-tuple-element.143), channel_id=1, source_target_pairs={{0,32},{32,0},{64,96},{96,64},{128,160},{160,128},{192,224},{224,1... | collective-permute-start | bytes 49160 | tf_op jit(solution)/shard_map/ppermute | solution.py:318
  50.4 4.7 %collective-permute-start.14 = (bf16[32,256]{1,0:T(8,128)(2,1)S(1)}, bf16[32,256]{1,0:T(8,128)(2,1)S(1)}, u32[]{:S(2)}, u32[]{:S(2)}) collective-permute-start(bf16[32,256]{1,0:T(8,128)(2,1)S(1)} %get-tuple-element.144), channel_id=1, source_target_pairs={{1,2},{3,4},{5,6},{7,8},{9,10},{11,12},{13,14},{15,16},{17,18},{19... | collective-permute-start | bytes 49160 | tf_op jit(solution)/shard_map/ppermute | solution.py:319
  52.0 4.0 %collective-permute-start.15 = (bf16[32,256]{1,0:T(8,128)(2,1)S(1)}, bf16[32,256]{1,0:T(8,128)(2,1)S(1)}, u32[]{:S(2)}, u32[]{:S(2)}) collective-permute-start(bf16[32,256]{1,0:T(8,128)(2,1)S(1)} %get-tuple-element.145), channel_id=1, source_target_pairs={{0,1},{1,0},{2,3},{3,2},{4,5},{5,4},{6,7},{7,6},{8,9},{9,8},{10,11... | collective-permute-start | bytes 49160 | tf_op jit(solution)/shard_map/ppermute | solution.py:320
  58.7 9.4 %collective-permute-start.16 = (bf16[32,256]{1,0:T(8,128)(2,1)S(1)}, bf16[32,256]{1,0:T(8,128)(2,1)S(1)}, u32[]{:S(2)}, u32[]{:S(2)}) collective-permute-start(bf16[32,256]{1,0:T(8,128)(2,1)S(1)} %get-tuple-element.152), channel_id=1, source_target_pairs={{32,64},{96,128},{160,192},{224,0},{64,32},{128,96},{192,160},{0,2... | collective-permute-start | bytes 49160 | tf_op jit(solution)/shard_map/ppermute | solution.py:317
  63.4 4.7 %collective-permute-start.17 = (bf16[32,256]{1,0:T(8,128)(2,1)S(1)}, bf16[32,256]{1,0:T(8,128)(2,1)S(1)}, u32[]{:S(2)}, u32[]{:S(2)}) collective-permute-start(bf16[32,256]{1,0:T(8,128)(2,1)S(1)} %get-tuple-element.153), channel_id=1, source_target_pairs={{0,32},{32,0},{64,96},{96,64},{128,160},{160,128},{192,224},{224,1... | collective-permute-start | bytes 49160 | tf_op jit(solution)/shard_map/ppermute | solution.py:318
  63.4 4.7 %collective-permute-start.18 = (bf16[32,256]{1,0:T(8,128)(2,1)S(1)}, bf16[32,256]{1,0:T(8,128)(2,1)S(1)}, u32[]{:S(2)}, u32[]{:S(2)}) collective-permute-start(bf16[32,256]{1,0:T(8,128)(2,1)S(1)} %get-tuple-element.154), channel_id=1, source_target_pairs={{1,2},{3,4},{5,6},{7,8},{9,10},{11,12},{13,14},{15,16},{17,18},{19... | collective-permute-start | bytes 49160 | tf_op jit(solution)/shard_map/ppermute | solution.py:319
  63.4 5.6 %collective-permute-start.19 = (bf16[32,256]{1,0:T(8,128)(2,1)S(1)}, bf16[32,256]{1,0:T(8,128)(2,1)S(1)}, u32[]{:S(2)}, u32[]{:S(2)}) collective-permute-start(bf16[32,256]{1,0:T(8,128)(2,1)S(1)} %get-tuple-element.155), channel_id=1, source_target_pairs={{0,1},{1,0},{2,3},{3,2},{4,5},{5,4},{6,7},{7,6},{8,9},{9,8},{10,11... | collective-permute-start | bytes 49160 | tf_op jit(solution)/shard_map/ppermute | solution.py:320
  70.4 8.3 %collective-permute-start.20 = (bf16[32,256]{1,0:T(8,128)(2,1)S(1)}, bf16[32,256]{1,0:T(8,128)(2,1)S(1)}, u32[]{:S(2)}, u32[]{:S(2)}) collective-permute-start(bf16[32,256]{1,0:T(8,128)(2,1)S(1)} %get-tuple-element.161), channel_id=1, source_target_pairs={{32,64},{96,128},{160,192},{224,0},{64,32},{128,96},{192,160},{0,2... | collective-permute-start | bytes 49160 | tf_op jit(solution)/shard_map/ppermute | solution.py:317
  73.9 4.7 %collective-permute-start.21 = (bf16[32,256]{1,0:T(8,128)(2,1)S(1)}, bf16[32,256]{1,0:T(8,128)(2,1)S(1)}, u32[]{:S(2)}, u32[]{:S(2)}) collective-permute-start(bf16[32,256]{1,0:T(8,128)(2,1)S(1)} %get-tuple-element.162), channel_id=1, source_target_pairs={{0,32},{32,0},{64,96},{96,64},{128,160},{160,128},{192,224},{224,1... | collective-permute-start | bytes 49160 | tf_op jit(solution)/shard_map/ppermute | solution.py:318
  73.9 4.7 %collective-permute-start.22 = (bf16[32,256]{1,0:T(8,128)(2,1)S(1)}, bf16[32,256]{1,0:T(8,128)(2,1)S(1)}, u32[]{:S(2)}, u32[]{:S(2)}) collective-permute-start(bf16[32,256]{1,0:T(8,128)(2,1)S(1)} %get-tuple-element.163), channel_id=1, source_target_pairs={{1,2},{3,4},{5,6},{7,8},{9,10},{11,12},{13,14},{15,16},{17,18},{19... | collective-permute-start | bytes 49160 | tf_op jit(solution)/shard_map/ppermute | solution.py:319
  73.9 5.6 %collective-permute-start.23 = (bf16[32,256]{1,0:T(8,128)(2,1)S(1)}, bf16[32,256]{1,0:T(8,128)(2,1)S(1)}, u32[]{:S(2)}, u32[]{:S(2)}) collective-permute-start(bf16[32,256]{1,0:T(8,128)(2,1)S(1)} %get-tuple-element.164), channel_id=1, source_target_pairs={{0,1},{1,0},{2,3},{3,2},{4,5},{5,4},{6,7},{7,6},{8,9},{9,8},{10,11... | collective-permute-start | bytes 49160 | tf_op jit(solution)/shard_map/ppermute | solution.py:320
  80.9 11.0 %collective-permute-start.24 = (bf16[32,256]{1,0:T(8,128)(2,1)S(1)}, bf16[32,256]{1,0:T(8,128)(2,1)S(1)}, u32[]{:S(2)}, u32[]{:S(2)}) collective-permute-start(bf16[32,256]{1,0:T(8,128)(2,1)S(1)} %get-tuple-element.170), channel_id=1, source_target_pairs={{32,64},{96,128},{160,192},{224,0},{64,32},{128,96},{192,160},{0,2... | collective-permute-start | bytes 49160 | tf_op jit(solution)/shard_map/ppermute | solution.py:317
  84.2 7.7 %collective-permute-start.25 = (bf16[32,256]{1,0:T(8,128)(2,1)S(1)}, bf16[32,256]{1,0:T(8,128)(2,1)S(1)}, u32[]{:S(2)}, u32[]{:S(2)}) collective-permute-start(bf16[32,256]{1,0:T(8,128)(2,1)S(1)} %get-tuple-element.171), channel_id=1, source_target_pairs={{0,32},{32,0},{64,96},{96,64},{128,160},{160,128},{192,224},{224,1... | collective-permute-start | bytes 49160 | tf_op jit(solution)/shard_map/ppermute | solution.py:318
  84.7 7.2 %collective-permute-start.26 = (bf16[32,256]{1,0:T(8,128)(2,1)S(1)}, bf16[32,256]{1,0:T(8,128)(2,1)S(1)}, u32[]{:S(2)}, u32[]{:S(2)}) collective-permute-start(bf16[32,256]{1,0:T(8,128)(2,1)S(1)} %get-tuple-element.172), channel_id=1, source_target_pairs={{1,2},{3,4},{5,6},{7,8},{9,10},{11,12},{13,14},{15,16},{17,18},{19... | collective-permute-start | bytes 49160 | tf_op jit(solution)/shard_map/ppermute | solution.py:319
  84.7 7.2 %collective-permute-start.27 = (bf16[32,256]{1,0:T(8,128)(2,1)S(1)}, bf16[32,256]{1,0:T(8,128)(2,1)S(1)}, u32[]{:S(2)}, u32[]{:S(2)}) collective-permute-start(bf16[32,256]{1,0:T(8,128)(2,1)S(1)} %get-tuple-element.173), channel_id=1, source_target_pairs={{0,1},{1,0},{2,3},{3,2},{4,5},{5,4},{6,7},{7,6},{8,9},{9,8},{10,11... | collective-permute-start | bytes 49160 | tf_op jit(solution)/shard_map/ppermute | solution.py:320
  94.6 4.6 %collective-permute-start.32 = (bf16[1024,256]{1,0:T(8,128)(2,1)S(1)}, bf16[1024,256]{1,0:T(8,128)(2,1)S(1)}, u32[]{:S(2)}, u32[]{:S(2)}) collective-permute-start(bf16[1024,256]{1,0:T(8,128)(2,1)S(1)} %slice_bitcast_fusion), channel_id=1, source_target_pairs={{0,1},{1,0},{2,3},{3,2},{4,5},{5,4},{6,7},{7,6},{8,9},{9,8},{10,11... | collective-permute-start | bytes 1572872 | tf_op jit(solution)/shard_map/ppermute | solution.py:326
  141.7 11.9 %collective-permute-start.33 = (bf16[1024,256]{1,0:T(8,128)(2,1)S(1)}, bf16[1024,256]{1,0:T(8,128)(2,1)S(1)}, u32[]{:S(2)}, u32[]{:S(2)}) collective-permute-start(bf16[1024,256]{1,0:T(8,128)(2,1)S(1)} %bitcast.13), channel_id=1, source_target_pairs={{0,1},{1,0},{2,3},{3,2},{4,5},{5,4},{6,7},{7,6},{8,9},{9,8},{10,11... | collective-permute-start | bytes 1572872 | tf_op jit(solution)/shard_map/ppermute | solution.py:335
  146.5 6.3 %collective-permute-start.28 = (bf16[32,256]{1,0:T(8,128)(2,1)S(1)}, bf16[32,256]{1,0:T(8,128)(2,1)S(1)}, u32[]{:S(2)}, u32[]{:S(2)}) collective-permute-start(bf16[32,256]{1,0:T(8,128)(2,1)S(1)} %get-tuple-element.179), channel_id=1, source_target_pairs={{32,64},{96,128},{160,192},{224,0},{64,32},{128,96},{192,160},{0,2... | collective-permute-start | bytes 49160 | tf_op jit(solution)/shard_map/ppermute | solution.py:317
  147.8 5.0 %collective-permute-start.29 = (bf16[32,256]{1,0:T(8,128)(2,1)S(1)}, bf16[32,256]{1,0:T(8,128)(2,1)S(1)}, u32[]{:S(2)}, u32[]{:S(2)}) collective-permute-start(bf16[32,256]{1,0:T(8,128)(2,1)S(1)} %get-tuple-element.180), channel_id=1, source_target_pairs={{0,32},{32,0},{64,96},{96,64},{128,160},{160,128},{192,224},{224,1... | collective-permute-start | bytes 49160 | tf_op jit(solution)/shard_map/ppermute | solution.py:318
  148.6 4.2 %collective-permute-start.30 = (bf16[32,256]{1,0:T(8,128)(2,1)S(1)}, bf16[32,256]{1,0:T(8,128)(2,1)S(1)}, u32[]{:S(2)}, u32[]{:S(2)}) collective-permute-start(bf16[32,256]{1,0:T(8,128)(2,1)S(1)} %get-tuple-element.181), channel_id=1, source_target_pairs={{1,2},{3,4},{5,6},{7,8},{9,10},{11,12},{13,14},{15,16},{17,18},{19... | collective-permute-start | bytes 49160 | tf_op jit(solution)/shard_map/ppermute | solution.py:319
  149.2 3.5 %collective-permute-start.31 = (bf16[32,256]{1,0:T(8,128)(2,1)S(1)}, bf16[32,256]{1,0:T(8,128)(2,1)S(1)}, u32[]{:S(2)}, u32[]{:S(2)}) collective-permute-start(bf16[32,256]{1,0:T(8,128)(2,1)S(1)} %get-tuple-element.182), channel_id=1, source_target_pairs={{0,1},{1,0},{2,3},{3,2},{4,5},{5,4},{6,7},{7,6},{8,9},{9,8},{10,11... | collective-permute-start | bytes 49160 | tf_op jit(solution)/shard_map/ppermute | solution.py:320
  (20 other events, 100.5 us)

commit v2 on v1

--- a/solution.py
+++ b/solution.py
@@ -44,9 +44,11 @@
     return 0.5 * jnp.tanh(0.5 * v) + 0.5
 
 
-def call(kernel, outs, *args, smem=0, **kw):
-    specs = [pl.BlockSpec(memory_space=pltpu.SMEM)] * smem
-    specs += [pl.BlockSpec(memory_space=pltpu.VMEM)] * (len(args) - smem)
+def call(kernel, outs, *args, space=pltpu.VMEM, scalars=0, **kw):
+    specs = [pl.BlockSpec(memory_space=pltpu.SMEM)] * scalars
+    specs += [pl.BlockSpec(memory_space=space)] * (len(args) - scalars)
+    if space is pltpu.HBM:
+        args = args[:scalars] + tuple(pltpu.with_memory_space_constraint(a, space) for a in args[scalars:])
     return pl.pallas_call(
         kernel,
         out_shape=[jax.ShapeDtypeStruct(s, d) for s, d in outs],
@@ -57,9 +59,9 @@
     )(*args)
 
 
-def slot_lists(place, lists):
-    slab_odd = place[1] % 2
-    region_odd = place[0] % 2
+def slot_lists(lists):
+    slab_odd = lax.axis_index("c")
+    region_odd = lax.axis_index("yh")
     a, b, c, d = (lists[i : i + 1, :] for i in range(4))
     return (
         jnp.where(region_odd == 1, d, c),
@@ -69,42 +71,57 @@
     )
 
 
-def first_kernel(place, nodes, lists, s0, s1, s2, s3, spread):
-    h = nodes[...]
+def first_kernel(nodes, lists, s0, s1, s2, s3, spread, h, rows, sems):
+    copies = [pltpu.make_async_copy(nodes, h, sems.at[0]), pltpu.make_async_copy(lists, rows, sems.at[1])]
+    for copy in copies:
+        copy.start()
+    for copy in copies:
+        copy.wait()
     row = lax.broadcasted_iota(jnp.int32, (OWN, HALO), 0)
-    for i, (idx, out) in enumerate(zip(slot_lists(place, lists[...]), (s0, s1, s2, s3))):
+    for i, (idx, out) in enumerate(zip(slot_lists(rows[...]), (s0, s1, s2, s3))):
         hot = (row == idx).astype(F32).astype(BF16)
         spread[:, i * HALO : (i + 1) * HALO] = hot
-        out[...] = mm_t(hot, h).astype(BF16)
+        out[...] = mm_t(hot, h[...]).astype(BF16)
 
 
 def prep_kernel(
-    place, count, send_idx, recv_idx, feats, edge_w1, edge_w2, node_w1, node_w2,
+    count, send_in, recv_in, gain_in, w1_in, feats_in, n1_in, w2_in, n2_in, cot_in, nodes_in,
     t_out, tt_out, s_out, st_out, fw_out, w1t_out, w2t_out, n1t_out, n2t_out,
-):
+    gain_out, w1, feats, n1, w2, n2, cot, nodes,
+    send_idx, recv_idx, gain, sems,
+):
+    pairs = (
+        (w1_in, w1), (feats_in, feats), (send_in, send_idx), (recv_in, recv_idx),
+        (n1_in, n1), (w2_in, w2), (n2_in, n2), (nodes_in, nodes), (gain_in, gain), (cot_in, cot),
+    )
+    copies = [pltpu.make_async_copy(a, b, sems.at[i]) for i, (a, b) in enumerate(pairs)]
+    for copy in copies:
+        copy.start()
+    for copy in copies:
+        copy.wait()
     edges = feats.shape[0]
     lane = lax.broadcasted_iota(jnp.int32, (1, edges), 1)
     live = lane < count[0, 0]
-    snd = send_idx[...]
+    snd = send_idx[...].reshape(1, edges)
     off = snd - OWN
-    slab_swap = jnp.where(place[1] % 2 == 1, 3 * HALO, 2 * HALO)
-    region_swap = jnp.where(place[0] % 2 == 1, 3 * HALO, 2 * HALO)
+    slab_swap = jnp.where(lax.axis_index("c") == 1, 3 * HALO, 2 * HALO)
+    region_swap = jnp.where(lax.axis_index("yh") == 1, 3 * HALO, 2 * HALO)
     flip = jnp.where(off < 2 * HALO, slab_swap, region_swap)
     snd = jnp.where(off >= 0, OWN + (off ^ flip), snd)
     snd = jnp.where(live, snd, -1)
-    rcv = jnp.where(live, recv_idx[...], -1)
+    rcv = jnp.where(live, recv_idx[...].reshape(1, edges), -1)
     tt = (lax.broadcasted_iota(jnp.int32, (2 * OWN, edges), 0) == snd).astype(F32)
     st = (lax.broadcasted_iota(jnp.int32, (OWN, edges), 0) == rcv).astype(F32)
     tt_out[...] = tt.astype(BF16)
     st_out[...] = st.astype(BF16)
     t_out[...] = tt.T.astype(BF16)
     s_out[...] = st.T.astype(BF16)
-    w1 = edge_w1[...]
     fw_out[...] = mm(feats[...], w1[2 * L :])
-    w1t_out[...] = w1.T
-    w2t_out[...] = edge_w2[...].T
-    n1t_out[...] = node_w1[...].T
-    n2t_out[...] = node_w2[...].T
+    w1t_out[...] = w1[...].T
+    w2t_out[...] = w2[...].T
+    n1t_out[...] = n1[...].T
+    n2t_out[...] = n2[...].T
+    gain_out[...] = gain[...].reshape(1, L)
 
 
 def forward_body(h, halo, t, s, st, fw, edge_w1, edge_w2, node_w1, node_w2):
@@ -267,9 +284,9 @@
     gain_acc[...] = gain_acc_in[...] + gain_in[...]
 
 
-def weight_last_kernel(place, *refs):
+def weight_last_kernel(*refs):
     gain_in, acc_in, gain_acc_in, out = refs[15:]
-    core = place[1] % 2
+    core = lax.axis_index("c")
     terms = weight_args(refs[:15])
     for i, term in enumerate(terms):
         out[(i // 4) ^ core, (i % 4) * L : (i % 4 + 1) * L, :] = (acc_in[i] + term).astype(BF16)
@@ -286,8 +303,8 @@
     out[...] = landed(own, spread, p0, p1, p2, p3)
 
 
-def finish_kernel(factor, place, mine, other, edge_in, edge_out, node_in, node_out, gain):
-    core = place[1] % 2
+def finish_kernel(factor, mine, other, edge_in, edge_out, node_in, node_out, gain):
+    core = lax.axis_index("c")
 
     def half(index, lo, hi):
         a = mine[lo:hi].astype(F32)
@@ -298,7 +315,7 @@
     edge_out[...] = half(0, 3 * L, 4 * L)
     node_in[...] = half(1, 0, 2 * L)
     node_out[...] = half(1, 2 * L, 3 * L)
-    gain[...] = half(1, 3 * L, 3 * L + 8)
+    gain[...] = half(1, 3 * L, 3 * L + 8)[0]
 
 
 def even_pairs(size):
@@ -321,39 +338,46 @@
     ]
 
 
-def reduce_all(payload):
+def reduce_all(payload, back):
     keep = payload[0].astype(F32)
     got = lax.ppermute(payload[1], "c", [(0, 1), (1, 0)])
     part = (keep + got.astype(F32)).astype(BF16).reshape(CHUNKS, CHUNK_ROWS, L)
     part = lax.all_to_all(part, PLANE, 0, 0, tiled=True)
     part = jnp.sum(part.astype(F32), axis=0).astype(BF16)
+    part, *back = lax.optimization_barrier((part, *back))
     deep = lax.axis_size("z")
     part = lax.all_to_all(jnp.broadcast_to(part[None], (deep,) + part.shape), "z", 0, 0, tiled=True)
     part = jnp.sum(part.astype(F32), axis=0).astype(BF16)
     part = jnp.broadcast_to(part[None], (CHUNKS,) + part.shape)
     mine = lax.all_to_all(part, PLANE, 0, 0, tiled=True).reshape(CHUNKS * CHUNK_ROWS, L)
     other = lax.ppermute(mine, "c", [(0, 1), (1, 0)])
-    return mine, other
+    return mine, other, back
 
 
 def local(
     nodes, feats, cotangent, edge_w1, edge_w2, node_w1, node_w2, ln_gain, senders, receivers, send_rows, edge_count
 ):
     edges = feats.shape[0]
-    place = jnp.stack([lax.axis_index(REGION), lax.axis_index(SLAB)]).astype(jnp.int32)
-    gain = ln_gain.reshape(1, L)
     halo_outs = [((HALO, L), BF16)] * 4
     *sends, spread = call(
-        first_kernel, halo_outs + [((OWN, 4 * HALO), BF16)], place, nodes, send_rows, smem=1
-    )
-    t, tt, s, st, fw, w1t, w2t, n1t, n2t = call(
+        first_kernel, halo_outs + [((OWN, 4 * HALO), BF16)], nodes, send_rows, space=pltpu.HBM,
+        scratch_shapes=[pltpu.VMEM((OWN, L), BF16), pltpu.VMEM((4, HALO), jnp.int32), pltpu.SemaphoreType.DMA((2,))],
+    )
+    t, tt, s, st, fw, w1t, w2t, n1t, n2t, gain, edge_w1, feats, node_w1, edge_w2, node_w2, cotangent, nodes = call(
         prep_kernel,
         [
             ((edges, 2 * OWN), BF16), ((2 * OWN, edges), BF16), ((edges, OWN), BF16), ((OWN, edges), BF16),
             ((edges, L), F32), ((L, 3 * L), BF16), ((L, L), BF16), ((L, 2 * L), BF16), ((L, L), BF16),
+            ((1, L), F32), ((3 * L, L), BF16), ((edges, L), BF16), ((2 * L, L), BF16), ((L, L), BF16), ((L, L), BF16),
+            ((OWN, L), F32), ((OWN, L), BF16),
         ],
-        place, edge_count, senders.reshape(1, edges), receivers.reshape(1, edges), feats, edge_w1, edge_w2, node_w1, node_w2,
-        smem=2,
+        edge_count, senders, receivers, ln_gain, edge_w1, feats, node_w1, edge_w2, node_w2, cotangent, nodes,
+        space=pltpu.HBM,
+        scalars=1,
+        scratch_shapes=[
+            pltpu.VMEM((edges,), jnp.int32), pltpu.VMEM((edges,), jnp.int32),
+            pltpu.VMEM((L,), F32), pltpu.SemaphoreType.DMA((10,)),
+        ],
     )
     h = nodes
     saved = []
@@ -397,9 +421,9 @@
         if layer > 0:
             totals = call(weight_kernel, acc_outs, *shared, w1t, gain_term, *totals)
     (payload,) = call(
-        weight_last_kernel, [((2, 4 * L, L), BF16)], place, *shared, gain_term, totals[0], totals[2], smem=1
-    )
-    mine, other = reduce_all(payload)
+        weight_last_kernel, [((2, 4 * L, L), BF16)], *shared, gain_term, totals[0], totals[2]
+    )
+    mine, other, back = reduce_all(payload, back)
     (edge_grad,) = call(edge_last_kernel, [((edges, L), F32)], terms[0], w1t, totals[1])
     (node_grad,) = call(node_last_kernel, [((OWN, L), F32)], own, *back, spread)
     devices = lax.axis_size(REGION) * lax.axis_size(SLAB)
@@ -409,9 +433,9 @@
         finish_kernel(factor, *refs)
 
     edge_in, edge_out, node_in, node_out, gain_grad = call(
-        finish, [((3 * L, L), F32), ((L, L), F32), ((2 * L, L), F32), ((L, L), F32), ((8, L), F32)], place, mine, other, smem=1
-    )
-    return node_grad, edge_grad, edge_in, edge_out, node_in, node_out, gain_grad[0]
+        finish, [((3 * L, L), F32), ((L, L), F32), ((2 * L, L), F32), ((L, L), F32), ((L,), F32)], mine, other
+    )
+    return node_grad, edge_grad, edge_in, edge_out, node_in, node_out, gain_grad
 
 
 def solution(mesh):

time: 158 us -> 143 us (0.905)
  blocking collectives: 42.1 us -> 29.4 us
  local copies, waits for them, and re-layouts: 12.7 us -> 0.1 us
  starting transfers between devices: 67.6 us -> 78.3 us
    all_to_all x1 -> x0, blocking collectives: 16.3 us -> none  [reduce_all(): part = lax.all_to_all(part, PLANE, 0, 0, tiled=True)]
    unnamed x36 -> x0, local copies, waits for them, and re-layouts: 10.6 us -> none
    all_to_all x0 -> x1, starting transfers between devices: none -> 6.13 us  [reduce_all(): part = lax.all_to_all(part, PLANE, 0, 0, tiled=True)]
    ppermute x8, starting transfers between devices: 27.5 us -> 32 us  [exchange(): lax.ppermute(parts[0], REGION, odd_pairs(regions))]
    ppermute x8, waiting for transfers between devices: 4.27 us -> 0.48 us  [exchange(): lax.ppermute(parts[0], REGION, odd_pairs(regions))]
    all_to_all x0 -> x1, waiting for transfers between devices: none -> 3.74 us  [reduce_all(): part = lax.all_to_all(part, PLANE, 0, 0, tiled=True)]
    all_to_all x1, blocking collectives: 12.5 us -> 14.8 us  [reduce_all(): lax.all_to_all(part, PLANE, 0, 0, tiled=True)]
    ppermute x8, starting transfers between devices: 25.6 us -> 27.8 us  [exchange(): lax.ppermute(parts[3], SLAB, even_pairs(slabs))]
  transfers between devices with their start and end apart: 34 -> 35, of which waited for: 10 -> 9; matrix products, arithmetic and copies ran while one was open for 1% -> 0% of each run, Pallas kernels for 3% -> 4%
where the time goes in v2:
time: 143 us; the launch traced here: 142 us
  starting transfers between devices  78.3 us (55%)
  blocking collectives  29.4 us (21%)
  Pallas kernels  21 us (15%)
  waiting for transfers between devices  10.8 us (8%)
  between operations  1.52 us (1%)
    ppermute x8, starting transfers between devices, exchange(): lax.ppermute(parts[0], REGION, odd_pairs(regions))  32 us
    ppermute x8, starting transfers between devices, exchange(): lax.ppermute(parts[3], SLAB, even_pairs(slabs))  27.8 us
    pallas_call x16, Pallas kernels, call(): pl.pallas_call(kernel, out_shape=[jax.ShapeDtypeStruct(s, d) for s, d in...  21 us
    all_to_all x1, blocking collectives, reduce_all(): lax.all_to_all(part, PLANE, 0, 0, tiled=True)  14.8 us
    all_to_all x1, blocking collectives, reduce_all(): lax.all_to_all(jnp.broadcast_to(part[None], (deep,) + part.shape), 'z', 0...  14.6 us
    all_to_all x1, starting transfers between devices, reduce_all(): part = lax.all_to_all(part, PLANE, 0, 0, tiled=True)  6.13 us
    all_to_all x1, waiting for transfers between devices, reduce_all(): part = lax.all_to_all(part, PLANE, 0, 0, tiled=True)  3.74 us
    ppermute x1, starting transfers between devices, reduce_all(): other = lax.ppermute(mine, 'c', [(0, 1), (1, 0)])  3.58 us
  transfers between devices with their start and end apart: 35, of which 9 were waited for; matrix products, arithmetic and copies ran while one was open for 0% of the time, Pallas kernels for 4%

profile of v2, /device:TPU:1, one launch (start us, length us, event | category | flops | bytes accessed | tf_op | source)
XLA Modules:
  0.0 142.2 jit_solution(2047712157187170414)
XLA Ops:
  1.7 6.0 %collective-permute-start = (bf16[32,256]{1,0:T(8,128)(2,1)S(1)}, bf16[32,256]{1,0:T(8,128)(2,1)S(1)}, u32[]{:S(2)}, u32[]{:S(2)}) collective-permute-start(bf16[32,256]{1,0:T(8,128)(2,1)S(1)} %get-tuple-element.136), channel_id=1, source_target_pairs={{32,64},{96,128},{160,192},{224,0},{64,32},{128,96},{192,160},{0,2... | collective-permute-start | bytes 49160 | tf_op jit(solution)/shard_map/ppermute | solution.py:334
  9.0 4.8 %collective-permute-start.3 = (bf16[32,256]{1,0:T(8,128)(2,1)S(1)}, bf16[32,256]{1,0:T(8,128)(2,1)S(1)}, u32[]{:S(2)}, u32[]{:S(2)}) collective-permute-start(bf16[32,256]{1,0:T(8,128)(2,1)S(1)} %get-tuple-element.139), channel_id=1, source_target_pairs={{0,1},{1,0},{2,3},{3,2},{4,5},{5,4},{6,7},{7,6},{8,9},{9,8},{10,11... | collective-permute-start | bytes 49160 | tf_op jit(solution)/shard_map/ppermute | solution.py:337
  14.5 1.9 %shard_map.171 = (bf16[640,256]{1,0:T(8,128)(2,1)S(1)}, bf16[256,640]{1,0:T(8,128)(2,1)S(1)}, bf16[640,128]{1,0:T(8,128)(2,1)S(1)}, bf16[128,640]{1,0:T(8,128)(2...) custom-call(s32[1,1]{1,0:T(1,128)S(6)} %copy.19.count, ...), custom_call_target="tpu_custom_call" | custom-call | tf_op jit(solution)/shard_map/pallas_call | solution.py:52
  16.5 1.6 %shard_map.173 = (bf16[128,256]{1,0:T(8,128)(2,1)S(1)}, bf16[32,256]{1,0:T(8,128)(2,1)S(1)}, bf16[32,256]{1,0:T(8,128)(2,1)S(1)}, bf16[32,256]{1,0:T(8,128)(2,1)...) custom-call(bf16[128,256]{1,0:T(8,128)(2,1)S(1)} %get-tuple-element., ...), custom_call_target="tpu_custom_call" | custom-call | tf_op jit(solution)/shard_map/pallas_call | solution.py:52
  18.1 3.9 %collective-permute-start.4 = (bf16[32,256]{1,0:T(8,128)(2,1)S(1)}, bf16[32,256]{1,0:T(8,128)(2,1)S(1)}, u32[]{:S(2)}, u32[]{:S(2)}) collective-permute-start(bf16[32,256]{1,0:T(8,128)(2,1)S(1)} %get-tuple-element.151), channel_id=1, source_target_pairs={{32,64},{96,128},{160,192},{224,0},{64,32},{128,96},{192,160},{0,2... | collective-permute-start | bytes 49160 | tf_op jit(solution)/shard_map/ppermute | solution.py:334
  22.0 2.4 %collective-permute-start.7 = (bf16[32,256]{1,0:T(8,128)(2,1)S(1)}, bf16[32,256]{1,0:T(8,128)(2,1)S(1)}, u32[]{:S(2)}, u32[]{:S(2)}) collective-permute-start(bf16[32,256]{1,0:T(8,128)(2,1)S(1)} %get-tuple-element.154), channel_id=1, source_target_pairs={{0,1},{1,0},{2,3},{3,2},{4,5},{5,4},{6,7},{7,6},{8,9},{9,8},{10,11... | collective-permute-start | bytes 49160 | tf_op jit(solution)/shard_map/ppermute | solution.py:337
  24.4 1.7 %collective-permute-done.5.p1.refs_2_ = bf16[32,256]{1,0:T(8,128)(2,1)S(1)} collective-permute-done((bf16[32,256]{1,0:T(8,128)(2,1)S(1)}, bf16[32,256]{1,0:T(8,128)(2,1)S(1)}, u32[]{:S(2)}, u32[]{:S(2)}) %collective-permute-start.5) | collective-permute-done | bytes 16416 | tf_op jit(solution)/shard_map/ppermute | solution.py:335
  26.1 1.6 %shard_map.174 = (bf16[128,256]{1,0:T(8,128)(2,1)S(1)}, bf16[32,256]{1,0:T(8,128)(2,1)S(1)}, bf16[32,256]{1,0:T(8,128)(2,1)S(1)}, bf16[32,256]{1,0:T(8,128)(2,1)...) custom-call(bf16[128,256]{1,0:T(8,128)(2,1)S(1)} %get-tuple-element., ...), custom_call_target="tpu_custom_call" | custom-call | tf_op jit(solution)/shard_map/pallas_call | solution.py:52
  27.7 2.4 %collective-permute-start.8 = (bf16[32,256]{1,0:T(8,128)(2,1)S(1)}, bf16[32,256]{1,0:T(8,128)(2,1)S(1)}, u32[]{:S(2)}, u32[]{:S(2)}) collective-permute-start(bf16[32,256]{1,0:T(8,128)(2,1)S(1)} %get-tuple-element.156), channel_id=1, source_target_pairs={{32,64},{96,128},{160,192},{224,0},{64,32},{128,96},{192,160},{0,2... | collective-permute-start | bytes 49160 | tf_op jit(solution)/shard_map/ppermute | solution.py:334
  31.4 3.6 %collective-permute-start.11 = (bf16[32,256]{1,0:T(8,128)(2,1)S(1)}, bf16[32,256]{1,0:T(8,128)(2,1)S(1)}, u32[]{:S(2)}, u32[]{:S(2)}) collective-permute-start(bf16[32,256]{1,0:T(8,128)(2,1)S(1)} %get-tuple-element.159), channel_id=1, source_target_pairs={{0,1},{1,0},{2,3},{3,2},{4,5},{5,4},{6,7},{7,6},{8,9},{9,8},{10,11... | collective-permute-start | bytes 49160 | tf_op jit(solution)/shard_map/ppermute | solution.py:337
  35.8 1.6 %shard_map.175 = (bf16[128,256]{1,0:T(8,128)(2,1)S(1)}, bf16[32,256]{1,0:T(8,128)(2,1)S(1)}, bf16[32,256]{1,0:T(8,128)(2,1)S(1)}, bf16[32,256]{1,0:T(8,128)(2,1)...) custom-call(bf16[128,256]{1,0:T(8,128)(2,1)S(1)} %get-tuple-element., ...), custom_call_target="tpu_custom_call" | custom-call | tf_op jit(solution)/shard_map/pallas_call | solution.py:52
  37.4 2.6 %collective-permute-start.12 = (bf16[32,256]{1,0:T(8,128)(2,1)S(1)}, bf16[32,256]{1,0:T(8,128)(2,1)S(1)}, u32[]{:S(2)}, u32[]{:S(2)}) collective-permute-start(bf16[32,256]{1,0:T(8,128)(2,1)S(1)} %get-tuple-element.161), channel_id=1, source_target_pairs={{32,64},{96,128},{160,192},{224,0},{64,32},{128,96},{192,160},{0,2... | collective-permute-start | bytes 49160 | tf_op jit(solution)/shard_map/ppermute | solution.py:334
  41.1 3.8 %collective-permute-start.15 = (bf16[32,256]{1,0:T(8,128)(2,1)S(1)}, bf16[32,256]{1,0:T(8,128)(2,1)S(1)}, u32[]{:S(2)}, u32[]{:S(2)}) collective-permute-start(bf16[32,256]{1,0:T(8,128)(2,1)S(1)} %get-tuple-element.164), channel_id=1, source_target_pairs={{0,1},{1,0},{2,3},{3,2},{4,5},{5,4},{6,7},{7,6},{8,9},{9,8},{10,11... | collective-permute-start | bytes 49160 | tf_op jit(solution)/shard_map/ppermute | solution.py:337
  45.7 2.8 %shard_map.176 = (f32[128,256]{1,0:T(8,128)S(1)}, bf16[32,256]{1,0:T(8,128)(2,1)S(1)}, bf16[32,256]{1,0:T(8,128)(2,1)S(1)}, bf16[32,256]{1,0:T(8,128)(2,1)S(1)},...) custom-call(bf16[128,256]{1,0:T(8,128)(2,1)S(1)} %get-tuple-element., ...), custom_call_target="tpu_custom_call" | custom-call | tf_op jit(solution)/shard_map/pallas_call | solution.py:52
  48.5 4.9 %collective-permute-start.16 = (bf16[32,256]{1,0:T(8,128)(2,1)S(1)}, bf16[32,256]{1,0:T(8,128)(2,1)S(1)}, u32[]{:S(2)}, u32[]{:S(2)}) collective-permute-start(bf16[32,256]{1,0:T(8,128)(2,1)S(1)} %get-tuple-element.172), channel_id=1, source_target_pairs={{32,64},{96,128},{160,192},{224,0},{64,32},{128,96},{192,160},{0,2... | collective-permute-start | bytes 49160 | tf_op jit(solution)/shard_map/ppermute | solution.py:334
  53.4 3.8 %collective-permute-start.19 = (bf16[32,256]{1,0:T(8,128)(2,1)S(1)}, bf16[32,256]{1,0:T(8,128)(2,1)S(1)}, u32[]{:S(2)}, u32[]{:S(2)}) collective-permute-start(bf16[32,256]{1,0:T(8,128)(2,1)S(1)} %get-tuple-element.175), channel_id=1, source_target_pairs={{0,1},{1,0},{2,3},{3,2},{4,5},{5,4},{6,7},{7,6},{8,9},{9,8},{10,11... | collective-permute-start | bytes 49160 | tf_op jit(solution)/shard_map/ppermute | solution.py:337
  58.0 1.4 shard_map.177
  59.5 3.9 %collective-permute-start.20 = (bf16[32,256]{1,0:T(8,128)(2,1)S(1)}, bf16[32,256]{1,0:T(8,128)(2,1)S(1)}, u32[]{:S(2)}, u32[]{:S(2)}) collective-permute-start(bf16[32,256]{1,0:T(8,128)(2,1)S(1)} %get-tuple-element.181), channel_id=1, source_target_pairs={{32,64},{96,128},{160,192},{224,0},{64,32},{128,96},{192,160},{0,2... | collective-permute-start | bytes 49160 | tf_op jit(solution)/shard_map/ppermute | solution.py:334
  63.4 4.4 %collective-permute-start.23 = (bf16[32,256]{1,0:T(8,128)(2,1)S(1)}, bf16[32,256]{1,0:T(8,128)(2,1)S(1)}, u32[]{:S(2)}, u32[]{:S(2)}) collective-permute-start(bf16[32,256]{1,0:T(8,128)(2,1)S(1)} %get-tuple-element.184), channel_id=1, source_target_pairs={{0,1},{1,0},{2,3},{3,2},{4,5},{5,4},{6,7},{7,6},{8,9},{9,8},{10,11... | collective-permute-start | bytes 49160 | tf_op jit(solution)/shard_map/ppermute | solution.py:337
  68.6 1.4 shard_map.178
  70.0 3.2 %collective-permute-start.24 = (bf16[32,256]{1,0:T(8,128)(2,1)S(1)}, bf16[32,256]{1,0:T(8,128)(2,1)S(1)}, u32[]{:S(2)}, u32[]{:S(2)}) collective-permute-start(bf16[32,256]{1,0:T(8,128)(2,1)S(1)} %get-tuple-element.190), channel_id=1, source_target_pairs={{32,64},{96,128},{160,192},{224,0},{64,32},{128,96},{192,160},{0,2... | collective-permute-start | bytes 49160 | tf_op jit(solution)/shard_map/ppermute | solution.py:334
  73.8 5.0 %collective-permute-start.27 = (bf16[32,256]{1,0:T(8,128)(2,1)S(1)}, bf16[32,256]{1,0:T(8,128)(2,1)S(1)}, u32[]{:S(2)}, u32[]{:S(2)}) collective-permute-start(bf16[32,256]{1,0:T(8,128)(2,1)S(1)} %get-tuple-element.193), channel_id=1, source_target_pairs={{0,1},{1,0},{2,3},{3,2},{4,5},{5,4},{6,7},{7,6},{8,9},{9,8},{10,11... | collective-permute-start | bytes 49160 | tf_op jit(solution)/shard_map/ppermute | solution.py:337
  81.0 1.4 %shard_map.179 = (f32[128,256]{1,0:T(8,128)S(1)}, bf16[32,256]{1,0:T(8,128)(2,1)S(1)}, bf16[32,256]{1,0:T(8,128)(2,1)S(1)}, bf16[32,256]{1,0:T(8,128)(2,1)S(1)},...) custom-call(f32[128,256]{1,0:T(8,128)S(1)} %get-tuple-element.189.ow, ...), custom_call_target="tpu_custom_call" | custom-call | tf_op jit(solution)/shard_map/pallas_call | solution.py:52
  83.1 3.1 %collective-permute-start.28 = (bf16[1024,256]{1,0:T(8,128)(2,1)S(1)}, bf16[1024,256]{1,0:T(8,128)(2,1)S(1)}, u32[]{:S(2)}, u32[]{:S(2)}) collective-permute-start(bf16[1024,256]{1,0:T(8,128)(2,1)S(1)} %slice_bitcast_fusion), channel_id=1, source_target_pairs={{0,1},{1,0},{2,3},{3,2},{4,5},{5,4},{6,7},{7,6},{8,9},{9,8},{10,11... | collective-permute-start | bytes 1572872 | tf_op jit(solution)/shard_map/ppermute | solution.py:343
  86.3 1.5 %collective-permute-done.28 = bf16[1024,256]{1,0:T(8,128)(2,1)S(1)} collective-permute-done((bf16[1024,256]{1,0:T(8,128)(2,1)S(1)}, bf16[1024,256]{1,0:T(8,128)(2,1)S(1)}, u32[]{:S(2)}, u32[]{:S(2)}) %collective-permute-start.28) | collective-permute-done | bytes 524320 | tf_op jit(solution)/shard_map/ppermute | solution.py:343
  88.7 6.1 %all-to-all-start = ((bf16[16,64,256]{2,1,0:T(8,128)(2,1)}), bf16[16,64,256]{2,1,0:T(8,128)(2,1)S(1)}, u32[]{:S(2)}, u32[]{:S(2)}) async-start(bf16[16,64,256]{2,1,0:T(8,128)(2,1)} %bitcast.2), calls=%async_computation | async-start | bytes 1048576 | tf_op jit(solution)/shard_map/all_to_all | solution.py:345
  94.9 5.0 %collective-permute-start.29 = (bf16[32,256]{1,0:T(8,128)(2,1)S(1)}, bf16[32,256]{1,0:T(8,128)(2,1)S(1)}, u32[]{:S(2)}, u32[]{:S(2)}) collective-permute-start(bf16[32,256]{1,0:T(8,128)(2,1)S(1)} %get-tuple-element.248), channel_id=1, source_target_pairs={{32,64},{96,128},{160,192},{224,0},{64,32},{128,96},{192,160},{0,2... | collective-permute-start | bytes 49160 | tf_op jit(solution)/shard_map/ppermute | solution.py:334
  99.9 1.6 %collective-permute-start.31 = (bf16[32,256]{1,0:T(8,128)(2,1)S(1)}, bf16[32,256]{1,0:T(8,128)(2,1)S(1)}, u32[]{:S(2)}, u32[]{:S(2)}) collective-permute-start(bf16[32,256]{1,0:T(8,128)(2,1)S(1)} %get-tuple-element.250), channel_id=1, source_target_pairs={{1,2},{3,4},{5,6},{7,8},{9,10},{11,12},{13,14},{15,16},{17,18},{19... | collective-permute-start | bytes 49160 | tf_op jit(solution)/shard_map/ppermute | solution.py:336
  101.5 3.7 %all-to-all-done = bf16[16,64,256]{2,1,0:T(8,128)(2,1)S(1)} async-done(((bf16[16,64,256]{2,1,0:T(8,128)(2,1)}), bf16[16,64,256]{2,1,0:T(8,128)(2,1)S(1)}, u32[]{:S(2)}, u32[]{:S(2)}) %all-to-all-start) | async-done | bytes 524320 | tf_op jit(solution)/shard_map/all_to_all | solution.py:345
  105.8 14.6 %all_to_all.15 = bf16[8,64,256]{2,1,0:T(8,128)(2,1)S(1)} all-to-all(bf16[8,64,256]{2,1,0:T(8,128)(2,1)S(1)} %broadcast_in_dim.4), channel_id=1, replica_groups=mesh['x'=4,'yh'=2,'z'=8,'yl'=2,'c'=2] {'z'}, dimensions={0} | all-to-all | bytes 524288 | tf_op jit(solution)/shard_map/all_to_all | solution.py:349
  120.5 14.8 %all_to_all.16 = bf16[16,64,256]{2,1,0:T(8,128)(2,1)S(1)} all-to-all(bf16[16,64,256]{2,1,0:T(8,128)(2,1)S(1)} %broadcast_in_dim.5), channel_id=1, replica_groups=mesh['x'=4,'yh'=2,'z'=8,'yl'=2,'c'=2] {'x','yh','yl'}, dimensions={0} | all-to-all | bytes 1048576 | tf_op jit(solution)/shard_map/all_to_all | solution.py:352
  135.3 3.6 %collective-permute-start.33 = (bf16[1024,256]{1,0:T(8,128)(2,1)S(1)}, bf16[1024,256]{1,0:T(8,128)(2,1)S(1)}, u32[]{:S(2)}, u32[]{:S(2)}) collective-permute-start(bf16[1024,256]{1,0:T(8,128)(2,1)S(1)} %bitcast.9), channel_id=1, source_target_pairs={{0,1},{1,0},{2,3},{3,2},{4,5},{5,4},{6,7},{7,6},{8,9},{9,8},{10,11... | collective-permute-start | bytes 1572872 | tf_op jit(solution)/shard_map/ppermute | solution.py:353
  (62 shorter events, 16.3 us)
Async XLA Ops:
  1.7 14.7 %collective-permute-start = (bf16[32,256]{1,0:T(8,128)(2,1)S(1)}, bf16[32,256]{1,0:T(8,128)(2,1)S(1)}, u32[]{:S(2)}, u32[]{:S(2)}) collective-permute-start(bf16[32,256]{1,0:T(8,128)(2,1)S(1)} %get-tuple-element.136), channel_id=1, source_target_pairs={{32,64},{96,128},{160,192},{224,0},{64,32},{128,96},{192,160},{0,2... | collective-permute-start | bytes 49160 | tf_op jit(solution)/shard_map/ppermute | solution.py:334
  7.7 8.7 %collective-permute-start.1 = (bf16[32,256]{1,0:T(8,128)(2,1)S(1)}, bf16[32,256]{1,0:T(8,128)(2,1)S(1)}, u32[]{:S(2)}, u32[]{:S(2)}) collective-permute-start(bf16[32,256]{1,0:T(8,128)(2,1)S(1)} %get-tuple-element.137), channel_id=1, source_target_pairs={{0,32},{32,0},{64,96},{96,64},{128,160},{160,128},{192,224},{224,1... | collective-permute-start | bytes 49160 | tf_op jit(solution)/shard_map/ppermute | solution.py:335
  7.8 8.7 %collective-permute-start.2 = (bf16[32,256]{1,0:T(8,128)(2,1)S(1)}, bf16[32,256]{1,0:T(8,128)(2,1)S(1)}, u32[]{:S(2)}, u32[]{:S(2)}) collective-permute-start(bf16[32,256]{1,0:T(8,128)(2,1)S(1)} %get-tuple-element.138), channel_id=1, source_target_pairs={{1,2},{3,4},{5,6},{7,8},{9,10},{11,12},{13,14},{15,16},{17,18},{19... | collective-permute-start | bytes 49160 | tf_op jit(solution)/shard_map/ppermute | solution.py:336
  9.0 7.5 %collective-permute-start.3 = (bf16[32,256]{1,0:T(8,128)(2,1)S(1)}, bf16[32,256]{1,0:T(8,128)(2,1)S(1)}, u32[]{:S(2)}, u32[]{:S(2)}) collective-permute-start(bf16[32,256]{1,0:T(8,128)(2,1)S(1)} %get-tuple-element.139), channel_id=1, source_target_pairs={{0,1},{1,0},{2,3},{3,2},{4,5},{5,4},{6,7},{7,6},{8,9},{9,8},{10,11... | collective-permute-start | bytes 49160 | tf_op jit(solution)/shard_map/ppermute | solution.py:337
  18.1 6.3 %collective-permute-start.4 = (bf16[32,256]{1,0:T(8,128)(2,1)S(1)}, bf16[32,256]{1,0:T(8,128)(2,1)S(1)}, u32[]{:S(2)}, u32[]{:S(2)}) collective-permute-start(bf16[32,256]{1,0:T(8,128)(2,1)S(1)} %get-tuple-element.151), channel_id=1, source_target_pairs={{32,64},{96,128},{160,192},{224,0},{64,32},{128,96},{192,160},{0,2... | collective-permute-start | bytes 49160 | tf_op jit(solution)/shard_map/ppermute | solution.py:334
  22.0 4.1 %collective-permute-start.5 = (bf16[32,256]{1,0:T(8,128)(2,1)S(1)}, bf16[32,256]{1,0:T(8,128)(2,1)S(1)}, u32[]{:S(2)}, u32[]{:S(2)}) collective-permute-start(bf16[32,256]{1,0:T(8,128)(2,1)S(1)} %get-tuple-element.152), channel_id=1, source_target_pairs={{0,32},{32,0},{64,96},{96,64},{128,160},{160,128},{192,224},{224,1... | collective-permute-start | bytes 49160 | tf_op jit(solution)/shard_map/ppermute | solution.py:335
  22.0 4.1 %collective-permute-start.6 = (bf16[32,256]{1,0:T(8,128)(2,1)S(1)}, bf16[32,256]{1,0:T(8,128)(2,1)S(1)}, u32[]{:S(2)}, u32[]{:S(2)}) collective-permute-start(bf16[32,256]{1,0:T(8,128)(2,1)S(1)} %get-tuple-element.153), channel_id=1, source_target_pairs={{1,2},{3,4},{5,6},{7,8},{9,10},{11,12},{13,14},{15,16},{17,18},{19... | collective-permute-start | bytes 49160 | tf_op jit(solution)/shard_map/ppermute | solution.py:336
  22.0 4.1 %collective-permute-start.7 = (bf16[32,256]{1,0:T(8,128)(2,1)S(1)}, bf16[32,256]{1,0:T(8,128)(2,1)S(1)}, u32[]{:S(2)}, u32[]{:S(2)}) collective-permute-start(bf16[32,256]{1,0:T(8,128)(2,1)S(1)} %get-tuple-element.154), channel_id=1, source_target_pairs={{0,1},{1,0},{2,3},{3,2},{4,5},{5,4},{6,7},{7,6},{8,9},{9,8},{10,11... | collective-permute-start | bytes 49160 | tf_op jit(solution)/shard_map/ppermute | solution.py:337
  27.7 7.2 %collective-permute-start.8 = (bf16[32,256]{1,0:T(8,128)(2,1)S(1)}, bf16[32,256]{1,0:T(8,128)(2,1)S(1)}, u32[]{:S(2)}, u32[]{:S(2)}) collective-permute-start(bf16[32,256]{1,0:T(8,128)(2,1)S(1)} %get-tuple-element.156), channel_id=1, source_target_pairs={{32,64},{96,128},{160,192},{224,0},{64,32},{128,96},{192,160},{0,2... | collective-permute-start | bytes 49160 | tf_op jit(solution)/shard_map/ppermute | solution.py:334
  30.1 4.9 %collective-permute-start.9 = (bf16[32,256]{1,0:T(8,128)(2,1)S(1)}, bf16[32,256]{1,0:T(8,128)(2,1)S(1)}, u32[]{:S(2)}, u32[]{:S(2)}) collective-permute-start(bf16[32,256]{1,0:T(8,128)(2,1)S(1)} %get-tuple-element.157), channel_id=1, source_target_pairs={{0,32},{32,0},{64,96},{96,64},{128,160},{160,128},{192,224},{224,1... | collective-permute-start | bytes 49160 | tf_op jit(solution)/shard_map/ppermute | solution.py:335
  31.4 4.4 %collective-permute-start.11 = (bf16[32,256]{1,0:T(8,128)(2,1)S(1)}, bf16[32,256]{1,0:T(8,128)(2,1)S(1)}, u32[]{:S(2)}, u32[]{:S(2)}) collective-permute-start(bf16[32,256]{1,0:T(8,128)(2,1)S(1)} %get-tuple-element.159), channel_id=1, source_target_pairs={{0,1},{1,0},{2,3},{3,2},{4,5},{5,4},{6,7},{7,6},{8,9},{9,8},{10,11... | collective-permute-start | bytes 49160 | tf_op jit(solution)/shard_map/ppermute | solution.py:337
  37.4 7.4 %collective-permute-start.12 = (bf16[32,256]{1,0:T(8,128)(2,1)S(1)}, bf16[32,256]{1,0:T(8,128)(2,1)S(1)}, u32[]{:S(2)}, u32[]{:S(2)}) collective-permute-start(bf16[32,256]{1,0:T(8,128)(2,1)S(1)} %get-tuple-element.161), channel_id=1, source_target_pairs={{32,64},{96,128},{160,192},{224,0},{64,32},{128,96},{192,160},{0,2... | collective-permute-start | bytes 49160 | tf_op jit(solution)/shard_map/ppermute | solution.py:334
  40.1 4.8 %collective-permute-start.13 = (bf16[32,256]{1,0:T(8,128)(2,1)S(1)}, bf16[32,256]{1,0:T(8,128)(2,1)S(1)}, u32[]{:S(2)}, u32[]{:S(2)}) collective-permute-start(bf16[32,256]{1,0:T(8,128)(2,1)S(1)} %get-tuple-element.162), channel_id=1, source_target_pairs={{0,32},{32,0},{64,96},{96,64},{128,160},{160,128},{192,224},{224,1... | collective-permute-start | bytes 49160 | tf_op jit(solution)/shard_map/ppermute | solution.py:335
  40.4 4.4 %collective-permute-start.14 = (bf16[32,256]{1,0:T(8,128)(2,1)S(1)}, bf16[32,256]{1,0:T(8,128)(2,1)S(1)}, u32[]{:S(2)}, u32[]{:S(2)}) collective-permute-start(bf16[32,256]{1,0:T(8,128)(2,1)S(1)} %get-tuple-element.163), channel_id=1, source_target_pairs={{1,2},{3,4},{5,6},{7,8},{9,10},{11,12},{13,14},{15,16},{17,18},{19... | collective-permute-start | bytes 49160 | tf_op jit(solution)/shard_map/ppermute | solution.py:336
  41.1 4.6 %collective-permute-start.15 = (bf16[32,256]{1,0:T(8,128)(2,1)S(1)}, bf16[32,256]{1,0:T(8,128)(2,1)S(1)}, u32[]{:S(2)}, u32[]{:S(2)}) collective-permute-start(bf16[32,256]{1,0:T(8,128)(2,1)S(1)} %get-tuple-element.164), channel_id=1, source_target_pairs={{0,1},{1,0},{2,3},{3,2},{4,5},{5,4},{6,7},{7,6},{8,9},{9,8},{10,11... | collective-permute-start | bytes 49160 | tf_op jit(solution)/shard_map/ppermute | solution.py:337
  48.5 8.7 %collective-permute-start.16 = (bf16[32,256]{1,0:T(8,128)(2,1)S(1)}, bf16[32,256]{1,0:T(8,128)(2,1)S(1)}, u32[]{:S(2)}, u32[]{:S(2)}) collective-permute-start(bf16[32,256]{1,0:T(8,128)(2,1)S(1)} %get-tuple-element.172), channel_id=1, source_target_pairs={{32,64},{96,128},{160,192},{224,0},{64,32},{128,96},{192,160},{0,2... | collective-permute-start | bytes 49160 | tf_op jit(solution)/shard_map/ppermute | solution.py:334
  53.4 4.7 %collective-permute-start.19 = (bf16[32,256]{1,0:T(8,128)(2,1)S(1)}, bf16[32,256]{1,0:T(8,128)(2,1)S(1)}, u32[]{:S(2)}, u32[]{:S(2)}) collective-permute-start(bf16[32,256]{1,0:T(8,128)(2,1)S(1)} %get-tuple-element.175), channel_id=1, source_target_pairs={{0,1},{1,0},{2,3},{3,2},{4,5},{5,4},{6,7},{7,6},{8,9},{9,8},{10,11... | collective-permute-start | bytes 49160 | tf_op jit(solution)/shard_map/ppermute | solution.py:337
  59.5 8.3 %collective-permute-start.20 = (bf16[32,256]{1,0:T(8,128)(2,1)S(1)}, bf16[32,256]{1,0:T(8,128)(2,1)S(1)}, u32[]{:S(2)}, u32[]{:S(2)}) collective-permute-start(bf16[32,256]{1,0:T(8,128)(2,1)S(1)} %get-tuple-element.181), channel_id=1, source_target_pairs={{32,64},{96,128},{160,192},{224,0},{64,32},{128,96},{192,160},{0,2... | collective-permute-start | bytes 49160 | tf_op jit(solution)/shard_map/ppermute | solution.py:334
  63.4 4.4 %collective-permute-start.21 = (bf16[32,256]{1,0:T(8,128)(2,1)S(1)}, bf16[32,256]{1,0:T(8,128)(2,1)S(1)}, u32[]{:S(2)}, u32[]{:S(2)}) collective-permute-start(bf16[32,256]{1,0:T(8,128)(2,1)S(1)} %get-tuple-element.182), channel_id=1, source_target_pairs={{0,32},{32,0},{64,96},{96,64},{128,160},{160,128},{192,224},{224,1... | collective-permute-start | bytes 49160 | tf_op jit(solution)/shard_map/ppermute | solution.py:335
  63.4 4.4 %collective-permute-start.22 = (bf16[32,256]{1,0:T(8,128)(2,1)S(1)}, bf16[32,256]{1,0:T(8,128)(2,1)S(1)}, u32[]{:S(2)}, u32[]{:S(2)}) collective-permute-start(bf16[32,256]{1,0:T(8,128)(2,1)S(1)} %get-tuple-element.183), channel_id=1, source_target_pairs={{1,2},{3,4},{5,6},{7,8},{9,10},{11,12},{13,14},{15,16},{17,18},{19... | collective-permute-start | bytes 49160 | tf_op jit(solution)/shard_map/ppermute | solution.py:336
  63.4 5.2 %collective-permute-start.23 = (bf16[32,256]{1,0:T(8,128)(2,1)S(1)}, bf16[32,256]{1,0:T(8,128)(2,1)S(1)}, u32[]{:S(2)}, u32[]{:S(2)}) collective-permute-start(bf16[32,256]{1,0:T(8,128)(2,1)S(1)} %get-tuple-element.184), channel_id=1, source_target_pairs={{0,1},{1,0},{2,3},{3,2},{4,5},{5,4},{6,7},{7,6},{8,9},{9,8},{10,11... | collective-permute-start | bytes 49160 | tf_op jit(solution)/shard_map/ppermute | solution.py:337
  70.0 10.9 %collective-permute-start.24 = (bf16[32,256]{1,0:T(8,128)(2,1)S(1)}, bf16[32,256]{1,0:T(8,128)(2,1)S(1)}, u32[]{:S(2)}, u32[]{:S(2)}) collective-permute-start(bf16[32,256]{1,0:T(8,128)(2,1)S(1)} %get-tuple-element.190), channel_id=1, source_target_pairs={{32,64},{96,128},{160,192},{224,0},{64,32},{128,96},{192,160},{0,2... | collective-permute-start | bytes 49160 | tf_op jit(solution)/shard_map/ppermute | solution.py:334
  73.3 7.7 %collective-permute-start.25 = (bf16[32,256]{1,0:T(8,128)(2,1)S(1)}, bf16[32,256]{1,0:T(8,128)(2,1)S(1)}, u32[]{:S(2)}, u32[]{:S(2)}) collective-permute-start(bf16[32,256]{1,0:T(8,128)(2,1)S(1)} %get-tuple-element.191), channel_id=1, source_target_pairs={{0,32},{32,0},{64,96},{96,64},{128,160},{160,128},{192,224},{224,1... | collective-permute-start | bytes 49160 | tf_op jit(solution)/shard_map/ppermute | solution.py:335
  73.8 7.2 %collective-permute-start.26 = (bf16[32,256]{1,0:T(8,128)(2,1)S(1)}, bf16[32,256]{1,0:T(8,128)(2,1)S(1)}, u32[]{:S(2)}, u32[]{:S(2)}) collective-permute-start(bf16[32,256]{1,0:T(8,128)(2,1)S(1)} %get-tuple-element.192), channel_id=1, source_target_pairs={{1,2},{3,4},{5,6},{7,8},{9,10},{11,12},{13,14},{15,16},{17,18},{19... | collective-permute-start | bytes 49160 | tf_op jit(solution)/shard_map/ppermute | solution.py:336
  73.8 7.2 %collective-permute-start.27 = (bf16[32,256]{1,0:T(8,128)(2,1)S(1)}, bf16[32,256]{1,0:T(8,128)(2,1)S(1)}, u32[]{:S(2)}, u32[]{:S(2)}) collective-permute-start(bf16[32,256]{1,0:T(8,128)(2,1)S(1)} %get-tuple-element.193), channel_id=1, source_target_pairs={{0,1},{1,0},{2,3},{3,2},{4,5},{5,4},{6,7},{7,6},{8,9},{9,8},{10,11... | collective-permute-start | bytes 49160 | tf_op jit(solution)/shard_map/ppermute | solution.py:337
  83.1 4.7 %collective-permute-start.28 = (bf16[1024,256]{1,0:T(8,128)(2,1)S(1)}, bf16[1024,256]{1,0:T(8,128)(2,1)S(1)}, u32[]{:S(2)}, u32[]{:S(2)}) collective-permute-start(bf16[1024,256]{1,0:T(8,128)(2,1)S(1)} %slice_bitcast_fusion), channel_id=1, source_target_pairs={{0,1},{1,0},{2,3},{3,2},{4,5},{5,4},{6,7},{7,6},{8,9},{9,8},{10,11... | collective-permute-start | bytes 1572872 | tf_op jit(solution)/shard_map/ppermute | solution.py:343
  88.7 16.5 %all-to-all-start = ((bf16[16,64,256]{2,1,0:T(8,128)(2,1)}), bf16[16,64,256]{2,1,0:T(8,128)(2,1)S(1)}, u32[]{:S(2)}, u32[]{:S(2)}) async-start(bf16[16,64,256]{2,1,0:T(8,128)(2,1)} %bitcast.2), calls=%async_computation | async-start | bytes 1048576 | tf_op jit(solution)/shard_map/all_to_all | solution.py:345
  94.9 10.9 %collective-permute-start.29 = (bf16[32,256]{1,0:T(8,128)(2,1)S(1)}, bf16[32,256]{1,0:T(8,128)(2,1)S(1)}, u32[]{:S(2)}, u32[]{:S(2)}) collective-permute-start(bf16[32,256]{1,0:T(8,128)(2,1)S(1)} %get-tuple-element.248), channel_id=1, source_target_pairs={{32,64},{96,128},{160,192},{224,0},{64,32},{128,96},{192,160},{0,2... | collective-permute-start | bytes 49160 | tf_op jit(solution)/shard_map/ppermute | solution.py:334
  99.9 5.9 %collective-permute-start.30 = (bf16[32,256]{1,0:T(8,128)(2,1)S(1)}, bf16[32,256]{1,0:T(8,128)(2,1)S(1)}, u32[]{:S(2)}, u32[]{:S(2)}) collective-permute-start(bf16[32,256]{1,0:T(8,128)(2,1)S(1)} %get-tuple-element.249), channel_id=1, source_target_pairs={{0,32},{32,0},{64,96},{96,64},{128,160},{160,128},{192,224},{224,1... | collective-permute-start | bytes 49160 | tf_op jit(solution)/shard_map/ppermute | solution.py:335
  99.9 5.9 %collective-permute-start.31 = (bf16[32,256]{1,0:T(8,128)(2,1)S(1)}, bf16[32,256]{1,0:T(8,128)(2,1)S(1)}, u32[]{:S(2)}, u32[]{:S(2)}) collective-permute-start(bf16[32,256]{1,0:T(8,128)(2,1)S(1)} %get-tuple-element.250), channel_id=1, source_target_pairs={{1,2},{3,4},{5,6},{7,8},{9,10},{11,12},{13,14},{15,16},{17,18},{19... | collective-permute-start | bytes 49160 | tf_op jit(solution)/shard_map/ppermute | solution.py:336
  101.5 4.3 %collective-permute-start.32 = (bf16[32,256]{1,0:T(8,128)(2,1)S(1)}, bf16[32,256]{1,0:T(8,128)(2,1)S(1)}, u32[]{:S(2)}, u32[]{:S(2)}) collective-permute-start(bf16[32,256]{1,0:T(8,128)(2,1)S(1)} %get-tuple-element.251), channel_id=1, source_target_pairs={{0,1},{1,0},{2,3},{3,2},{4,5},{5,4},{6,7},{7,6},{8,9},{9,8},{10,11... | collective-permute-start | bytes 49160 | tf_op jit(solution)/shard_map/ppermute | solution.py:337
  135.3 5.5 %collective-permute-start.33 = (bf16[1024,256]{1,0:T(8,128)(2,1)S(1)}, bf16[1024,256]{1,0:T(8,128)(2,1)S(1)}, u32[]{:S(2)}, u32[]{:S(2)}) collective-permute-start(bf16[1024,256]{1,0:T(8,128)(2,1)S(1)} %bitcast.9), channel_id=1, source_target_pairs={{0,1},{1,0},{2,3},{3,2},{4,5},{5,4},{6,7},{7,6},{8,9},{9,8},{10,11... | collective-permute-start | bytes 1572872 | tf_op jit(solution)/shard_map/ppermute | solution.py:353
  (3 other events, 11.8 us)

commit v3 on v2

v3 whole, which is shorter than its diff:
```python
import jax
import jax.numpy as jnp
from jax import lax
from jax.experimental import pallas as pl
from jax.experimental.pallas import tpu as pltpu
from jax.sharding import Mesh
from jax.sharding import PartitionSpec as P

STEPS = 4
EPS = 1e-05
L = 256
OWN = 128
HALO = 32
BF16 = jnp.bfloat16
F32 = jnp.float32
AXES = ("x", "yh", "z", "yl", "c")
REGION = ("x", "yh")
SLAB = ("z", "yl", "c")
PLANE = ("x", "yh", "yl")
CHUNK = 128
CHUNKS = 16
CHUNK_ROWS = 64


def mm(a, b):
    return jnp.dot(a, b, preferred_element_type=F32)


def mm_t(a, b):
    return lax.dot_general(a, b, (((0,), (0,)), ((), ())), preferred_element_type=F32)


def split(v):
    high = v.astype(BF16)
    low = (v - high.astype(F32)).astype(BF16)
    return high, low


def mm_split(v, w):
    high, low = split(v)
    return mm(high, w) + mm(low, w)


def sigmoid(v):
    return 0.5 * jnp.tanh(0.5 * v) + 0.5


def call(kernel, outs, *args, space=pltpu.VMEM, free=(), **kw):
    specs = [pl.BlockSpec(memory_space=pl.ANY if i in free else space) for i in range(len(args))]
    if space is pltpu.HBM:
        args = [a if i in free else pltpu.with_memory_space_constraint(a, space) for i, a in enumerate(args)]
    return pl.pallas_call(
        kernel,
        out_shape=[jax.ShapeDtypeStruct(s, d) for s, d in outs],
        in_specs=specs,
        out_specs=[pl.BlockSpec(memory_space=pltpu.VMEM)] * len(outs),
        compiler_params=pltpu.CompilerParams(vmem_limit_bytes=32 * 1024 * 1024),
        **kw,
    )(*args)


def slot_lists(lists):
    slab_odd = lax.axis_index("c")
    region_odd = lax.axis_index("yh")
    a, b, c, d = (lists[i : i + 1, :] for i in range(4))
    return (
        jnp.where(region_odd == 1, d, c),
        jnp.where(region_odd == 1, c, d),
        jnp.where(slab_odd == 1, b, a),
        jnp.where(slab_odd == 1, a, b),
    )


def first_kernel(nodes, lists, s0, s1, s2, s3, spread, h, rows, sems):
    copies = [pltpu.make_async_copy(nodes, h, sems.at[0]), pltpu.make_async_copy(lists, rows, sems.at[1])]
    for copy in copies:
        copy.start()
    for copy in copies:
        copy.wait()
    row = lax.broadcasted_iota(jnp.int32, (OWN, HALO), 0)
    for i, (idx, out) in enumerate(zip(slot_lists(rows[...]), (s0, s1, s2, s3))):
        hot = (row == idx).astype(F32).astype(BF16)
        spread[:, i * HALO : (i + 1) * HALO] = hot
        out[...] = mm_t(hot, h[...]).astype(BF16)


def prep_kernel(
    count_in, send_in, recv_in, gain_in, w1_in, feats_in, n1_in, w2_in, n2_in, cot_in, nodes_in, spread_in,
    tos_out, th_out, ss_out, ttst_out, st_out, st_sent_out, pre_out, fw_out, w1t_out, back_out, n2t_out, mix_out,
    gain_out, w1, feats, n1, w2, n2, cot, nodes,
    spread, count, send_idx, recv_idx, gain, sems,
):
    pairs = (
        (w1_in, w1), (feats_in, feats), (count_in, count), (spread_in, spread), (send_in, send_idx), (recv_in, recv_idx),
        (n1_in, n1), (w2_in, w2), (n2_in, n2), (nodes_in, nodes), (gain_in, gain), (cot_in, cot),
    )
    copies = [pltpu.make_async_copy(a, b, sems.at[i]) for i, (a, b) in enumerate(pairs)]
    for copy in copies:
        copy.start()
    for copy in copies:
        copy.wait()
    edges = feats.shape[0]
    lane = lax.broadcasted_iota(jnp.int32, (1, edges), 1)
    live = lane < count[0, 0]
    snd = send_idx[...].reshape(1, edges)
    off = snd - OWN
    slab_swap = jnp.where(lax.axis_index("c") == 1, 3 * HALO, 2 * HALO)
    region_swap = jnp.where(lax.axis_index("yh") == 1, 3 * HALO, 2 * HALO)
    flip = jnp.where(off < 2 * HALO, slab_swap, region_swap)
    snd = jnp.where(off >= 0, OWN + (off ^ flip), snd)
    snd = jnp.where(live, snd, -1)
    rcv = jnp.where(live, recv_idx[...].reshape(1, edges), -1)
    tt = (lax.broadcasted_iota(jnp.int32, (2 * OWN, edges), 0) == snd).astype(F32)
    st = (lax.broadcasted_iota(jnp.int32, (OWN, edges), 0) == rcv).astype(F32)
    spread_t = spread[...].T
    tt16 = tt.astype(BF16)
    st16 = st.astype(BF16)
    t16 = tt.T.astype(BF16)
    s16 = st.T.astype(BF16)
    ttst_out[: 2 * OWN] = tt16
    ttst_out[2 * OWN :] = st16
    st_out[...] = st16
    st_sent_out[...] = mm(spread_t, st16).astype(BF16)
    for i in range(2):
        tos_out[:, i * OWN : (i + 1) * OWN] = t16[:, :OWN]
        th_out[:, i * OWN : (i + 1) * OWN] = t16[:, OWN:]
        tos_out[:, (2 + i) * OWN : (3 + i) * OWN] = s16
        ss_out[:, i * OWN : (i + 1) * OWN] = s16
    fw_out[...] = mm(feats[...], w1[2 * L :])
    own_pre(nodes[...], tos_out, fw_out, w1, pre_out)
    w1t_out[...] = w1[...].T
    n2t_out[...] = n2[...].T
    mix_high, mix_low = split(mm(w2[...], n1[L:]))
    mix_out[:, :L] = mix_high
    mix_out[:, L:] = mix_low
    back_out[:, : 2 * L] = n1[...].T
    back_out[:, 2 * L : 3 * L] = mix_high.T
    back_out[:, 3 * L :] = mix_low.T
    gain_out[...] = gain[...].reshape(1, L)


def edge_hidden(halo, th, pre_part, edge_w1, keep):
    high, low = split(mm(jnp.concatenate(halo, axis=0), edge_w1[:L]))
    table = jnp.concatenate([high, low], axis=0)
    hidden = []
    for lo in range(0, pre_part.shape[0], CHUNK):
        pre = mm(th[lo : lo + CHUNK], table) + pre_part[lo : lo + CHUNK]
        hidden.append(keep(lo, pre))
    return jnp.concatenate(hidden, axis=0)


def edge_slopes(pre):
    sig = sigmoid(pre)
    silu = pre * sig
    return silu, sig + silu * (1.0 - sig)


def node_body(h, hidden_sum, node_w1, mix, node_w2):
    high, low = split(hidden_sum)
    pre_node = mm(h, node_w1[:L]) + mm(high, mix[:, :L]) + mm(high, mix[:, L:]) + mm(low, mix[:, :L])
    silu_n, node_slope = edge_slopes(pre_node)
    hidden_node = silu_n.astype(BF16)
    update = mm(hidden_node, node_w2[...])
    centre = update - jnp.mean(update, axis=-1, keepdims=True)
    inv_dev = lax.rsqrt(jnp.mean(centre * centre, axis=-1, keepdims=True) + EPS)
    return node_slope, hidden_node, centre * inv_dev, inv_dev


def own_pre(h, tos, fw, edge_w1, out):
    far_high, far_low = split(mm(h, edge_w1[:L]))
    near_high, near_low = split(mm(h, edge_w1[L : 2 * L]))
    table = jnp.concatenate([far_high, far_low, near_high, near_low], axis=0)
    for lo in range(0, fw.shape[0], CHUNK):
        out[lo : lo + CHUNK] = mm(tos[lo : lo + CHUNK], table) + fw[lo : lo + CHUNK]


def forward_kernel(
    p0, p1, p2, p3, q0, q1, q2, q3, pre_part, th, st_sent, edge_w1, node_w1, mix, node_w2, gain,
    s0, s1, s2, s3, pre_o, hidden_o,
):
    def keep(lo, pre):
        pre_o[lo : lo + CHUNK] = pre
        part = (pre * sigmoid(pre)).astype(BF16)
        hidden_o[lo : lo + CHUNK] = part
        return part

    hidden = edge_hidden([p0[...], p1[...], p2[...], p3[...]], th, pre_part, edge_w1, keep)
    h = jnp.concatenate([q0[...], q1[...], q2[...], q3[...]], axis=0)
    normed = node_body(h, mm(st_sent[...], hidden), node_w1, mix, node_w2)[2]
    sent = (h.astype(F32) + normed * gain[...]).astype(BF16)
    for i, out in enumerate((s0, s1, s2, s3)):
        out[...] = sent[i * HALO : (i + 1) * HALO]


def own_kernel(
    h_ref, pre, hidden, st, tos, fw, edge_w1, node_w1, mix, node_w2, gain,
    h_out, pre_part_o, edge_slope_o, hidden_sum_o, node_slope_o, hidden_node_o, normed_o, inv_dev_o,
):
    h = h_ref[...]
    hidden_sum = mm(st[...], hidden[...])
    node_slope, hidden_node, normed, inv_dev = node_body(h, hidden_sum, node_w1, mix, node_w2)
    nxt = (h.astype(F32) + normed * gain[...]).astype(BF16)
    h_out[...] = nxt
    own_pre(nxt, tos, fw, edge_w1, pre_part_o)
    edge_slope_o[...] = edge_slopes(pre[...])[1]
    hidden_sum_o[...] = hidden_sum
    node_slope_o[...] = node_slope
    hidden_node_o[...] = hidden_node
    normed_o[...] = normed
    inv_dev_o[...] = jnp.broadcast_to(inv_dev, inv_dev_o.shape)


def backward_body(
    up, parts, gain, ss, ttst, w1t, back, n2t, g0, g1, g2, g3, gpe_o, qr_o, gpn_o, gu_o, gain_o
):
    edge_slope, node_slope, normed, inv_dev = parts
    gain_o[...] = jnp.sum(up * normed, axis=0, keepdims=True)
    scaled = up * gain
    gu = inv_dev * (
        scaled
        - jnp.mean(scaled, axis=-1, keepdims=True)
        - normed * jnp.mean(scaled * normed, axis=-1, keepdims=True)
    )
    gu = gu.astype(BF16)
    gpn = (mm(gu, n2t[...]) * node_slope).astype(BF16)
    gu_o[...] = gu
    gpn_o[...] = gpn
    gh = mm(gpn, back[:, 2 * L : 3 * L]) + mm(gpn, back[:, 3 * L :])
    high, low = split(gh)
    pair = jnp.concatenate([high, low], axis=0)
    gpe = []
    for lo in range(0, edge_slope.shape[0], CHUNK):
        part = (mm(ss[lo : lo + CHUNK], pair) * edge_slope[lo : lo + CHUNK]).astype(BF16)
        gpe_o[lo : lo + CHUNK] = part
        gpe.append(part)
    qr = mm(ttst[...], jnp.concatenate(gpe, axis=0))
    q_high, q_low = split(qr[OWN : 2 * OWN])
    far = w1t[:, :L]
    ge = mm(q_high, far) + mm(q_low, far)
    for i, out in enumerate((g0, g1, g2, g3)):
        out[...] = ge[i * HALO : (i + 1) * HALO].astype(BF16)
    qr_o[...] = qr


def rest_kernel(up, qr, gpn, w1t, back, own_out):
    q_high, q_low = split(qr[:OWN])
    r_high, r_low = split(qr[2 * OWN :])
    far, near = w1t[:, :L], w1t[:, L : 2 * L]
    own_out[...] = (
        up[...] + mm(gpn[...], back[:, :L]) + mm(q_high, far) + mm(q_low, far) + mm(r_high, near) + mm(r_low, near)
    )


def landed(own, spread, p0, p1, p2, p3):
    parts = jnp.concatenate([p0[...], p1[...], p2[...], p3[...]], axis=0)
    return own[...] + mm(spread[...], parts)


def turn_kernel(
    h_ref, p0, p1, p2, p3, pre_part, th, st, edge_w1, node_w1, mix, node_w2, gain, cot, ss, ttst, w1t, back, n2t,
    g0, g1, g2, g3, gpe_o, qr_o, gpn_o, gu_o, gain_o, hidden_sum_o, hidden_node_o, edge_slope,
):
    def keep(lo, pre):
        silu, slope = edge_slopes(pre)
        edge_slope[lo : lo + CHUNK] = slope
        return silu.astype(BF16)

    hidden = edge_hidden([p0[...], p1[...], p2[...], p3[...]], th, pre_part, edge_w1, keep)
    hidden_sum = mm(st[...], hidden)
    node_slope, hidden_node, normed, inv_dev = node_body(h_ref[...], hidden_sum, node_w1, mix, node_w2)
    hidden_sum_o[...] = hidden_sum
    hidden_node_o[...] = hidden_node
    backward_body(
        cot[...], (edge_slope, node_slope, normed, inv_dev), gain[...], ss, ttst, w1t, back, n2t,
        g0, g1, g2, g3, gpe_o, qr_o, gpn_o, gu_o, gain_o,
    )


def backward_kernel(
    own, p0, p1, p2, p3, spread, edge_slope, node_slope, normed, inv_dev, gain, ss, ttst, w1t, back, n2t,
    g0, g1, g2, g3, gpe_o, qr_o, gpn_o, gu_o, gain_o, up_o,
):
    up = landed(own, spread, p0, p1, p2, p3)
    up_o[...] = up
    backward_body(
        up, (edge_slope, node_slope[...], normed[...], inv_dev[:, :1]), gain[...], ss, ttst, w1t, back, n2t,
        g0, g1, g2, g3, gpe_o, qr_o, gpn_o, gu_o, gain_o,
    )


def weight_args(refs):
    h_ref, p0, p1, p2, p3, feats, edge_w2, hidden_sum, hidden_node, back, gpe, qr, gpn, gu = refs
    gm = mm(gpn[...], back[:, L : 2 * L]).astype(BF16)
    h = h_ref[...]
    extended = jnp.concatenate([h, p0[...], p1[...], p2[...], p3[...]], axis=0)
    qr_high, qr_low = split(qr[...])
    h_high, h_low = split(hidden_sum[...])
    summed = (mm(h_high, edge_w2[...]) + mm(h_low, edge_w2[...])).astype(BF16)
    return (
        mm_t(extended, qr_high[: 2 * OWN]) + mm_t(extended, qr_low[: 2 * OWN]),
        mm_t(h, qr_high[2 * OWN :]) + mm_t(h, qr_low[2 * OWN :]),
        mm_t(feats[...], gpe[...]),
        mm_t(h_high, gm) + mm_t(h_low, gm),
        mm_t(h, gpn[...]),
        mm_t(summed, gpn[...]),
        mm_t(hidden_node[...], gu[...]),
    )


def weight_first_kernel(*refs):
    w1t, gain_in, acc, edge_acc, gain_acc = refs[14:]
    for i, term in enumerate(weight_args(refs[:14])):
        acc[i] = term
    edge_acc[...] = mm(refs[10][...], w1t[:, 2 * L :])
    gain_acc[...] = gain_in[...]


def weight_kernel(*refs):
    w1t, gain_in, acc_in, edge_in, gain_acc_in, acc, edge_acc, gain_acc = refs[14:]
    for i, term in enumerate(weight_args(refs[:14])):
        acc[i] = acc_in[i] + term
    edge_acc[...] = edge_in[...] + mm(refs[10][...], w1t[:, 2 * L :])
    gain_acc[...] = gain_acc_in[...] + gain_in[...]


def weight_last_kernel(*refs):
    gain_in, acc_in, gain_acc_in, out = refs[14:]
    core = lax.axis_index("c")
    terms = weight_args(refs[:14])
    for i, term in enumerate(terms):
        out[(i // 4) ^ core, (i % 4) * L : (i % 4 + 1) * L, :] = (acc_in[i] + term).astype(BF16)
    row = lax.broadcasted_iota(jnp.int32, (L, L), 0)
    gain = gain_acc_in[...] + gain_in[...]
    out[1 ^ core, 3 * L :, :] = jnp.where(row == 0, gain, 0.0).astype(BF16)


def edge_last_kernel(gpe, w1t, edge_in, out):
    out[...] = edge_in[...] + mm(gpe[...], w1t[:, 2 * L :])


def node_last_kernel(own, p0, p1, p2, p3, spread, out):
    out[...] = landed(own, spread, p0, p1, p2, p3)


def finish_kernel(factor, mine, other, edge_in, edge_out, node_in, node_out, gain):
    core = lax.axis_index("c")

    def half(index, lo, hi):
        a = mine[lo:hi].astype(F32)
        b = other[lo:hi].astype(F32)
        return jnp.where(core == index, a, b) * factor

    edge_in[...] = half(0, 0, 3 * L)
    edge_out[...] = half(0, 3 * L, 4 * L)
    node_in[...] = half(1, 0, 2 * L)
    node_out[...] = half(1, 2 * L, 3 * L)
    gain[...] = half(1, 3 * L, 3 * L + 8)[0]


def even_pairs(size):
    return [(i, i ^ 1) for i in range(size)]


def odd_pairs(size):
    up = [((i + 1) % size, (i + 2) % size) for i in range(0, size, 2)]
    return up + [(b, a) for a, b in up]


def exchange(parts):
    slabs = lax.axis_size(SLAB)
    regions = lax.axis_size(REGION)
    return [
        lax.ppermute(parts[0], REGION, odd_pairs(regions)),
        lax.ppermute(parts[1], REGION, even_pairs(regions)),
        lax.ppermute(parts[2], SLAB, odd_pairs(slabs)),
        lax.ppermute(parts[3], SLAB, even_pairs(slabs)),
    ]


def reduce_all(payload, back):
    keep = payload[0].astype(F32)
    got = lax.ppermute(payload[1], "c", [(0, 1), (1, 0)])
    part = (keep + got.astype(F32)).astype(BF16).reshape(CHUNKS, CHUNK_ROWS, L)
    part = lax.all_to_all(part, PLANE, 0, 0, tiled=True)
    part = jnp.sum(part.astype(F32), axis=0).astype(BF16)
    deep = lax.axis_size("z")
    part = lax.all_to_all(jnp.broadcast_to(part[None], (deep,) + part.shape), "z", 0, 0, tiled=True)
    part = jnp.sum(part.astype(F32), axis=0).astype(BF16)
    part, *back = lax.optimization_barrier((part, *back))
    part = jnp.broadcast_to(part[None], (CHUNKS,) + part.shape)
    mine = lax.all_to_all(part, PLANE, 0, 0, tiled=True).reshape(CHUNKS * CHUNK_ROWS, L)
    other = lax.ppermute(mine, "c", [(0, 1), (1, 0)])
    return mine, other, back


def local(
    nodes, feats, cotangent, edge_w1, edge_w2, node_w1, node_w2, ln_gain, senders, receivers, send_rows, edge_count
):
    edges = feats.shape[0]
    halo_outs = [((HALO, L), BF16)] * 4
    *sends, spread = call(
        first_kernel, halo_outs + [((OWN, 4 * HALO), BF16)], nodes, send_rows, space=pltpu.HBM,
        scratch_shapes=[pltpu.VMEM((OWN, L), BF16), pltpu.VMEM((4, HALO), jnp.int32), pltpu.SemaphoreType.DMA((2,))],
    )
    tos, th, ss, ttst, st, st_sent, pre_part, fw, w1t, back_w, n2t, mix, gain, edge_w1, feats, node_w1, edge_w2, node_w2, cotangent, nodes = call(
        prep_kernel,
        [
            ((edges, 4 * OWN), BF16), ((edges, 2 * OWN), BF16), ((edges, 2 * OWN), BF16), ((3 * OWN, edges), BF16),
            ((OWN, edges), BF16), ((OWN, edges), BF16), ((edges, L), F32),
            ((edges, L), F32), ((L, 3 * L), BF16), ((L, 4 * L), BF16), ((L, L), BF16), ((L, 2 * L), BF16),
            ((1, L), F32), ((3 * L, L), BF16), ((edges, L), BF16), ((2 * L, L), BF16), ((L, L), BF16), ((L, L), BF16),
            ((OWN, L), F32), ((OWN, L), BF16),
        ],
        edge_count, senders, receivers, ln_gain, edge_w1, feats, node_w1, edge_w2, node_w2, cotangent, nodes, spread,
        space=pltpu.HBM,
        free=(0, 11),
        scratch_shapes=[
            pltpu.VMEM((OWN, 4 * HALO), BF16), pltpu.SMEM((1, 1), jnp.int32),
            pltpu.VMEM((edges,), jnp.int32), pltpu.VMEM((edges,), jnp.int32),
            pltpu.VMEM((L,), F32), pltpu.SemaphoreType.DMA((12,)),
        ],
    )
    h = nodes
    saved = []
    for _ in range(STEPS - 1):
        halo = exchange(sends)
        *sends, pre, hidden = call(
            forward_kernel,
            halo_outs + [((edges, L), F32), ((edges, L), BF16)],
            *halo, *sends, pre_part, th, st_sent, edge_w1, node_w1, mix, node_w2, gain,
        )
        nxt, pre_part, *rest = call(
            own_kernel,
            [
                ((OWN, L), BF16), ((edges, L), F32), ((edges, L), F32), ((OWN, L), F32), ((OWN, L), F32), ((OWN, L), BF16),
                ((OWN, L), F32), ((OWN, 128), F32),
            ],
            h, pre, hidden, st, tos, fw, edge_w1, node_w1, mix, node_w2, gain,
        )
        saved.append((h, halo, rest))
        h = nxt
    halo = exchange(sends)
    back_outs = halo_outs + [
        ((edges, L), BF16), ((3 * OWN, L), F32), ((OWN, L), BF16), ((OWN, L), BF16), ((1, L), F32),
    ]
    g0, g1, g2, g3, *terms, gain_term, hidden_sum, hidden_node = call(
        turn_kernel,
        back_outs + [((OWN, L), F32), ((OWN, L), BF16)],
        h, *halo, pre_part, th, st, edge_w1, node_w1, mix, node_w2, gain, cotangent, ss, ttst, w1t, back_w, n2t,
        scratch_shapes=[pltpu.VMEM((edges, L), F32)],
    )
    back = exchange([g0, g1, g2, g3])
    own_out = [((OWN, L), F32)]
    (own,) = call(rest_kernel, own_out, cotangent, terms[1], terms[2], w1t, back_w)
    acc_outs = [((7, L, L), F32), ((edges, L), F32), ((1, L), F32)]
    totals = call(
        weight_first_kernel, acc_outs, h, *halo, feats, edge_w2, hidden_sum, hidden_node, back_w, *terms, w1t, gain_term
    )
    for layer in reversed(range(STEPS - 1)):
        h, halo, (edge_slope, hidden_sum, node_slope, hidden_node, normed, inv_dev) = saved[layer]
        g0, g1, g2, g3, *terms, gain_term, up = call(
            backward_kernel, back_outs + own_out,
            own, *back, spread, edge_slope, node_slope, normed, inv_dev, gain, ss, ttst, w1t, back_w, n2t,
        )
        back = exchange([g0, g1, g2, g3])
        (own,) = call(rest_kernel, own_out, up, terms[1], terms[2], w1t, back_w)
        shared = (h, *halo, feats, edge_w2, hidden_sum, hidden_node, back_w, *terms)
        if layer > 0:
            totals = call(weight_kernel, acc_outs, *shared, w1t, gain_term, *totals)
    (payload,) = call(
        weight_last_kernel, [((2, 4 * L, L), BF16)], *shared, gain_term, totals[0], totals[2]
    )
    mine, other, back = reduce_all(payload, back)
    (edge_grad,) = call(edge_last_kernel, [((edges, L), F32)], terms[0], w1t, totals[1])
    (node_grad,) = call(node_last_kernel, [((OWN, L), F32)], own, *back, spread)
    devices = lax.axis_size(REGION) * lax.axis_size(SLAB)
    factor = float(OWN * devices) ** (-0.5)

    def finish(*refs):
        finish_kernel(factor, *refs)

    edge_in, edge_out, node_in, node_out, gain_grad = call(
        finish, [((3 * L, L), F32), ((L, L), F32), ((2 * L, L), F32), ((L, L), F32), ((L,), F32)], mine, other
    )
    return node_grad, edge_grad, edge_in, edge_out, node_in, node_out, gain_grad


def solution(mesh):
    fine = Mesh(mesh.devices.reshape(4, 2, 8, 2, 2), AXES)
    split_rows = P(AXES, None)
    placed = (
        split_rows, split_rows, split_rows, P(), P(), P(), P(), P(), P(AXES), P(AXES), split_rows, P(REGION, SLAB),
    )
    return jax.shard_map(
        local,
        mesh=fine,
        in_specs=placed,
        out_specs=(split_rows, split_rows, P(), P(), P(), P(), P()),
        check_vma=False,
    )
```

time: 143 us -> 139 us (0.972)
  starting transfers between devices: 78.3 us -> 74.3 us
  Pallas kernels: 21 us -> 24.8 us
  waiting for transfers between devices: 10.8 us -> 7.27 us
    pallas_call x16 -> x23, Pallas kernels: 21 us -> 24.8 us  [call(): pl.pallas_call(kernel, out_shape=[jax.ShapeDtypeStruct(s, d) for s, d in...]
    ppermute x8, starting transfers between devices: 32 us -> 28.7 us  [exchange(): lax.ppermute(parts[0], REGION, odd_pairs(regions))]
    ppermute x8, waiting for transfers between devices: 3.07 us -> 0.75 us  [exchange(): lax.ppermute(parts[3], SLAB, even_pairs(slabs))]
    all_to_all x1, blocking collectives: 14.6 us -> 16.3 us  [reduce_all(): part = lax.all_to_all(part, PLANE, 0, 0, tiled=True)]
    all_to_all x1, blocking collectives: 14.8 us -> 13.1 us  [reduce_all(): lax.all_to_all(part, PLANE, 0, 0, tiled=True)]
  transfers between devices with their start and end apart: 35 -> 35, of which waited for: 9 -> 6; matrix products, arithmetic and copies ran while one was open for 0% -> 0% of each run, Pallas kernels for 4% -> 9%
where the time goes in v3:
time: 139 us
  starting transfers between devices  74.3 us (53%)
  blocking collectives  29.4 us (21%)
  Pallas kernels  24.8 us (18%)
  waiting for transfers between devices  7.27 us (5%)
  between operations  1.67 us (1%)
    ppermute x8, starting transfers between devices, exchange(): lax.ppermute(parts[0], REGION, odd_pairs(regions))  28.7 us
    ppermute x8, starting transfers between devices, exchange(): lax.ppermute(parts[3], SLAB, even_pairs(slabs))  27 us
    pallas_call x23, Pallas kernels, call(): pl.pallas_call(kernel, out_shape=[jax.ShapeDtypeStruct(s, d) for s, d in...  24.8 us
    all_to_all x1, blocking collectives, reduce_all(): part = lax.all_to_all(part, PLANE, 0, 0, tiled=True)  16.3 us
    all_to_all x1, blocking collectives, reduce_all(): lax.all_to_all(part, PLANE, 0, 0, tiled=True)  13.1 us
    all_to_all x1, starting transfers between devices, reduce_all(): lax.all_to_all(jnp.broadcast_to(part[None], (deep,) + part.shape), 'z', 0...  4.95 us
    ppermute x8, starting transfers between devices, exchange(): lax.ppermute(parts[2], SLAB, odd_pairs(slabs))  4.21 us
    ppermute x1, starting transfers between devices, reduce_all(): other = lax.ppermute(mine, 'c', [(0, 1), (1, 0)])  4.16 us
  transfers between devices with their start and end apart: 35, of which 6 were waited for; matrix products, arithmetic and copies ran while one was open for 0% of the time, Pallas kernels for 9%

profile of v3, /device:TPU:1, one launch (start us, length us, event | category | flops | bytes accessed | tf_op | source)
XLA Modules:
  0.0 138.5 jit_solution(9999715037707191360)
XLA Ops:
  1.7 6.0 %collective-permute-start = (bf16[32,256]{1,0:T(8,128)(2,1)S(1)}, bf16[32,256]{1,0:T(8,128)(2,1)S(1)}, u32[]{:S(2)}, u32[]{:S(2)}) collective-permute-start(bf16[32,256]{1,0:T(8,128)(2,1)S(1)} %get-tuple-element.137.q0), channel_id=1, source_target_pairs={{32,64},{96,128},{160,192},{224,0},{64,32},{128,96},{192,160},{0,2... | collective-permute-start | bytes 49160 | tf_op jit(solution)/shard_map/ppermute | solution.py:373
  9.0 4.8 %collective-permute-start.3 = (bf16[32,256]{1,0:T(8,128)(2,1)S(1)}, bf16[32,256]{1,0:T(8,128)(2,1)S(1)}, u32[]{:S(2)}, u32[]{:S(2)}) collective-permute-start(bf16[32,256]{1,0:T(8,128)(2,1)S(1)} %get-tuple-element.140.q3), channel_id=1, source_target_pairs={{0,1},{1,0},{2,3},{3,2},{4,5},{5,4},{6,7},{7,6},{8,9},{9,8},{10,11... | collective-permute-start | bytes 49160 | tf_op jit(solution)/shard_map/ppermute | solution.py:376
  14.5 2.3 %shard_map.172 = (bf16[640,512]{1,0:T(8,128)(2,1)S(1)}, bf16[640,256]{1,0:T(8,128)(2,1)S(1)}, bf16[640,256]{1,0:T(8,128)(2,1)S(1)}, bf16[384,640]{1,0:T(8,128)(2...) custom-call(s32[1,1]{1,0:T(1,128)S(6)} %copy.19.count_in, ...), custom_call_target="tpu_custom_call" | custom-call | tf_op jit(solution)/shard_map/pallas_call | solution.py:52
  18.1 3.9 %collective-permute-start.4 = (bf16[32,256]{1,0:T(8,128)(2,1)S(1)}, bf16[32,256]{1,0:T(8,128)(2,1)S(1)}, u32[]{:S(2)}, u32[]{:S(2)}) collective-permute-start(bf16[32,256]{1,0:T(8,128)(2,1)S(1)} %get-tuple-element.155.q0), channel_id=1, source_target_pairs={{32,64},{96,128},{160,192},{224,0},{64,32},{128,96},{192,160},{0,2... | collective-permute-start | bytes 49160 | tf_op jit(solution)/shard_map/ppermute | solution.py:373
  22.0 2.0 %collective-permute-start.7 = (bf16[32,256]{1,0:T(8,128)(2,1)S(1)}, bf16[32,256]{1,0:T(8,128)(2,1)S(1)}, u32[]{:S(2)}, u32[]{:S(2)}) collective-permute-start(bf16[32,256]{1,0:T(8,128)(2,1)S(1)} %get-tuple-element.158.q3), channel_id=1, source_target_pairs={{0,1},{1,0},{2,3},{3,2},{4,5},{5,4},{6,7},{7,6},{8,9},{9,8},{10,11... | collective-permute-start | bytes 49160 | tf_op jit(solution)/shard_map/ppermute | solution.py:376
  24.0 1.5 %shard_map.174 = (bf16[128,256]{1,0:T(8,128)(2,1)S(1)}, f32[640,256]{1,0:T(8,128)S(1)}, f32[640,256]{1,0:T(8,128)S(1)}, f32[128,256]{1,0:T(8,128)S(1)}, f32[128,...) custom-call(bf16[128,256]{1,0:T(8,128)(2,1)S(1)} %get-tuple-element.136.h_ref.re, ...), custom_call_target="tpu_custom_call" | custom-call | tf_op jit(solution)/shard_map/pallas_call | solution.py:52
  27.3 2.7 %collective-permute-start.8 = (bf16[32,256]{1,0:T(8,128)(2,1)S(1)}, bf16[32,256]{1,0:T(8,128)(2,1)S(1)}, u32[]{:S(2)}, u32[]{:S(2)}) collective-permute-start(bf16[32,256]{1,0:T(8,128)(2,1)S(1)} %get-tuple-element.163.q0), channel_id=1, source_target_pairs={{32,64},{96,128},{160,192},{224,0},{64,32},{128,96},{192,160},{0,2... | collective-permute-start | bytes 49160 | tf_op jit(solution)/shard_map/ppermute | solution.py:373
  31.0 3.1 %collective-permute-start.11 = (bf16[32,256]{1,0:T(8,128)(2,1)S(1)}, bf16[32,256]{1,0:T(8,128)(2,1)S(1)}, u32[]{:S(2)}, u32[]{:S(2)}) collective-permute-start(bf16[32,256]{1,0:T(8,128)(2,1)S(1)} %get-tuple-element.166.q3), channel_id=1, source_target_pairs={{0,1},{1,0},{2,3},{3,2},{4,5},{5,4},{6,7},{7,6},{8,9},{9,8},{10,11... | collective-permute-start | bytes 49160 | tf_op jit(solution)/shard_map/ppermute | solution.py:376
  34.1 1.5 %shard_map.176 = (bf16[128,256]{1,0:T(8,128)(2,1)S(1)}, f32[640,256]{1,0:T(8,128)S(1)}, f32[640,256]{1,0:T(8,128)S(1)}, f32[128,256]{1,0:T(8,128)S(1)}, f32[128,...) custom-call(bf16[128,256]{1,0:T(8,128)(2,1)S(1)} %get-tuple-element.154.h_ref.re, ...), custom_call_target="tpu_custom_call" | custom-call | tf_op jit(solution)/shard_map/pallas_call | solution.py:52
  36.9 2.6 %collective-permute-start.12 = (bf16[32,256]{1,0:T(8,128)(2,1)S(1)}, bf16[32,256]{1,0:T(8,128)(2,1)S(1)}, u32[]{:S(2)}, u32[]{:S(2)}) collective-permute-start(bf16[32,256]{1,0:T(8,128)(2,1)S(1)} %get-tuple-element.171), channel_id=1, source_target_pairs={{32,64},{96,128},{160,192},{224,0},{64,32},{128,96},{192,160},{0,2... | collective-permute-start | bytes 49160 | tf_op jit(solution)/shard_map/ppermute | solution.py:373
  40.3 3.3 %collective-permute-start.15 = (bf16[32,256]{1,0:T(8,128)(2,1)S(1)}, bf16[32,256]{1,0:T(8,128)(2,1)S(1)}, u32[]{:S(2)}, u32[]{:S(2)}) collective-permute-start(bf16[32,256]{1,0:T(8,128)(2,1)S(1)} %get-tuple-element.174), channel_id=1, source_target_pairs={{0,1},{1,0},{2,3},{3,2},{4,5},{5,4},{6,7},{7,6},{8,9},{9,8},{10,11... | collective-permute-start | bytes 49160 | tf_op jit(solution)/shard_map/ppermute | solution.py:376
  43.6 1.5 %shard_map.178 = (bf16[128,256]{1,0:T(8,128)(2,1)S(1)}, f32[640,256]{1,0:T(8,128)S(1)}, f32[640,256]{1,0:T(8,128)S(1)}, f32[128,256]{1,0:T(8,128)S(1)}, f32[128,...) custom-call(bf16[128,256]{1,0:T(8,128)(2,1)S(1)} %get-tuple-element.162.h_ref.re, ...), custom_call_target="tpu_custom_call" | custom-call | tf_op jit(solution)/shard_map/pallas_call | solution.py:52
  45.2 2.3 %shard_map.179 = (bf16[32,256]{1,0:T(8,128)(2,1)S(1)}, bf16[32,256]{1,0:T(8,128)(2,1)S(1)}, bf16[32,256]{1,0:T(8,128)(2,1)S(1)}, bf16[32,256]{1,0:T(8,128)(2,1)S...) custom-call(bf16[128,256]{1,0:T(8,128)(2,1)S(1)} %get-tuple-element., ...), custom_call_target="tpu_custom_call" | custom-call | tf_op jit(solution)/shard_map/pallas_call | solution.py:52
  47.4 4.9 %collective-permute-start.16 = (bf16[32,256]{1,0:T(8,128)(2,1)S(1)}, bf16[32,256]{1,0:T(8,128)(2,1)S(1)}, u32[]{:S(2)}, u32[]{:S(2)}) collective-permute-start(bf16[32,256]{1,0:T(8,128)(2,1)S(1)} %get-tuple-element.183), channel_id=1, source_target_pairs={{32,64},{96,128},{160,192},{224,0},{64,32},{128,96},{192,160},{0,2... | collective-permute-start | bytes 49160 | tf_op jit(solution)/shard_map/ppermute | solution.py:373
  52.3 3.4 %collective-permute-start.19 = (bf16[32,256]{1,0:T(8,128)(2,1)S(1)}, bf16[32,256]{1,0:T(8,128)(2,1)S(1)}, u32[]{:S(2)}, u32[]{:S(2)}) collective-permute-start(bf16[32,256]{1,0:T(8,128)(2,1)S(1)} %get-tuple-element.186), channel_id=1, source_target_pairs={{0,1},{1,0},{2,3},{3,2},{4,5},{5,4},{6,7},{7,6},{8,9},{9,8},{10,11... | collective-permute-start | bytes 49160 | tf_op jit(solution)/shard_map/ppermute | solution.py:376
  56.6 1.3 shard_map.181
  57.9 3.6 %collective-permute-start.20 = (bf16[32,256]{1,0:T(8,128)(2,1)S(1)}, bf16[32,256]{1,0:T(8,128)(2,1)S(1)}, u32[]{:S(2)}, u32[]{:S(2)}) collective-permute-start(bf16[32,256]{1,0:T(8,128)(2,1)S(1)} %get-tuple-element.194), channel_id=1, source_target_pairs={{32,64},{96,128},{160,192},{224,0},{64,32},{128,96},{192,160},{0,2... | collective-permute-start | bytes 49160 | tf_op jit(solution)/shard_map/ppermute | solution.py:373
  61.5 4.8 %collective-permute-start.23 = (bf16[32,256]{1,0:T(8,128)(2,1)S(1)}, bf16[32,256]{1,0:T(8,128)(2,1)S(1)}, u32[]{:S(2)}, u32[]{:S(2)}) collective-permute-start(bf16[32,256]{1,0:T(8,128)(2,1)S(1)} %get-tuple-element.197), channel_id=1, source_target_pairs={{0,1},{1,0},{2,3},{3,2},{4,5},{5,4},{6,7},{7,6},{8,9},{9,8},{10,11... | collective-permute-start | bytes 49160 | tf_op jit(solution)/shard_map/ppermute | solution.py:376
  67.2 1.3 shard_map.183
  68.5 3.2 %collective-permute-start.24 = (bf16[32,256]{1,0:T(8,128)(2,1)S(1)}, bf16[32,256]{1,0:T(8,128)(2,1)S(1)}, u32[]{:S(2)}, u32[]{:S(2)}) collective-permute-start(bf16[32,256]{1,0:T(8,128)(2,1)S(1)} %get-tuple-element.205), channel_id=1, source_target_pairs={{32,64},{96,128},{160,192},{224,0},{64,32},{128,96},{192,160},{0,2... | collective-permute-start | bytes 49160 | tf_op jit(solution)/shard_map/ppermute | solution.py:373
  72.0 5.0 %collective-permute-start.27 = (bf16[32,256]{1,0:T(8,128)(2,1)S(1)}, bf16[32,256]{1,0:T(8,128)(2,1)S(1)}, u32[]{:S(2)}, u32[]{:S(2)}) collective-permute-start(bf16[32,256]{1,0:T(8,128)(2,1)S(1)} %get-tuple-element.208), channel_id=1, source_target_pairs={{0,1},{1,0},{2,3},{3,2},{4,5},{5,4},{6,7},{7,6},{8,9},{9,8},{10,11... | collective-permute-start | bytes 49160 | tf_op jit(solution)/shard_map/ppermute | solution.py:376
  79.6 1.3 shard_map.185
  81.6 2.7 %collective-permute-start.28 = (bf16[1024,256]{1,0:T(8,128)(2,1)S(1)}, bf16[1024,256]{1,0:T(8,128)(2,1)S(1)}, u32[]{:S(2)}, u32[]{:S(2)}) collective-permute-start(bf16[1024,256]{1,0:T(8,128)(2,1)S(1)} %slice_bitcast_fusion), channel_id=1, source_target_pairs={{0,1},{1,0},{2,3},{3,2},{4,5},{5,4},{6,7},{7,6},{8,9},{9,8},{10,11... | collective-permute-start | bytes 1572872 | tf_op jit(solution)/shard_map/ppermute | solution.py:382
  84.4 1.5 %collective-permute-done.28 = bf16[1024,256]{1,0:T(8,128)(2,1)S(1)} collective-permute-done((bf16[1024,256]{1,0:T(8,128)(2,1)S(1)}, bf16[1024,256]{1,0:T(8,128)(2,1)S(1)}, u32[]{:S(2)}, u32[]{:S(2)}) %collective-permute-start.28) | collective-permute-done | bytes 524320 | tf_op jit(solution)/shard_map/ppermute | solution.py:382
  86.1 16.3 %all_to_all.15 = bf16[16,64,256]{2,1,0:T(8,128)(2,1)S(1)} all-to-all(bf16[16,64,256]{2,1,0:T(8,128)(2,1)S(1)} %bitcast.11), channel_id=1, replica_groups=mesh['x'=4,'yh'=2,'z'=8,'yl'=2,'c'=2] {'x','yh','yl'}, dimensions={0} | all-to-all | bytes 1048576 | tf_op jit(solution)/shard_map/all_to_all | solution.py:384
  103.1 5.0 %all-to-all-start.1 = ((bf16[8,64,256]{2,1,0:T(8,128)(2,1)}), bf16[8,64,256]{2,1,0:T(8,128)(2,1)S(1)}, u32[]{:S(2)}, u32[]{:S(2)}) async-start(bf16[8,64,256]{2,1,0:T(8,128)(2,1)} %broadcast_in_dim.4), calls=%async_computation.1 | async-start | bytes 524288 | tf_op jit(solution)/shard_map/all_to_all | solution.py:387
  108.1 1.7 %collective-permute-start.29 = (bf16[32,256]{1,0:T(8,128)(2,1)S(1)}, bf16[32,256]{1,0:T(8,128)(2,1)S(1)}, u32[]{:S(2)}, u32[]{:S(2)}) collective-permute-start(bf16[32,256]{1,0:T(8,128)(2,1)S(1)} %get-tuple-element.246), channel_id=1, source_target_pairs={{32,64},{96,128},{160,192},{224,0},{64,32},{128,96},{192,160},{0,2... | collective-permute-start | bytes 49160 | tf_op jit(solution)/shard_map/ppermute | solution.py:373
  110.5 2.6 %collective-permute-start.31 = (bf16[32,256]{1,0:T(8,128)(2,1)S(1)}, bf16[32,256]{1,0:T(8,128)(2,1)S(1)}, u32[]{:S(2)}, u32[]{:S(2)}) collective-permute-start(bf16[32,256]{1,0:T(8,128)(2,1)S(1)} %get-tuple-element.248), channel_id=1, source_target_pairs={{1,2},{3,4},{5,6},{7,8},{9,10},{11,12},{13,14},{15,16},{17,18},{19... | collective-permute-start | bytes 49160 | tf_op jit(solution)/shard_map/ppermute | solution.py:375
  113.6 3.9 %all-to-all-done.1 = bf16[8,64,256]{2,1,0:T(8,128)(2,1)S(1)} async-done(((bf16[8,64,256]{2,1,0:T(8,128)(2,1)}), bf16[8,64,256]{2,1,0:T(8,128)(2,1)S(1)}, u32[]{:S(2)}, u32[]{:S(2)}) %all-to-all-start.1) | async-done | bytes 262176 | tf_op jit(solution)/shard_map/all_to_all | solution.py:387
  117.7 13.1 %all_to_all.16 = bf16[16,64,256]{2,1,0:T(8,128)(2,1)S(1)} all-to-all(bf16[16,64,256]{2,1,0:T(8,128)(2,1)S(1)} %broadcast_in_dim.5), channel_id=1, replica_groups=mesh['x'=4,'yh'=2,'z'=8,'yl'=2,'c'=2] {'x','yh','yl'}, dimensions={0} | all-to-all | bytes 1048576 | tf_op jit(solution)/shard_map/all_to_all | solution.py:391
  130.8 4.2 %collective-permute-start.33 = (bf16[1024,256]{1,0:T(8,128)(2,1)S(1)}, bf16[1024,256]{1,0:T(8,128)(2,1)S(1)}, u32[]{:S(2)}, u32[]{:S(2)}) collective-permute-start(bf16[1024,256]{1,0:T(8,128)(2,1)S(1)} %bitcast.9), channel_id=1, source_target_pairs={{0,1},{1,0},{2,3},{3,2},{4,5},{5,4},{6,7},{7,6},{8,9},{9,8},{10,11... | collective-permute-start | bytes 1572872 | tf_op jit(solution)/shard_map/ppermute | solution.py:392
  137.1 1.4 %shard_map.193 = (f32[768,256]{1,0:T(8,128)}, f32[256,256]{1,0:T(8,128)}, f32[512,256]{1,0:T(8,128)}, f32[256,256]{1,0:T(8,128)}, f32[256]{0:T(256)}) custom-call(bf16[1024,256]{1,0:T(8,128)(2,1)S(1)} %bitcast.10, bf16[1024,256]{1,0:T(8,128)(2,1)S(1)} %collective-permute-done.33.refs_1_), custom_call_target="tpu_custom_call" | custom-call | tf_op jit(solution)/shard_map/pallas_call | solution.py:52
  (69 shorter events, 18.0 us)
Async XLA Ops:
  1.7 15.1 %collective-permute-start = (bf16[32,256]{1,0:T(8,128)(2,1)S(1)}, bf16[32,256]{1,0:T(8,128)(2,1)S(1)}, u32[]{:S(2)}, u32[]{:S(2)}) collective-permute-start(bf16[32,256]{1,0:T(8,128)(2,1)S(1)} %get-tuple-element.137.q0), channel_id=1, source_target_pairs={{32,64},{96,128},{160,192},{224,0},{64,32},{128,96},{192,160},{0,2... | collective-permute-start | bytes 49160 | tf_op jit(solution)/shard_map/ppermute | solution.py:373
  7.7 9.1 %collective-permute-start.1 = (bf16[32,256]{1,0:T(8,128)(2,1)S(1)}, bf16[32,256]{1,0:T(8,128)(2,1)S(1)}, u32[]{:S(2)}, u32[]{:S(2)}) collective-permute-start(bf16[32,256]{1,0:T(8,128)(2,1)S(1)} %get-tuple-element.138.q1), channel_id=1, source_target_pairs={{0,32},{32,0},{64,96},{96,64},{128,160},{160,128},{192,224},{224,1... | collective-permute-start | bytes 49160 | tf_op jit(solution)/shard_map/ppermute | solution.py:374
  7.8 9.1 %collective-permute-start.2 = (bf16[32,256]{1,0:T(8,128)(2,1)S(1)}, bf16[32,256]{1,0:T(8,128)(2,1)S(1)}, u32[]{:S(2)}, u32[]{:S(2)}) collective-permute-start(bf16[32,256]{1,0:T(8,128)(2,1)S(1)} %get-tuple-element.139.q2), channel_id=1, source_target_pairs={{1,2},{3,4},{5,6},{7,8},{9,10},{11,12},{13,14},{15,16},{17,18},{19... | collective-permute-start | bytes 49160 | tf_op jit(solution)/shard_map/ppermute | solution.py:375
  9.0 7.9 %collective-permute-start.3 = (bf16[32,256]{1,0:T(8,128)(2,1)S(1)}, bf16[32,256]{1,0:T(8,128)(2,1)S(1)}, u32[]{:S(2)}, u32[]{:S(2)}) collective-permute-start(bf16[32,256]{1,0:T(8,128)(2,1)S(1)} %get-tuple-element.140.q3), channel_id=1, source_target_pairs={{0,1},{1,0},{2,3},{3,2},{4,5},{5,4},{6,7},{7,6},{8,9},{9,8},{10,11... | collective-permute-start | bytes 49160 | tf_op jit(solution)/shard_map/ppermute | solution.py:376
  18.1 7.4 %collective-permute-start.4 = (bf16[32,256]{1,0:T(8,128)(2,1)S(1)}, bf16[32,256]{1,0:T(8,128)(2,1)S(1)}, u32[]{:S(2)}, u32[]{:S(2)}) collective-permute-start(bf16[32,256]{1,0:T(8,128)(2,1)S(1)} %get-tuple-element.155.q0), channel_id=1, source_target_pairs={{32,64},{96,128},{160,192},{224,0},{64,32},{128,96},{192,160},{0,2... | collective-permute-start | bytes 49160 | tf_op jit(solution)/shard_map/ppermute | solution.py:373
  22.0 4.1 %collective-permute-start.6 = (bf16[32,256]{1,0:T(8,128)(2,1)S(1)}, bf16[32,256]{1,0:T(8,128)(2,1)S(1)}, u32[]{:S(2)}, u32[]{:S(2)}) collective-permute-start(bf16[32,256]{1,0:T(8,128)(2,1)S(1)} %get-tuple-element.157.q2), channel_id=1, source_target_pairs={{1,2},{3,4},{5,6},{7,8},{9,10},{11,12},{13,14},{15,16},{17,18},{19... | collective-permute-start | bytes 49160 | tf_op jit(solution)/shard_map/ppermute | solution.py:375
  22.0 4.1 %collective-permute-start.7 = (bf16[32,256]{1,0:T(8,128)(2,1)S(1)}, bf16[32,256]{1,0:T(8,128)(2,1)S(1)}, u32[]{:S(2)}, u32[]{:S(2)}) collective-permute-start(bf16[32,256]{1,0:T(8,128)(2,1)S(1)} %get-tuple-element.158.q3), channel_id=1, source_target_pairs={{0,1},{1,0},{2,3},{3,2},{4,5},{5,4},{6,7},{7,6},{8,9},{9,8},{10,11... | collective-permute-start | bytes 49160 | tf_op jit(solution)/shard_map/ppermute | solution.py:376
  27.3 8.3 %collective-permute-start.8 = (bf16[32,256]{1,0:T(8,128)(2,1)S(1)}, bf16[32,256]{1,0:T(8,128)(2,1)S(1)}, u32[]{:S(2)}, u32[]{:S(2)}) collective-permute-start(bf16[32,256]{1,0:T(8,128)(2,1)S(1)} %get-tuple-element.163.q0), channel_id=1, source_target_pairs={{32,64},{96,128},{160,192},{224,0},{64,32},{128,96},{192,160},{0,2... | collective-permute-start | bytes 49160 | tf_op jit(solution)/shard_map/ppermute | solution.py:373
  30.0 5.7 %collective-permute-start.9 = (bf16[32,256]{1,0:T(8,128)(2,1)S(1)}, bf16[32,256]{1,0:T(8,128)(2,1)S(1)}, u32[]{:S(2)}, u32[]{:S(2)}) collective-permute-start(bf16[32,256]{1,0:T(8,128)(2,1)S(1)} %get-tuple-element.164.q1), channel_id=1, source_target_pairs={{0,32},{32,0},{64,96},{96,64},{128,160},{160,128},{192,224},{224,1... | collective-permute-start | bytes 49160 | tf_op jit(solution)/shard_map/ppermute | solution.py:374
  31.0 4.7 %collective-permute-start.10 = (bf16[32,256]{1,0:T(8,128)(2,1)S(1)}, bf16[32,256]{1,0:T(8,128)(2,1)S(1)}, u32[]{:S(2)}, u32[]{:S(2)}) collective-permute-start(bf16[32,256]{1,0:T(8,128)(2,1)S(1)} %get-tuple-element.165.q2), channel_id=1, source_target_pairs={{1,2},{3,4},{5,6},{7,8},{9,10},{11,12},{13,14},{15,16},{17,18},{19... | collective-permute-start | bytes 49160 | tf_op jit(solution)/shard_map/ppermute | solution.py:375
  31.0 4.7 %collective-permute-start.11 = (bf16[32,256]{1,0:T(8,128)(2,1)S(1)}, bf16[32,256]{1,0:T(8,128)(2,1)S(1)}, u32[]{:S(2)}, u32[]{:S(2)}) collective-permute-start(bf16[32,256]{1,0:T(8,128)(2,1)S(1)} %get-tuple-element.166.q3), channel_id=1, source_target_pairs={{0,1},{1,0},{2,3},{3,2},{4,5},{5,4},{6,7},{7,6},{8,9},{9,8},{10,11... | collective-permute-start | bytes 49160 | tf_op jit(solution)/shard_map/ppermute | solution.py:376
  36.9 8.2 %collective-permute-start.12 = (bf16[32,256]{1,0:T(8,128)(2,1)S(1)}, bf16[32,256]{1,0:T(8,128)(2,1)S(1)}, u32[]{:S(2)}, u32[]{:S(2)}) collective-permute-start(bf16[32,256]{1,0:T(8,128)(2,1)S(1)} %get-tuple-element.171), channel_id=1, source_target_pairs={{32,64},{96,128},{160,192},{224,0},{64,32},{128,96},{192,160},{0,2... | collective-permute-start | bytes 49160 | tf_op jit(solution)/shard_map/ppermute | solution.py:373
  39.5 5.6 %collective-permute-start.13 = (bf16[32,256]{1,0:T(8,128)(2,1)S(1)}, bf16[32,256]{1,0:T(8,128)(2,1)S(1)}, u32[]{:S(2)}, u32[]{:S(2)}) collective-permute-start(bf16[32,256]{1,0:T(8,128)(2,1)S(1)} %get-tuple-element.172), channel_id=1, source_target_pairs={{0,32},{32,0},{64,96},{96,64},{128,160},{160,128},{192,224},{224,1... | collective-permute-start | bytes 49160 | tf_op jit(solution)/shard_map/ppermute | solution.py:374
  39.9 5.3 %collective-permute-start.14 = (bf16[32,256]{1,0:T(8,128)(2,1)S(1)}, bf16[32,256]{1,0:T(8,128)(2,1)S(1)}, u32[]{:S(2)}, u32[]{:S(2)}) collective-permute-start(bf16[32,256]{1,0:T(8,128)(2,1)S(1)} %get-tuple-element.173), channel_id=1, source_target_pairs={{1,2},{3,4},{5,6},{7,8},{9,10},{11,12},{13,14},{15,16},{17,18},{19... | collective-permute-start | bytes 49160 | tf_op jit(solution)/shard_map/ppermute | solution.py:375
  40.3 4.9 %collective-permute-start.15 = (bf16[32,256]{1,0:T(8,128)(2,1)S(1)}, bf16[32,256]{1,0:T(8,128)(2,1)S(1)}, u32[]{:S(2)}, u32[]{:S(2)}) collective-permute-start(bf16[32,256]{1,0:T(8,128)(2,1)S(1)} %get-tuple-element.174), channel_id=1, source_target_pairs={{0,1},{1,0},{2,3},{3,2},{4,5},{5,4},{6,7},{7,6},{8,9},{9,8},{10,11... | collective-permute-start | bytes 49160 | tf_op jit(solution)/shard_map/ppermute | solution.py:376
  47.4 8.6 %collective-permute-start.16 = (bf16[32,256]{1,0:T(8,128)(2,1)S(1)}, bf16[32,256]{1,0:T(8,128)(2,1)S(1)}, u32[]{:S(2)}, u32[]{:S(2)}) collective-permute-start(bf16[32,256]{1,0:T(8,128)(2,1)S(1)} %get-tuple-element.183), channel_id=1, source_target_pairs={{32,64},{96,128},{160,192},{224,0},{64,32},{128,96},{192,160},{0,2... | collective-permute-start | bytes 49160 | tf_op jit(solution)/shard_map/ppermute | solution.py:373
  52.3 4.3 %collective-permute-start.19 = (bf16[32,256]{1,0:T(8,128)(2,1)S(1)}, bf16[32,256]{1,0:T(8,128)(2,1)S(1)}, u32[]{:S(2)}, u32[]{:S(2)}) collective-permute-start(bf16[32,256]{1,0:T(8,128)(2,1)S(1)} %get-tuple-element.186), channel_id=1, source_target_pairs={{0,1},{1,0},{2,3},{3,2},{4,5},{5,4},{6,7},{7,6},{8,9},{9,8},{10,11... | collective-permute-start | bytes 49160 | tf_op jit(solution)/shard_map/ppermute | solution.py:376
  57.9 8.7 %collective-permute-start.20 = (bf16[32,256]{1,0:T(8,128)(2,1)S(1)}, bf16[32,256]{1,0:T(8,128)(2,1)S(1)}, u32[]{:S(2)}, u32[]{:S(2)}) collective-permute-start(bf16[32,256]{1,0:T(8,128)(2,1)S(1)} %get-tuple-element.194), channel_id=1, source_target_pairs={{32,64},{96,128},{160,192},{224,0},{64,32},{128,96},{192,160},{0,2... | collective-permute-start | bytes 49160 | tf_op jit(solution)/shard_map/ppermute | solution.py:373
  61.5 5.1 %collective-permute-start.21 = (bf16[32,256]{1,0:T(8,128)(2,1)S(1)}, bf16[32,256]{1,0:T(8,128)(2,1)S(1)}, u32[]{:S(2)}, u32[]{:S(2)}) collective-permute-start(bf16[32,256]{1,0:T(8,128)(2,1)S(1)} %get-tuple-element.195), channel_id=1, source_target_pairs={{0,32},{32,0},{64,96},{96,64},{128,160},{160,128},{192,224},{224,1... | collective-permute-start | bytes 49160 | tf_op jit(solution)/shard_map/ppermute | solution.py:374
  61.5 5.1 %collective-permute-start.22 = (bf16[32,256]{1,0:T(8,128)(2,1)S(1)}, bf16[32,256]{1,0:T(8,128)(2,1)S(1)}, u32[]{:S(2)}, u32[]{:S(2)}) collective-permute-start(bf16[32,256]{1,0:T(8,128)(2,1)S(1)} %get-tuple-element.196), channel_id=1, source_target_pairs={{1,2},{3,4},{5,6},{7,8},{9,10},{11,12},{13,14},{15,16},{17,18},{19... | collective-permute-start | bytes 49160 | tf_op jit(solution)/shard_map/ppermute | solution.py:375
  61.5 5.7 %collective-permute-start.23 = (bf16[32,256]{1,0:T(8,128)(2,1)S(1)}, bf16[32,256]{1,0:T(8,128)(2,1)S(1)}, u32[]{:S(2)}, u32[]{:S(2)}) collective-permute-start(bf16[32,256]{1,0:T(8,128)(2,1)S(1)} %get-tuple-element.197), channel_id=1, source_target_pairs={{0,1},{1,0},{2,3},{3,2},{4,5},{5,4},{6,7},{7,6},{8,9},{9,8},{10,11... | collective-permute-start | bytes 49160 | tf_op jit(solution)/shard_map/ppermute | solution.py:376
  68.5 11.1 %collective-permute-start.24 = (bf16[32,256]{1,0:T(8,128)(2,1)S(1)}, bf16[32,256]{1,0:T(8,128)(2,1)S(1)}, u32[]{:S(2)}, u32[]{:S(2)}) collective-permute-start(bf16[32,256]{1,0:T(8,128)(2,1)S(1)} %get-tuple-element.205), channel_id=1, source_target_pairs={{32,64},{96,128},{160,192},{224,0},{64,32},{128,96},{192,160},{0,2... | collective-permute-start | bytes 49160 | tf_op jit(solution)/shard_map/ppermute | solution.py:373
  71.6 8.0 %collective-permute-start.25 = (bf16[32,256]{1,0:T(8,128)(2,1)S(1)}, bf16[32,256]{1,0:T(8,128)(2,1)S(1)}, u32[]{:S(2)}, u32[]{:S(2)}) collective-permute-start(bf16[32,256]{1,0:T(8,128)(2,1)S(1)} %get-tuple-element.206), channel_id=1, source_target_pairs={{0,32},{32,0},{64,96},{96,64},{128,160},{160,128},{192,224},{224,1... | collective-permute-start | bytes 49160 | tf_op jit(solution)/shard_map/ppermute | solution.py:374
  72.0 7.6 %collective-permute-start.26 = (bf16[32,256]{1,0:T(8,128)(2,1)S(1)}, bf16[32,256]{1,0:T(8,128)(2,1)S(1)}, u32[]{:S(2)}, u32[]{:S(2)}) collective-permute-start(bf16[32,256]{1,0:T(8,128)(2,1)S(1)} %get-tuple-element.207), channel_id=1, source_target_pairs={{1,2},{3,4},{5,6},{7,8},{9,10},{11,12},{13,14},{15,16},{17,18},{19... | collective-permute-start | bytes 49160 | tf_op jit(solution)/shard_map/ppermute | solution.py:375
  72.0 7.6 %collective-permute-start.27 = (bf16[32,256]{1,0:T(8,128)(2,1)S(1)}, bf16[32,256]{1,0:T(8,128)(2,1)S(1)}, u32[]{:S(2)}, u32[]{:S(2)}) collective-permute-start(bf16[32,256]{1,0:T(8,128)(2,1)S(1)} %get-tuple-element.208), channel_id=1, source_target_pairs={{0,1},{1,0},{2,3},{3,2},{4,5},{5,4},{6,7},{7,6},{8,9},{9,8},{10,11... | collective-permute-start | bytes 49160 | tf_op jit(solution)/shard_map/ppermute | solution.py:376
  81.6 4.3 %collective-permute-start.28 = (bf16[1024,256]{1,0:T(8,128)(2,1)S(1)}, bf16[1024,256]{1,0:T(8,128)(2,1)S(1)}, u32[]{:S(2)}, u32[]{:S(2)}) collective-permute-start(bf16[1024,256]{1,0:T(8,128)(2,1)S(1)} %slice_bitcast_fusion), channel_id=1, source_target_pairs={{0,1},{1,0},{2,3},{3,2},{4,5},{5,4},{6,7},{7,6},{8,9},{9,8},{10,11... | collective-permute-start | bytes 1572872 | tf_op jit(solution)/shard_map/ppermute | solution.py:382
  103.1 14.4 %all-to-all-start.1 = ((bf16[8,64,256]{2,1,0:T(8,128)(2,1)}), bf16[8,64,256]{2,1,0:T(8,128)(2,1)S(1)}, u32[]{:S(2)}, u32[]{:S(2)}) async-start(bf16[8,64,256]{2,1,0:T(8,128)(2,1)} %broadcast_in_dim.4), calls=%async_computation.1 | async-start | bytes 524288 | tf_op jit(solution)/shard_map/all_to_all | solution.py:387
  108.1 9.5 %collective-permute-start.29 = (bf16[32,256]{1,0:T(8,128)(2,1)S(1)}, bf16[32,256]{1,0:T(8,128)(2,1)S(1)}, u32[]{:S(2)}, u32[]{:S(2)}) collective-permute-start(bf16[32,256]{1,0:T(8,128)(2,1)S(1)} %get-tuple-element.246), channel_id=1, source_target_pairs={{32,64},{96,128},{160,192},{224,0},{64,32},{128,96},{192,160},{0,2... | collective-permute-start | bytes 49160 | tf_op jit(solution)/shard_map/ppermute | solution.py:373
  109.8 7.8 %collective-permute-start.30 = (bf16[32,256]{1,0:T(8,128)(2,1)S(1)}, bf16[32,256]{1,0:T(8,128)(2,1)S(1)}, u32[]{:S(2)}, u32[]{:S(2)}) collective-permute-start(bf16[32,256]{1,0:T(8,128)(2,1)S(1)} %get-tuple-element.247), channel_id=1, source_target_pairs={{0,32},{32,0},{64,96},{96,64},{128,160},{160,128},{192,224},{224,1... | collective-permute-start | bytes 49160 | tf_op jit(solution)/shard_map/ppermute | solution.py:374
  110.5 7.1 %collective-permute-start.31 = (bf16[32,256]{1,0:T(8,128)(2,1)S(1)}, bf16[32,256]{1,0:T(8,128)(2,1)S(1)}, u32[]{:S(2)}, u32[]{:S(2)}) collective-permute-start(bf16[32,256]{1,0:T(8,128)(2,1)S(1)} %get-tuple-element.248), channel_id=1, source_target_pairs={{1,2},{3,4},{5,6},{7,8},{9,10},{11,12},{13,14},{15,16},{17,18},{19... | collective-permute-start | bytes 49160 | tf_op jit(solution)/shard_map/ppermute | solution.py:375
  113.1 4.5 %collective-permute-start.32 = (bf16[32,256]{1,0:T(8,128)(2,1)S(1)}, bf16[32,256]{1,0:T(8,128)(2,1)S(1)}, u32[]{:S(2)}, u32[]{:S(2)}) collective-permute-start(bf16[32,256]{1,0:T(8,128)(2,1)S(1)} %get-tuple-element.249), channel_id=1, source_target_pairs={{0,1},{1,0},{2,3},{3,2},{4,5},{5,4},{6,7},{7,6},{8,9},{9,8},{10,11... | collective-permute-start | bytes 49160 | tf_op jit(solution)/shard_map/ppermute | solution.py:376
  130.8 6.3 %collective-permute-start.33 = (bf16[1024,256]{1,0:T(8,128)(2,1)S(1)}, bf16[1024,256]{1,0:T(8,128)(2,1)S(1)}, u32[]{:S(2)}, u32[]{:S(2)}) collective-permute-start(bf16[1024,256]{1,0:T(8,128)(2,1)S(1)} %bitcast.9), channel_id=1, source_target_pairs={{0,1},{1,0},{2,3},{3,2},{4,5},{5,4},{6,7},{7,6},{8,9},{9,8},{10,11... | collective-permute-start | bytes 1572872 | tf_op jit(solution)/shard_map/ppermute | solution.py:392
  (3 other events, 12.3 us)

commit v4 on v3

--- a/solution.py
+++ b/solution.py
@@ -1,3 +1,5 @@
+import functools
+
 import jax
 import jax.numpy as jnp
 from jax import lax
@@ -211,7 +213,7 @@
 
 
 def backward_body(
-    up, parts, gain, ss, ttst, w1t, back, n2t, g0, g1, g2, g3, gpe_o, qr_o, gpn_o, gu_o, gain_o
+    up, parts, gain, ss, ttst, w1t, back, n2t, sends, gpe_o, qr_o, gpn_o, gu_o, gain_o
 ):
     edge_slope, node_slope, normed, inv_dev = parts
     gain_o[...] = jnp.sum(up * normed, axis=0, keepdims=True)
@@ -234,15 +236,22 @@
         gpe_o[lo : lo + CHUNK] = part
         gpe.append(part)
     qr = mm(ttst[...], jnp.concatenate(gpe, axis=0))
+    if sends:
+        halo_grads(qr, w1t, sends)
+    qr_o[...] = qr
+
+
+def halo_grads(qr, w1t, sends):
     q_high, q_low = split(qr[OWN : 2 * OWN])
     far = w1t[:, :L]
     ge = mm(q_high, far) + mm(q_low, far)
-    for i, out in enumerate((g0, g1, g2, g3)):
+    for i, out in enumerate(sends):
         out[...] = ge[i * HALO : (i + 1) * HALO].astype(BF16)
-    qr_o[...] = qr
-
-
-def rest_kernel(up, qr, gpn, w1t, back, own_out):
+
+
+def rest_kernel(up, qr, gpn, w1t, back, own_out, *sends):
+    if sends:
+        halo_grads(qr, w1t, sends)
     q_high, q_low = split(qr[:OWN])
     r_high, r_low = split(qr[2 * OWN :])
     far, near = w1t[:, :L], w1t[:, L : 2 * L]
@@ -272,19 +281,19 @@
     hidden_node_o[...] = hidden_node
     backward_body(
         cot[...], (edge_slope, node_slope, normed, inv_dev), gain[...], ss, ttst, w1t, back, n2t,
-        g0, g1, g2, g3, gpe_o, qr_o, gpn_o, gu_o, gain_o,
+        (g0, g1, g2, g3), gpe_o, qr_o, gpn_o, gu_o, gain_o,
     )
 
 
 def backward_kernel(
     own, p0, p1, p2, p3, spread, edge_slope, node_slope, normed, inv_dev, gain, ss, ttst, w1t, back, n2t,
-    g0, g1, g2, g3, gpe_o, qr_o, gpn_o, gu_o, gain_o, up_o,
+    gpe_o, qr_o, gpn_o, gu_o, gain_o, up_o, *sends,
 ):
     up = landed(own, spread, p0, p1, p2, p3)
     up_o[...] = up
     backward_body(
         up, (edge_slope, node_slope[...], normed[...], inv_dev[:, :1]), gain[...], ss, ttst, w1t, back, n2t,
-        g0, g1, g2, g3, gpe_o, qr_o, gpn_o, gu_o, gain_o,
+        sends, gpe_o, qr_o, gpn_o, gu_o, gain_o,
     )
 
 
@@ -342,19 +351,43 @@
     out[...] = landed(own, spread, p0, p1, p2, p3)
 
 
-def finish_kernel(factor, mine, other, edge_in, edge_out, node_in, node_out, gain):
+def finish_kernel(factor, mine, half_ref, *refs):
+    edge_in, edge_out, node_in, node_out, gain, buf, row, sems = refs[-8:]
     core = lax.axis_index("c")
-
-    def half(index, lo, hi):
-        a = mine[lo:hi].astype(F32)
-        b = other[lo:hi].astype(F32)
-        return jnp.where(core == index, a, b) * factor
-
-    edge_in[...] = half(0, 0, 3 * L)
-    edge_out[...] = half(0, 3 * L, 4 * L)
-    node_in[...] = half(1, 0, 2 * L)
-    node_out[...] = half(1, 2 * L, 3 * L)
-    gain[...] = half(1, 3 * L, 3 * L + 8)[0]
+    which = core if mine else 1 - core
+    targets = (
+        (edge_in.at[:L], edge_in.at[L : 2 * L], edge_in.at[2 * L :], edge_out),
+        (node_in.at[:L], node_in.at[L :], node_out, gain),
+    )
+
+    def copies(half, i):
+        source = row if half == 1 and i == 3 else buf.at[i * L : (i + 1) * L]
+        return pltpu.make_async_copy(source, targets[half][i], sems.at[i])
+
+    for i in range(4):
+        block = half_ref[i * L : (i + 1) * L].astype(F32) * factor
+        buf[i * L : (i + 1) * L] = block
+        if i == 3:
+            row[...] = block[0]
+        for half in range(2):
+            pl.when(which == half)(lambda half=half, i=i: copies(half, i).start())
+    for half in range(2):
+        for i in range(4):
+            pl.when(which == half)(lambda half=half, i=i: copies(half, i).wait())
+
+
+def finish(factor, mine, half, *parts):
+    outs = [((3 * L, L), F32), ((L, L), F32), ((2 * L, L), F32), ((L, L), F32), ((L,), F32)]
+    hbm = pl.BlockSpec(memory_space=pltpu.HBM)
+    return pl.pallas_call(
+        functools.partial(finish_kernel, factor, mine),
+        out_shape=[jax.ShapeDtypeStruct(s, d) for s, d in outs],
+        in_specs=[pl.BlockSpec(memory_space=pltpu.VMEM)] + [hbm] * len(parts),
+        out_specs=[hbm] * 5,
+        input_output_aliases={i + 1: i for i in range(len(parts))},
+        scratch_shapes=[pltpu.VMEM((4 * L, L), F32), pltpu.VMEM((L,), F32), pltpu.SemaphoreType.DMA((4,))],
+        compiler_params=pltpu.CompilerParams(vmem_limit_bytes=32 * 1024 * 1024),
+    )(half, *parts)
 
 
 def even_pairs(size):
@@ -377,7 +410,7 @@
     ]
 
 
-def reduce_all(payload, back):
+def reduce_all(payload, late):
     keep = payload[0].astype(F32)
     got = lax.ppermute(payload[1], "c", [(0, 1), (1, 0)])
     part = (keep + got.astype(F32)).astype(BF16).reshape(CHUNKS, CHUNK_ROWS, L)
@@ -386,11 +419,11 @@
     deep = lax.axis_size("z")
     part = lax.all_to_all(jnp.broadcast_to(part[None], (deep,) + part.shape), "z", 0, 0, tiled=True)
     part = jnp.sum(part.astype(F32), axis=0).astype(BF16)
-    part, *back = lax.optimization_barrier((part, *back))
+    part, *late = lax.optimization_barrier((part, *late))
     part = jnp.broadcast_to(part[None], (CHUNKS,) + part.shape)
     mine = lax.all_to_all(part, PLANE, 0, 0, tiled=True).reshape(CHUNKS * CHUNK_ROWS, L)
     other = lax.ppermute(mine, "c", [(0, 1), (1, 0)])
-    return mine, other, back
+    return mine, other, late
 
 
 def local(
@@ -440,12 +473,12 @@
         saved.append((h, halo, rest))
         h = nxt
     halo = exchange(sends)
-    back_outs = halo_outs + [
+    back_outs = [
         ((edges, L), BF16), ((3 * OWN, L), F32), ((OWN, L), BF16), ((OWN, L), BF16), ((1, L), F32),
     ]
     g0, g1, g2, g3, *terms, gain_term, hidden_sum, hidden_node = call(
         turn_kernel,
-        back_outs + [((OWN, L), F32), ((OWN, L), BF16)],
+        halo_outs + back_outs + [((OWN, L), F32), ((OWN, L), BF16)],
         h, *halo, pre_part, th, st, edge_w1, node_w1, mix, node_w2, gain, cotangent, ss, ttst, w1t, back_w, n2t,
         scratch_shapes=[pltpu.VMEM((edges, L), F32)],
     )
@@ -458,30 +491,28 @@
     )
     for layer in reversed(range(STEPS - 1)):
         h, halo, (edge_slope, hidden_sum, node_slope, hidden_node, normed, inv_dev) = saved[layer]
-        g0, g1, g2, g3, *terms, gain_term, up = call(
-            backward_kernel, back_outs + own_out,
+        gpe, qr, gpn, gu, gain_term, up, *sends = call(
+            backward_kernel, back_outs + own_out + (halo_outs if layer > 0 else []),
             own, *back, spread, edge_slope, node_slope, normed, inv_dev, gain, ss, ttst, w1t, back_w, n2t,
         )
-        back = exchange([g0, g1, g2, g3])
-        (own,) = call(rest_kernel, own_out, up, terms[1], terms[2], w1t, back_w)
+        terms = (gpe, qr, gpn, gu)
+        rest_outs = own_out if layer > 0 else own_out + halo_outs
+        own, *late = call(rest_kernel, rest_outs, up, terms[1], terms[2], w1t, back_w)
+        back = exchange(sends + late)
         shared = (h, *halo, feats, edge_w2, hidden_sum, hidden_node, back_w, *terms)
         if layer > 0:
             totals = call(weight_kernel, acc_outs, *shared, w1t, gain_term, *totals)
     (payload,) = call(
         weight_last_kernel, [((2, 4 * L, L), BF16)], *shared, gain_term, totals[0], totals[2]
     )
-    mine, other, back = reduce_all(payload, back)
     (edge_grad,) = call(edge_last_kernel, [((edges, L), F32)], terms[0], w1t, totals[1])
     (node_grad,) = call(node_last_kernel, [((OWN, L), F32)], own, *back, spread)
+    mine, other, (node_grad, edge_grad) = reduce_all(payload, (node_grad, edge_grad))
     devices = lax.axis_size(REGION) * lax.axis_size(SLAB)
     factor = float(OWN * devices) ** (-0.5)
 
-    def finish(*refs):
-        finish_kernel(factor, *refs)
-
-    edge_in, edge_out, node_in, node_out, gain_grad = call(
-        finish, [((3 * L, L), F32), ((L, L), F32), ((2 * L, L), F32), ((L, L), F32), ((L,), F32)], mine, other
-    )
+    parts = finish(factor, True, mine)
+    edge_in, edge_out, node_in, node_out, gain_grad = finish(factor, False, other, *parts)
     return node_grad, edge_grad, edge_in, edge_out, node_in, node_out, gain_grad
 
 

time: 139 us -> 138 us (level)
  waiting for transfers between devices: 7.27 us -> 5.77 us
    all_to_all x1, waiting for transfers between devices: 3.94 us -> 1.53 us  [reduce_all(): lax.all_to_all(jnp.broadcast_to(part[None], (deep,) + part.shape), 'z', 0...]
    pallas_call x0 -> x2, Pallas kernels: none -> 1.95 us  [finish(): pl.pallas_call(functools.partial(finish_kernel, factor, mine), out_shape=...]
    pallas_call x23 -> x22, Pallas kernels: 24.8 us -> 23.3 us  [call(): pl.pallas_call(kernel, out_shape=[jax.ShapeDtypeStruct(s, d) for s, d in...]
  transfers between devices with their start and end apart: 35 -> 35, of which waited for: 6 -> 8; matrix products, arithmetic and copies ran while one was open for 0% -> 0% of each run, Pallas kernels for 9% -> 9%
where the time goes in v4:
time: 138 us
  starting transfers between devices  73.5 us (53%)
  blocking collectives  30.7 us (22%)
  Pallas kernels  25.3 us (18%)
  waiting for transfers between devices  5.77 us (4%)
  between operations  1.83 us (1%)
    ppermute x8, starting transfers between devices, exchange(): lax.ppermute(parts[0], REGION, odd_pairs(regions))  28.8 us
    ppermute x8, starting transfers between devices, exchange(): lax.ppermute(parts[3], SLAB, even_pairs(slabs))  27 us
    pallas_call x22, Pallas kernels, call(): pl.pallas_call(kernel, out_shape=[jax.ShapeDtypeStruct(s, d) for s, d in...  23.3 us
    all_to_all x1, blocking collectives, reduce_all(): part = lax.all_to_all(part, PLANE, 0, 0, tiled=True)  16.3 us
    all_to_all x1, blocking collectives, reduce_all(): lax.all_to_all(part, PLANE, 0, 0, tiled=True)  14.4 us
    all_to_all x1, starting transfers between devices, reduce_all(): lax.all_to_all(jnp.broadcast_to(part[None], (deep,) + part.shape), 'z', 0...  4.94 us
    ppermute x8, starting transfers between devices, exchange(): lax.ppermute(parts[2], SLAB, odd_pairs(slabs))  4.21 us
    ppermute x1, starting transfers between devices, reduce_all(): other = lax.ppermute(mine, 'c', [(0, 1), (1, 0)])  3.3 us
  transfers between devices with their start and end apart: 35, of which 8 were waited for; matrix products, arithmetic and copies ran while one was open for 0% of the time, Pallas kernels for 9%

profile of v4, /device:TPU:1, one launch (start us, length us, event | category | flops | bytes accessed | tf_op | source)
XLA Modules:
  0.0 138.1 jit_solution(10540910721310120384)
XLA Ops:
  1.7 6.0 %collective-permute-start = (bf16[32,256]{1,0:T(8,128)(2,1)S(1)}, bf16[32,256]{1,0:T(8,128)(2,1)S(1)}, u32[]{:S(2)}, u32[]{:S(2)}) collective-permute-start(bf16[32,256]{1,0:T(8,128)(2,1)S(1)} %get-tuple-element.140.q0), channel_id=1, source_target_pairs={{32,64},{96,128},{160,192},{224,0},{64,32},{128,96},{192,160},{0,2... | collective-permute-start | bytes 49160 | tf_op jit(solution)/shard_map/ppermute | solution.py:406
  7.8 1.2 collective-permute-start.2
  9.0 4.8 %collective-permute-start.3 = (bf16[32,256]{1,0:T(8,128)(2,1)S(1)}, bf16[32,256]{1,0:T(8,128)(2,1)S(1)}, u32[]{:S(2)}, u32[]{:S(2)}) collective-permute-start(bf16[32,256]{1,0:T(8,128)(2,1)S(1)} %get-tuple-element.143.q3), channel_id=1, source_target_pairs={{0,1},{1,0},{2,3},{3,2},{4,5},{5,4},{6,7},{7,6},{8,9},{9,8},{10,11... | collective-permute-start | bytes 49160 | tf_op jit(solution)/shard_map/ppermute | solution.py:409
  14.5 2.3 %shard_map.172 = (bf16[640,512]{1,0:T(8,128)(2,1)S(1)}, bf16[640,256]{1,0:T(8,128)(2,1)S(1)}, bf16[640,256]{1,0:T(8,128)(2,1)S(1)}, bf16[384,640]{1,0:T(8,128)(2...) custom-call(s32[1,1]{1,0:T(1,128)S(6)} %copy.29.count_in, ...), custom_call_target="tpu_custom_call" | custom-call | tf_op jit(solution)/shard_map/pallas_call | solution.py:54
  18.1 3.9 %collective-permute-start.4 = (bf16[32,256]{1,0:T(8,128)(2,1)S(1)}, bf16[32,256]{1,0:T(8,128)(2,1)S(1)}, u32[]{:S(2)}, u32[]{:S(2)}) collective-permute-start(bf16[32,256]{1,0:T(8,128)(2,1)S(1)} %get-tuple-element.164.q0), channel_id=1, source_target_pairs={{32,64},{96,128},{160,192},{224,0},{64,32},{128,96},{192,160},{0,2... | collective-permute-start | bytes 49160 | tf_op jit(solution)/shard_map/ppermute | solution.py:406
  22.0 2.0 %collective-permute-start.7 = (bf16[32,256]{1,0:T(8,128)(2,1)S(1)}, bf16[32,256]{1,0:T(8,128)(2,1)S(1)}, u32[]{:S(2)}, u32[]{:S(2)}) collective-permute-start(bf16[32,256]{1,0:T(8,128)(2,1)S(1)} %get-tuple-element.167.q3), channel_id=1, source_target_pairs={{0,1},{1,0},{2,3},{3,2},{4,5},{5,4},{6,7},{7,6},{8,9},{9,8},{10,11... | collective-permute-start | bytes 49160 | tf_op jit(solution)/shard_map/ppermute | solution.py:409
  24.0 1.5 %shard_map.174 = (bf16[128,256]{1,0:T(8,128)(2,1)S(1)}, f32[640,256]{1,0:T(8,128)S(1)}, f32[640,256]{1,0:T(8,128)S(1)}, f32[128,256]{1,0:T(8,128)S(1)}, f32[128,...) custom-call(bf16[128,256]{1,0:T(8,128)(2,1)S(1)} %get-tuple-element.139.h_ref.re, ...), custom_call_target="tpu_custom_call" | custom-call | tf_op jit(solution)/shard_map/pallas_call | solution.py:54
  27.3 2.7 %collective-permute-start.8 = (bf16[32,256]{1,0:T(8,128)(2,1)S(1)}, bf16[32,256]{1,0:T(8,128)(2,1)S(1)}, u32[]{:S(2)}, u32[]{:S(2)}) collective-permute-start(bf16[32,256]{1,0:T(8,128)(2,1)S(1)} %get-tuple-element.172.q0), channel_id=1, source_target_pairs={{32,64},{96,128},{160,192},{224,0},{64,32},{128,96},{192,160},{0,2... | collective-permute-start | bytes 49160 | tf_op jit(solution)/shard_map/ppermute | solution.py:406
  31.0 3.1 %collective-permute-start.11 = (bf16[32,256]{1,0:T(8,128)(2,1)S(1)}, bf16[32,256]{1,0:T(8,128)(2,1)S(1)}, u32[]{:S(2)}, u32[]{:S(2)}) collective-permute-start(bf16[32,256]{1,0:T(8,128)(2,1)S(1)} %get-tuple-element.175.q3), channel_id=1, source_target_pairs={{0,1},{1,0},{2,3},{3,2},{4,5},{5,4},{6,7},{7,6},{8,9},{9,8},{10,11... | collective-permute-start | bytes 49160 | tf_op jit(solution)/shard_map/ppermute | solution.py:409
  34.1 1.5 %shard_map.176 = (bf16[128,256]{1,0:T(8,128)(2,1)S(1)}, f32[640,256]{1,0:T(8,128)S(1)}, f32[640,256]{1,0:T(8,128)S(1)}, f32[128,256]{1,0:T(8,128)S(1)}, f32[128,...) custom-call(bf16[128,256]{1,0:T(8,128)(2,1)S(1)} %get-tuple-element.163.h_ref.re, ...), custom_call_target="tpu_custom_call" | custom-call | tf_op jit(solution)/shard_map/pallas_call | solution.py:54
  35.7 1.2 shard_map.177
  36.9 2.6 %collective-permute-start.12 = (bf16[32,256]{1,0:T(8,128)(2,1)S(1)}, bf16[32,256]{1,0:T(8,128)(2,1)S(1)}, u32[]{:S(2)}, u32[]{:S(2)}) collective-permute-start(bf16[32,256]{1,0:T(8,128)(2,1)S(1)} %get-tuple-element.180), channel_id=1, source_target_pairs={{32,64},{96,128},{160,192},{224,0},{64,32},{128,96},{192,160},{0,2... | collective-permute-start | bytes 49160 | tf_op jit(solution)/shard_map/ppermute | solution.py:406
  40.3 3.3 %collective-permute-start.15 = (bf16[32,256]{1,0:T(8,128)(2,1)S(1)}, bf16[32,256]{1,0:T(8,128)(2,1)S(1)}, u32[]{:S(2)}, u32[]{:S(2)}) collective-permute-start(bf16[32,256]{1,0:T(8,128)(2,1)S(1)} %get-tuple-element.183), channel_id=1, source_target_pairs={{0,1},{1,0},{2,3},{3,2},{4,5},{5,4},{6,7},{7,6},{8,9},{9,8},{10,11... | collective-permute-start | bytes 49160 | tf_op jit(solution)/shard_map/ppermute | solution.py:409
  43.6 1.5 %shard_map.178 = (bf16[128,256]{1,0:T(8,128)(2,1)S(1)}, f32[640,256]{1,0:T(8,128)S(1)}, f32[640,256]{1,0:T(8,128)S(1)}, f32[128,256]{1,0:T(8,128)S(1)}, f32[128,...) custom-call(bf16[128,256]{1,0:T(8,128)(2,1)S(1)} %get-tuple-element.171.h_ref.re, ...), custom_call_target="tpu_custom_call" | custom-call | tf_op jit(solution)/shard_map/pallas_call | solution.py:54
  45.2 2.3 %shard_map.179 = (bf16[32,256]{1,0:T(8,128)(2,1)S(1)}, bf16[32,256]{1,0:T(8,128)(2,1)S(1)}, bf16[32,256]{1,0:T(8,128)(2,1)S(1)}, bf16[32,256]{1,0:T(8,128)(2,1)S...) custom-call(bf16[128,256]{1,0:T(8,128)(2,1)S(1)} %get-tuple-element., ...), custom_call_target="tpu_custom_call" | custom-call | tf_op jit(solution)/shard_map/pallas_call | solution.py:54
  47.4 4.9 %collective-permute-start.16 = (bf16[32,256]{1,0:T(8,128)(2,1)S(1)}, bf16[32,256]{1,0:T(8,128)(2,1)S(1)}, u32[]{:S(2)}, u32[]{:S(2)}) collective-permute-start(bf16[32,256]{1,0:T(8,128)(2,1)S(1)} %get-tuple-element.191), channel_id=1, source_target_pairs={{32,64},{96,128},{160,192},{224,0},{64,32},{128,96},{192,160},{0,2... | collective-permute-start | bytes 49160 | tf_op jit(solution)/shard_map/ppermute | solution.py:406
  52.3 3.4 %collective-permute-start.19 = (bf16[32,256]{1,0:T(8,128)(2,1)S(1)}, bf16[32,256]{1,0:T(8,128)(2,1)S(1)}, u32[]{:S(2)}, u32[]{:S(2)}) collective-permute-start(bf16[32,256]{1,0:T(8,128)(2,1)S(1)} %get-tuple-element.194), channel_id=1, source_target_pairs={{0,1},{1,0},{2,3},{3,2},{4,5},{5,4},{6,7},{7,6},{8,9},{9,8},{10,11... | collective-permute-start | bytes 49160 | tf_op jit(solution)/shard_map/ppermute | solution.py:409
  56.6 1.3 shard_map.181
  57.9 3.6 %collective-permute-start.20 = (bf16[32,256]{1,0:T(8,128)(2,1)S(1)}, bf16[32,256]{1,0:T(8,128)(2,1)S(1)}, u32[]{:S(2)}, u32[]{:S(2)}) collective-permute-start(bf16[32,256]{1,0:T(8,128)(2,1)S(1)} %get-tuple-element.202), channel_id=1, source_target_pairs={{32,64},{96,128},{160,192},{224,0},{64,32},{128,96},{192,160},{0,2... | collective-permute-start | bytes 49160 | tf_op jit(solution)/shard_map/ppermute | solution.py:406
  61.5 4.8 %collective-permute-start.23 = (bf16[32,256]{1,0:T(8,128)(2,1)S(1)}, bf16[32,256]{1,0:T(8,128)(2,1)S(1)}, u32[]{:S(2)}, u32[]{:S(2)}) collective-permute-start(bf16[32,256]{1,0:T(8,128)(2,1)S(1)} %get-tuple-element.205), channel_id=1, source_target_pairs={{0,1},{1,0},{2,3},{3,2},{4,5},{5,4},{6,7},{7,6},{8,9},{9,8},{10,11... | collective-permute-start | bytes 49160 | tf_op jit(solution)/shard_map/ppermute | solution.py:409
  67.2 1.3 shard_map.183
  68.5 3.2 %collective-permute-start.24 = (bf16[32,256]{1,0:T(8,128)(2,1)S(1)}, bf16[32,256]{1,0:T(8,128)(2,1)S(1)}, u32[]{:S(2)}, u32[]{:S(2)}) collective-permute-start(bf16[32,256]{1,0:T(8,128)(2,1)S(1)} %get-tuple-element.213), channel_id=1, source_target_pairs={{32,64},{96,128},{160,192},{224,0},{64,32},{128,96},{192,160},{0,2... | collective-permute-start | bytes 49160 | tf_op jit(solution)/shard_map/ppermute | solution.py:406
  72.0 5.0 %collective-permute-start.27 = (bf16[32,256]{1,0:T(8,128)(2,1)S(1)}, bf16[32,256]{1,0:T(8,128)(2,1)S(1)}, u32[]{:S(2)}, u32[]{:S(2)}) collective-permute-start(bf16[32,256]{1,0:T(8,128)(2,1)S(1)} %get-tuple-element.216), channel_id=1, source_target_pairs={{0,1},{1,0},{2,3},{3,2},{4,5},{5,4},{6,7},{7,6},{8,9},{9,8},{10,11... | collective-permute-start | bytes 49160 | tf_op jit(solution)/shard_map/ppermute | solution.py:409
  81.5 2.7 %collective-permute-start.28 = (bf16[1024,256]{1,0:T(8,128)(2,1)S(1)}, bf16[1024,256]{1,0:T(8,128)(2,1)S(1)}, u32[]{:S(2)}, u32[]{:S(2)}) collective-permute-start(bf16[1024,256]{1,0:T(8,128)(2,1)S(1)} %slice_bitcast_fusion), channel_id=1, source_target_pairs={{0,1},{1,0},{2,3},{3,2},{4,5},{5,4},{6,7},{7,6},{8,9},{9,8},{10,11... | collective-permute-start | bytes 1572872 | tf_op jit(solution)/shard_map/ppermute | solution.py:415
  84.2 1.5 %collective-permute-done.28 = bf16[1024,256]{1,0:T(8,128)(2,1)S(1)} collective-permute-done((bf16[1024,256]{1,0:T(8,128)(2,1)S(1)}, bf16[1024,256]{1,0:T(8,128)(2,1)S(1)}, u32[]{:S(2)}, u32[]{:S(2)}) %collective-permute-start.28) | collective-permute-done | bytes 524320 | tf_op jit(solution)/shard_map/ppermute | solution.py:415
  85.9 16.3 %all_to_all.15 = bf16[16,64,256]{2,1,0:T(8,128)(2,1)S(1)} all-to-all(bf16[16,64,256]{2,1,0:T(8,128)(2,1)S(1)} %bitcast.11), channel_id=1, replica_groups=mesh['x'=4,'yh'=2,'z'=8,'yl'=2,'c'=2] {'x','yh','yl'}, dimensions={0} | all-to-all | bytes 1048576 | tf_op jit(solution)/shard_map/all_to_all | solution.py:417
  103.0 4.9 %all-to-all-start.1 = ((bf16[8,64,256]{2,1,0:T(8,128)(2,1)}), bf16[8,64,256]{2,1,0:T(8,128)(2,1)S(1)}, u32[]{:S(2)}, u32[]{:S(2)}) async-start(bf16[8,64,256]{2,1,0:T(8,128)(2,1)} %broadcast_in_dim.4), calls=%async_computation.1 | async-start | bytes 524288 | tf_op jit(solution)/shard_map/all_to_all | solution.py:420
  108.2 1.8 %collective-permute-start.29 = (bf16[32,256]{1,0:T(8,128)(2,1)S(1)}, bf16[32,256]{1,0:T(8,128)(2,1)S(1)}, u32[]{:S(2)}, u32[]{:S(2)}) collective-permute-start(bf16[32,256]{1,0:T(8,128)(2,1)S(1)} %get-tuple-element.251), channel_id=1, source_target_pairs={{32,64},{96,128},{160,192},{224,0},{64,32},{128,96},{192,160},{0,2... | collective-permute-start | bytes 49160 | tf_op jit(solution)/shard_map/ppermute | solution.py:406
  110.7 2.6 %collective-permute-start.31 = (bf16[32,256]{1,0:T(8,128)(2,1)S(1)}, bf16[32,256]{1,0:T(8,128)(2,1)S(1)}, u32[]{:S(2)}, u32[]{:S(2)}) collective-permute-start(bf16[32,256]{1,0:T(8,128)(2,1)S(1)} %get-tuple-element.253), channel_id=1, source_target_pairs={{1,2},{3,4},{5,6},{7,8},{9,10},{11,12},{13,14},{15,16},{17,18},{19... | collective-permute-start | bytes 49160 | tf_op jit(solution)/shard_map/ppermute | solution.py:408
  116.0 1.5 %all-to-all-done.1 = bf16[8,64,256]{2,1,0:T(8,128)(2,1)S(1)} async-done(((bf16[8,64,256]{2,1,0:T(8,128)(2,1)}), bf16[8,64,256]{2,1,0:T(8,128)(2,1)S(1)}, u32[]{:S(2)}, u32[]{:S(2)}) %all-to-all-start.1) | async-done | bytes 262176 | tf_op jit(solution)/shard_map/all_to_all | solution.py:420
  117.6 14.4 %all_to_all.16 = bf16[16,64,256]{2,1,0:T(8,128)(2,1)S(1)} all-to-all(bf16[16,64,256]{2,1,0:T(8,128)(2,1)S(1)} %broadcast_in_dim.5), channel_id=1, replica_groups=mesh['x'=4,'yh'=2,'z'=8,'yl'=2,'c'=2] {'x','yh','yl'}, dimensions={0} | all-to-all | bytes 1048576 | tf_op jit(solution)/shard_map/all_to_all | solution.py:424
  132.1 3.3 %collective-permute-start.33 = (bf16[1024,256]{1,0:T(8,128)(2,1)S(1)}, bf16[1024,256]{1,0:T(8,128)(2,1)S(1)}, u32[]{:S(2)}, u32[]{:S(2)}) collective-permute-start(bf16[1024,256]{1,0:T(8,128)(2,1)S(1)} %bitcast.9), channel_id=1, source_target_pairs={{0,1},{1,0},{2,3},{3,2},{4,5},{5,4},{6,7},{7,6},{8,9},{9,8},{10,11... | collective-permute-start | bytes 1572872 | tf_op jit(solution)/shard_map/ppermute | solution.py:425
  (70 shorter events, 19.6 us)
Async XLA Ops:
  1.7 15.1 %collective-permute-start = (bf16[32,256]{1,0:T(8,128)(2,1)S(1)}, bf16[32,256]{1,0:T(8,128)(2,1)S(1)}, u32[]{:S(2)}, u32[]{:S(2)}) collective-permute-start(bf16[32,256]{1,0:T(8,128)(2,1)S(1)} %get-tuple-element.140.q0), channel_id=1, source_target_pairs={{32,64},{96,128},{160,192},{224,0},{64,32},{128,96},{192,160},{0,2... | collective-permute-start | bytes 49160 | tf_op jit(solution)/shard_map/ppermute | solution.py:406
  7.7 9.1 %collective-permute-start.1 = (bf16[32,256]{1,0:T(8,128)(2,1)S(1)}, bf16[32,256]{1,0:T(8,128)(2,1)S(1)}, u32[]{:S(2)}, u32[]{:S(2)}) collective-permute-start(bf16[32,256]{1,0:T(8,128)(2,1)S(1)} %get-tuple-element.141.q1), channel_id=1, source_target_pairs={{0,32},{32,0},{64,96},{96,64},{128,160},{160,128},{192,224},{224,1... | collective-permute-start | bytes 49160 | tf_op jit(solution)/shard_map/ppermute | solution.py:407
  7.8 9.1 %collective-permute-start.2 = (bf16[32,256]{1,0:T(8,128)(2,1)S(1)}, bf16[32,256]{1,0:T(8,128)(2,1)S(1)}, u32[]{:S(2)}, u32[]{:S(2)}) collective-permute-start(bf16[32,256]{1,0:T(8,128)(2,1)S(1)} %get-tuple-element.142.q2), channel_id=1, source_target_pairs={{1,2},{3,4},{5,6},{7,8},{9,10},{11,12},{13,14},{15,16},{17,18},{19... | collective-permute-start | bytes 49160 | tf_op jit(solution)/shard_map/ppermute | solution.py:408
  9.0 7.9 %collective-permute-start.3 = (bf16[32,256]{1,0:T(8,128)(2,1)S(1)}, bf16[32,256]{1,0:T(8,128)(2,1)S(1)}, u32[]{:S(2)}, u32[]{:S(2)}) collective-permute-start(bf16[32,256]{1,0:T(8,128)(2,1)S(1)} %get-tuple-element.143.q3), channel_id=1, source_target_pairs={{0,1},{1,0},{2,3},{3,2},{4,5},{5,4},{6,7},{7,6},{8,9},{9,8},{10,11... | collective-permute-start | bytes 49160 | tf_op jit(solution)/shard_map/ppermute | solution.py:409
  18.1 7.4 %collective-permute-start.4 = (bf16[32,256]{1,0:T(8,128)(2,1)S(1)}, bf16[32,256]{1,0:T(8,128)(2,1)S(1)}, u32[]{:S(2)}, u32[]{:S(2)}) collective-permute-start(bf16[32,256]{1,0:T(8,128)(2,1)S(1)} %get-tuple-element.164.q0), channel_id=1, source_target_pairs={{32,64},{96,128},{160,192},{224,0},{64,32},{128,96},{192,160},{0,2... | collective-permute-start | bytes 49160 | tf_op jit(solution)/shard_map/ppermute | solution.py:406
  22.0 4.1 %collective-permute-start.5 = (bf16[32,256]{1,0:T(8,128)(2,1)S(1)}, bf16[32,256]{1,0:T(8,128)(2,1)S(1)}, u32[]{:S(2)}, u32[]{:S(2)}) collective-permute-start(bf16[32,256]{1,0:T(8,128)(2,1)S(1)} %get-tuple-element.165.q1), channel_id=1, source_target_pairs={{0,32},{32,0},{64,96},{96,64},{128,160},{160,128},{192,224},{224,1... | collective-permute-start | bytes 49160 | tf_op jit(solution)/shard_map/ppermute | solution.py:407
  22.0 4.1 %collective-permute-start.6 = (bf16[32,256]{1,0:T(8,128)(2,1)S(1)}, bf16[32,256]{1,0:T(8,128)(2,1)S(1)}, u32[]{:S(2)}, u32[]{:S(2)}) collective-permute-start(bf16[32,256]{1,0:T(8,128)(2,1)S(1)} %get-tuple-element.166.q2), channel_id=1, source_target_pairs={{1,2},{3,4},{5,6},{7,8},{9,10},{11,12},{13,14},{15,16},{17,18},{19... | collective-permute-start | bytes 49160 | tf_op jit(solution)/shard_map/ppermute | solution.py:408
  22.0 4.1 %collective-permute-start.7 = (bf16[32,256]{1,0:T(8,128)(2,1)S(1)}, bf16[32,256]{1,0:T(8,128)(2,1)S(1)}, u32[]{:S(2)}, u32[]{:S(2)}) collective-permute-start(bf16[32,256]{1,0:T(8,128)(2,1)S(1)} %get-tuple-element.167.q3), channel_id=1, source_target_pairs={{0,1},{1,0},{2,3},{3,2},{4,5},{5,4},{6,7},{7,6},{8,9},{9,8},{10,11... | collective-permute-start | bytes 49160 | tf_op jit(solution)/shard_map/ppermute | solution.py:409
  27.3 8.3 %collective-permute-start.8 = (bf16[32,256]{1,0:T(8,128)(2,1)S(1)}, bf16[32,256]{1,0:T(8,128)(2,1)S(1)}, u32[]{:S(2)}, u32[]{:S(2)}) collective-permute-start(bf16[32,256]{1,0:T(8,128)(2,1)S(1)} %get-tuple-element.172.q0), channel_id=1, source_target_pairs={{32,64},{96,128},{160,192},{224,0},{64,32},{128,96},{192,160},{0,2... | collective-permute-start | bytes 49160 | tf_op jit(solution)/shard_map/ppermute | solution.py:406
  30.0 5.7 %collective-permute-start.9 = (bf16[32,256]{1,0:T(8,128)(2,1)S(1)}, bf16[32,256]{1,0:T(8,128)(2,1)S(1)}, u32[]{:S(2)}, u32[]{:S(2)}) collective-permute-start(bf16[32,256]{1,0:T(8,128)(2,1)S(1)} %get-tuple-element.173.q1), channel_id=1, source_target_pairs={{0,32},{32,0},{64,96},{96,64},{128,160},{160,128},{192,224},{224,1... | collective-permute-start | bytes 49160 | tf_op jit(solution)/shard_map/ppermute | solution.py:407
  31.0 4.7 %collective-permute-start.10 = (bf16[32,256]{1,0:T(8,128)(2,1)S(1)}, bf16[32,256]{1,0:T(8,128)(2,1)S(1)}, u32[]{:S(2)}, u32[]{:S(2)}) collective-permute-start(bf16[32,256]{1,0:T(8,128)(2,1)S(1)} %get-tuple-element.174.q2), channel_id=1, source_target_pairs={{1,2},{3,4},{5,6},{7,8},{9,10},{11,12},{13,14},{15,16},{17,18},{19... | collective-permute-start | bytes 49160 | tf_op jit(solution)/shard_map/ppermute | solution.py:408
  31.0 4.7 %collective-permute-start.11 = (bf16[32,256]{1,0:T(8,128)(2,1)S(1)}, bf16[32,256]{1,0:T(8,128)(2,1)S(1)}, u32[]{:S(2)}, u32[]{:S(2)}) collective-permute-start(bf16[32,256]{1,0:T(8,128)(2,1)S(1)} %get-tuple-element.175.q3), channel_id=1, source_target_pairs={{0,1},{1,0},{2,3},{3,2},{4,5},{5,4},{6,7},{7,6},{8,9},{9,8},{10,11... | collective-permute-start | bytes 49160 | tf_op jit(solution)/shard_map/ppermute | solution.py:409
  36.9 8.2 %collective-permute-start.12 = (bf16[32,256]{1,0:T(8,128)(2,1)S(1)}, bf16[32,256]{1,0:T(8,128)(2,1)S(1)}, u32[]{:S(2)}, u32[]{:S(2)}) collective-permute-start(bf16[32,256]{1,0:T(8,128)(2,1)S(1)} %get-tuple-element.180), channel_id=1, source_target_pairs={{32,64},{96,128},{160,192},{224,0},{64,32},{128,96},{192,160},{0,2... | collective-permute-start | bytes 49160 | tf_op jit(solution)/shard_map/ppermute | solution.py:406
  39.5 5.6 %collective-permute-start.13 = (bf16[32,256]{1,0:T(8,128)(2,1)S(1)}, bf16[32,256]{1,0:T(8,128)(2,1)S(1)}, u32[]{:S(2)}, u32[]{:S(2)}) collective-permute-start(bf16[32,256]{1,0:T(8,128)(2,1)S(1)} %get-tuple-element.181), channel_id=1, source_target_pairs={{0,32},{32,0},{64,96},{96,64},{128,160},{160,128},{192,224},{224,1... | collective-permute-start | bytes 49160 | tf_op jit(solution)/shard_map/ppermute | solution.py:407
  39.9 5.3 %collective-permute-start.14 = (bf16[32,256]{1,0:T(8,128)(2,1)S(1)}, bf16[32,256]{1,0:T(8,128)(2,1)S(1)}, u32[]{:S(2)}, u32[]{:S(2)}) collective-permute-start(bf16[32,256]{1,0:T(8,128)(2,1)S(1)} %get-tuple-element.182), channel_id=1, source_target_pairs={{1,2},{3,4},{5,6},{7,8},{9,10},{11,12},{13,14},{15,16},{17,18},{19... | collective-permute-start | bytes 49160 | tf_op jit(solution)/shard_map/ppermute | solution.py:408
  40.3 4.9 %collective-permute-start.15 = (bf16[32,256]{1,0:T(8,128)(2,1)S(1)}, bf16[32,256]{1,0:T(8,128)(2,1)S(1)}, u32[]{:S(2)}, u32[]{:S(2)}) collective-permute-start(bf16[32,256]{1,0:T(8,128)(2,1)S(1)} %get-tuple-element.183), channel_id=1, source_target_pairs={{0,1},{1,0},{2,3},{3,2},{4,5},{5,4},{6,7},{7,6},{8,9},{9,8},{10,11... | collective-permute-start | bytes 49160 | tf_op jit(solution)/shard_map/ppermute | solution.py:409
  47.4 8.6 %collective-permute-start.16 = (bf16[32,256]{1,0:T(8,128)(2,1)S(1)}, bf16[32,256]{1,0:T(8,128)(2,1)S(1)}, u32[]{:S(2)}, u32[]{:S(2)}) collective-permute-start(bf16[32,256]{1,0:T(8,128)(2,1)S(1)} %get-tuple-element.191), channel_id=1, source_target_pairs={{32,64},{96,128},{160,192},{224,0},{64,32},{128,96},{192,160},{0,2... | collective-permute-start | bytes 49160 | tf_op jit(solution)/shard_map/ppermute | solution.py:406
  52.3 4.3 %collective-permute-start.19 = (bf16[32,256]{1,0:T(8,128)(2,1)S(1)}, bf16[32,256]{1,0:T(8,128)(2,1)S(1)}, u32[]{:S(2)}, u32[]{:S(2)}) collective-permute-start(bf16[32,256]{1,0:T(8,128)(2,1)S(1)} %get-tuple-element.194), channel_id=1, source_target_pairs={{0,1},{1,0},{2,3},{3,2},{4,5},{5,4},{6,7},{7,6},{8,9},{9,8},{10,11... | collective-permute-start | bytes 49160 | tf_op jit(solution)/shard_map/ppermute | solution.py:409
  57.9 8.7 %collective-permute-start.20 = (bf16[32,256]{1,0:T(8,128)(2,1)S(1)}, bf16[32,256]{1,0:T(8,128)(2,1)S(1)}, u32[]{:S(2)}, u32[]{:S(2)}) collective-permute-start(bf16[32,256]{1,0:T(8,128)(2,1)S(1)} %get-tuple-element.202), channel_id=1, source_target_pairs={{32,64},{96,128},{160,192},{224,0},{64,32},{128,96},{192,160},{0,2... | collective-permute-start | bytes 49160 | tf_op jit(solution)/shard_map/ppermute | solution.py:406
  61.5 5.1 %collective-permute-start.21 = (bf16[32,256]{1,0:T(8,128)(2,1)S(1)}, bf16[32,256]{1,0:T(8,128)(2,1)S(1)}, u32[]{:S(2)}, u32[]{:S(2)}) collective-permute-start(bf16[32,256]{1,0:T(8,128)(2,1)S(1)} %get-tuple-element.203), channel_id=1, source_target_pairs={{0,32},{32,0},{64,96},{96,64},{128,160},{160,128},{192,224},{224,1... | collective-permute-start | bytes 49160 | tf_op jit(solution)/shard_map/ppermute | solution.py:407
  61.5 5.1 %collective-permute-start.22 = (bf16[32,256]{1,0:T(8,128)(2,1)S(1)}, bf16[32,256]{1,0:T(8,128)(2,1)S(1)}, u32[]{:S(2)}, u32[]{:S(2)}) collective-permute-start(bf16[32,256]{1,0:T(8,128)(2,1)S(1)} %get-tuple-element.204), channel_id=1, source_target_pairs={{1,2},{3,4},{5,6},{7,8},{9,10},{11,12},{13,14},{15,16},{17,18},{19... | collective-permute-start | bytes 49160 | tf_op jit(solution)/shard_map/ppermute | solution.py:408
  61.5 5.7 %collective-permute-start.23 = (bf16[32,256]{1,0:T(8,128)(2,1)S(1)}, bf16[32,256]{1,0:T(8,128)(2,1)S(1)}, u32[]{:S(2)}, u32[]{:S(2)}) collective-permute-start(bf16[32,256]{1,0:T(8,128)(2,1)S(1)} %get-tuple-element.205), channel_id=1, source_target_pairs={{0,1},{1,0},{2,3},{3,2},{4,5},{5,4},{6,7},{7,6},{8,9},{9,8},{10,11... | collective-permute-start | bytes 49160 | tf_op jit(solution)/shard_map/ppermute | solution.py:409
  68.5 11.1 %collective-permute-start.24 = (bf16[32,256]{1,0:T(8,128)(2,1)S(1)}, bf16[32,256]{1,0:T(8,128)(2,1)S(1)}, u32[]{:S(2)}, u32[]{:S(2)}) collective-permute-start(bf16[32,256]{1,0:T(8,128)(2,1)S(1)} %get-tuple-element.213), channel_id=1, source_target_pairs={{32,64},{96,128},{160,192},{224,0},{64,32},{128,96},{192,160},{0,2... | collective-permute-start | bytes 49160 | tf_op jit(solution)/shard_map/ppermute | solution.py:406
  71.6 8.0 %collective-permute-start.25 = (bf16[32,256]{1,0:T(8,128)(2,1)S(1)}, bf16[32,256]{1,0:T(8,128)(2,1)S(1)}, u32[]{:S(2)}, u32[]{:S(2)}) collective-permute-start(bf16[32,256]{1,0:T(8,128)(2,1)S(1)} %get-tuple-element.214), channel_id=1, source_target_pairs={{0,32},{32,0},{64,96},{96,64},{128,160},{160,128},{192,224},{224,1... | collective-permute-start | bytes 49160 | tf_op jit(solution)/shard_map/ppermute | solution.py:407
  72.0 7.6 %collective-permute-start.26 = (bf16[32,256]{1,0:T(8,128)(2,1)S(1)}, bf16[32,256]{1,0:T(8,128)(2,1)S(1)}, u32[]{:S(2)}, u32[]{:S(2)}) collective-permute-start(bf16[32,256]{1,0:T(8,128)(2,1)S(1)} %get-tuple-element.215), channel_id=1, source_target_pairs={{1,2},{3,4},{5,6},{7,8},{9,10},{11,12},{13,14},{15,16},{17,18},{19... | collective-permute-start | bytes 49160 | tf_op jit(solution)/shard_map/ppermute | solution.py:408
  72.0 7.6 %collective-permute-start.27 = (bf16[32,256]{1,0:T(8,128)(2,1)S(1)}, bf16[32,256]{1,0:T(8,128)(2,1)S(1)}, u32[]{:S(2)}, u32[]{:S(2)}) collective-permute-start(bf16[32,256]{1,0:T(8,128)(2,1)S(1)} %get-tuple-element.216), channel_id=1, source_target_pairs={{0,1},{1,0},{2,3},{3,2},{4,5},{5,4},{6,7},{7,6},{8,9},{9,8},{10,11... | collective-permute-start | bytes 49160 | tf_op jit(solution)/shard_map/ppermute | solution.py:409
  81.5 4.3 %collective-permute-start.28 = (bf16[1024,256]{1,0:T(8,128)(2,1)S(1)}, bf16[1024,256]{1,0:T(8,128)(2,1)S(1)}, u32[]{:S(2)}, u32[]{:S(2)}) collective-permute-start(bf16[1024,256]{1,0:T(8,128)(2,1)S(1)} %slice_bitcast_fusion), channel_id=1, source_target_pairs={{0,1},{1,0},{2,3},{3,2},{4,5},{5,4},{6,7},{7,6},{8,9},{9,8},{10,11... | collective-permute-start | bytes 1572872 | tf_op jit(solution)/shard_map/ppermute | solution.py:415
  103.0 14.6 %all-to-all-start.1 = ((bf16[8,64,256]{2,1,0:T(8,128)(2,1)}), bf16[8,64,256]{2,1,0:T(8,128)(2,1)S(1)}, u32[]{:S(2)}, u32[]{:S(2)}) async-start(bf16[8,64,256]{2,1,0:T(8,128)(2,1)} %broadcast_in_dim.4), calls=%async_computation.1 | async-start | bytes 524288 | tf_op jit(solution)/shard_map/all_to_all | solution.py:420
  108.2 6.7 %collective-permute-start.29 = (bf16[32,256]{1,0:T(8,128)(2,1)S(1)}, bf16[32,256]{1,0:T(8,128)(2,1)S(1)}, u32[]{:S(2)}, u32[]{:S(2)}) collective-permute-start(bf16[32,256]{1,0:T(8,128)(2,1)S(1)} %get-tuple-element.251), channel_id=1, source_target_pairs={{32,64},{96,128},{160,192},{224,0},{64,32},{128,96},{192,160},{0,2... | collective-permute-start | bytes 49160 | tf_op jit(solution)/shard_map/ppermute | solution.py:406
  110.0 4.9 %collective-permute-start.30 = (bf16[32,256]{1,0:T(8,128)(2,1)S(1)}, bf16[32,256]{1,0:T(8,128)(2,1)S(1)}, u32[]{:S(2)}, u32[]{:S(2)}) collective-permute-start(bf16[32,256]{1,0:T(8,128)(2,1)S(1)} %get-tuple-element.252), channel_id=1, source_target_pairs={{0,32},{32,0},{64,96},{96,64},{128,160},{160,128},{192,224},{224,1... | collective-permute-start | bytes 49160 | tf_op jit(solution)/shard_map/ppermute | solution.py:407
  110.7 4.5 %collective-permute-start.31 = (bf16[32,256]{1,0:T(8,128)(2,1)S(1)}, bf16[32,256]{1,0:T(8,128)(2,1)S(1)}, u32[]{:S(2)}, u32[]{:S(2)}) collective-permute-start(bf16[32,256]{1,0:T(8,128)(2,1)S(1)} %get-tuple-element.253), channel_id=1, source_target_pairs={{1,2},{3,4},{5,6},{7,8},{9,10},{11,12},{13,14},{15,16},{17,18},{19... | collective-permute-start | bytes 49160 | tf_op jit(solution)/shard_map/ppermute | solution.py:408
  132.1 4.8 %collective-permute-start.33 = (bf16[1024,256]{1,0:T(8,128)(2,1)S(1)}, bf16[1024,256]{1,0:T(8,128)(2,1)S(1)}, u32[]{:S(2)}, u32[]{:S(2)}) collective-permute-start(bf16[1024,256]{1,0:T(8,128)(2,1)S(1)} %bitcast.9), channel_id=1, source_target_pairs={{0,1},{1,0},{2,3},{3,2},{4,5},{5,4},{6,7},{7,6},{8,9},{9,8},{10,11... | collective-permute-start | bytes 1572872 | tf_op jit(solution)/shard_map/ppermute | solution.py:425
  (3 other events, 10.1 us)

commit v5 on v4

--- a/solution.py
+++ b/solution.py
@@ -18,8 +18,9 @@
 AXES = ("x", "yh", "z", "yl", "c")
 REGION = ("x", "yh")
 SLAB = ("z", "yl", "c")
-PLANE = ("x", "yh", "yl")
+PLANE = ("yl", "yh", "x")
 CHUNK = 128
+EDGE_CHUNK = 640
 CHUNKS = 16
 CHUNK_ROWS = 64
 
@@ -77,11 +78,11 @@
     copies = [pltpu.make_async_copy(nodes, h, sems.at[0]), pltpu.make_async_copy(lists, rows, sems.at[1])]
     for copy in copies:
         copy.start()
-    for copy in copies:
-        copy.wait()
+    copies[1].wait()
     row = lax.broadcasted_iota(jnp.int32, (OWN, HALO), 0)
-    for i, (idx, out) in enumerate(zip(slot_lists(rows[...]), (s0, s1, s2, s3))):
-        hot = (row == idx).astype(F32).astype(BF16)
+    hots = [(row == idx).astype(F32).astype(BF16) for idx in slot_lists(rows[...])]
+    copies[0].wait()
+    for i, (hot, out) in enumerate(zip(hots, (s0, s1, s2, s3))):
         spread[:, i * HALO : (i + 1) * HALO] = hot
         out[...] = mm_t(hot, h[...]).astype(BF16)
 
@@ -145,8 +146,8 @@
     high, low = split(mm(jnp.concatenate(halo, axis=0), edge_w1[:L]))
     table = jnp.concatenate([high, low], axis=0)
     hidden = []
-    for lo in range(0, pre_part.shape[0], CHUNK):
-        pre = mm(th[lo : lo + CHUNK], table) + pre_part[lo : lo + CHUNK]
+    for lo in range(0, pre_part.shape[0], EDGE_CHUNK):
+        pre = mm(th[lo : lo + EDGE_CHUNK], table) + pre_part[lo : lo + EDGE_CHUNK]
         hidden.append(keep(lo, pre))
     return jnp.concatenate(hidden, axis=0)
 
@@ -181,9 +182,9 @@
     s0, s1, s2, s3, pre_o, hidden_o,
 ):
     def keep(lo, pre):
-        pre_o[lo : lo + CHUNK] = pre
+        pre_o[lo : lo + EDGE_CHUNK] = pre
         part = (pre * sigmoid(pre)).astype(BF16)
-        hidden_o[lo : lo + CHUNK] = part
+        hidden_o[lo : lo + EDGE_CHUNK] = part
         return part
 
     hidden = edge_hidden([p0[...], p1[...], p2[...], p3[...]], th, pre_part, edge_w1, keep)
@@ -271,7 +272,7 @@
 ):
     def keep(lo, pre):
         silu, slope = edge_slopes(pre)
-        edge_slope[lo : lo + CHUNK] = slope
+        edge_slope[lo : lo + EDGE_CHUNK] = slope
         return silu.astype(BF16)
 
     hidden = edge_hidden([p0[...], p1[...], p2[...], p3[...]], th, pre_part, edge_w1, keep)

time: 138 us -> 138 us (level)
  no operation moved by 1% of the time
where the time goes in v5:
time: 138 us
  starting transfers between devices  72.6 us (53%)
  blocking collectives  31.9 us (23%)
  Pallas kernels  25.2 us (18%)
  waiting for transfers between devices  5.52 us (4%)
  between operations  1.83 us (1%)
    ppermute x8, starting transfers between devices, exchange(): lax.ppermute(parts[0], REGION, odd_pairs(regions))  28 us
    ppermute x8, starting transfers between devices, exchange(): lax.ppermute(parts[3], SLAB, even_pairs(slabs))  27.1 us
    pallas_call x22, Pallas kernels, call(): pl.pallas_call(kernel, out_shape=[jax.ShapeDtypeStruct(s, d) for s, d in...  23.2 us
    all_to_all x1, blocking collectives, reduce_all(): part = lax.all_to_all(part, PLANE, 0, 0, tiled=True)  16.9 us
    all_to_all x1, blocking collectives, reduce_all(): lax.all_to_all(part, PLANE, 0, 0, tiled=True)  15 us
    all_to_all x1, starting transfers between devices, reduce_all(): lax.all_to_all(jnp.broadcast_to(part[None], (deep,) + part.shape), 'z', 0...  4.95 us
    ppermute x8, starting transfers between devices, exchange(): lax.ppermute(parts[1], REGION, even_pairs(regions))  3.87 us
    ppermute x8, starting transfers between devices, exchange(): lax.ppermute(parts[2], SLAB, odd_pairs(slabs))  3.77 us
  transfers between devices with their start and end apart: 35, of which 8 were waited for; matrix products, arithmetic and copies ran while one was open for 0% of the time, Pallas kernels for 9%

profile of v5, /device:TPU:1, one launch (start us, length us, event | category | flops | bytes accessed | tf_op | source)
XLA Modules:
  0.0 138.1 jit_solution(16555924776414759068)
XLA Ops:
  1.7 6.0 %collective-permute-start = (bf16[32,256]{1,0:T(8,128)(2,1)S(1)}, bf16[32,256]{1,0:T(8,128)(2,1)S(1)}, u32[]{:S(2)}, u32[]{:S(2)}) collective-permute-start(bf16[32,256]{1,0:T(8,128)(2,1)S(1)} %get-tuple-element.140.q0), channel_id=1, source_target_pairs={{32,64},{96,128},{160,192},{224,0},{64,32},{128,96},{192,160},{0,2... | collective-permute-start | bytes 49160 | tf_op jit(solution)/shard_map/ppermute | solution.py:407
  7.7 1.2 collective-permute-start.2
  9.0 4.8 %collective-permute-start.3 = (bf16[32,256]{1,0:T(8,128)(2,1)S(1)}, bf16[32,256]{1,0:T(8,128)(2,1)S(1)}, u32[]{:S(2)}, u32[]{:S(2)}) collective-permute-start(bf16[32,256]{1,0:T(8,128)(2,1)S(1)} %get-tuple-element.143.q3), channel_id=1, source_target_pairs={{0,1},{1,0},{2,3},{3,2},{4,5},{5,4},{6,7},{7,6},{8,9},{9,8},{10,11... | collective-permute-start | bytes 49160 | tf_op jit(solution)/shard_map/ppermute | solution.py:410
  14.5 2.3 %shard_map.172 = (bf16[640,512]{1,0:T(8,128)(2,1)S(1)}, bf16[640,256]{1,0:T(8,128)(2,1)S(1)}, bf16[640,256]{1,0:T(8,128)(2,1)S(1)}, bf16[384,640]{1,0:T(8,128)(2...) custom-call(s32[1,1]{1,0:T(1,128)S(6)} %copy.29.count_in, ...), custom_call_target="tpu_custom_call" | custom-call | tf_op jit(solution)/shard_map/pallas_call | solution.py:55
  16.9 1.2 shard_map.173
  18.0 3.9 %collective-permute-start.4 = (bf16[32,256]{1,0:T(8,128)(2,1)S(1)}, bf16[32,256]{1,0:T(8,128)(2,1)S(1)}, u32[]{:S(2)}, u32[]{:S(2)}) collective-permute-start(bf16[32,256]{1,0:T(8,128)(2,1)S(1)} %get-tuple-element.164.q0), channel_id=1, source_target_pairs={{32,64},{96,128},{160,192},{224,0},{64,32},{128,96},{192,160},{0,2... | collective-permute-start | bytes 49160 | tf_op jit(solution)/shard_map/ppermute | solution.py:407
  22.0 2.0 %collective-permute-start.7 = (bf16[32,256]{1,0:T(8,128)(2,1)S(1)}, bf16[32,256]{1,0:T(8,128)(2,1)S(1)}, u32[]{:S(2)}, u32[]{:S(2)}) collective-permute-start(bf16[32,256]{1,0:T(8,128)(2,1)S(1)} %get-tuple-element.167.q3), channel_id=1, source_target_pairs={{0,1},{1,0},{2,3},{3,2},{4,5},{5,4},{6,7},{7,6},{8,9},{9,8},{10,11... | collective-permute-start | bytes 49160 | tf_op jit(solution)/shard_map/ppermute | solution.py:410
  23.9 1.5 %shard_map.174 = (bf16[128,256]{1,0:T(8,128)(2,1)S(1)}, f32[640,256]{1,0:T(8,128)S(1)}, f32[640,256]{1,0:T(8,128)S(1)}, f32[128,256]{1,0:T(8,128)S(1)}, f32[128,...) custom-call(bf16[128,256]{1,0:T(8,128)(2,1)S(1)} %get-tuple-element.139.h_ref.re, ...), custom_call_target="tpu_custom_call" | custom-call | tf_op jit(solution)/shard_map/pallas_call | solution.py:55
  27.2 2.7 %collective-permute-start.8 = (bf16[32,256]{1,0:T(8,128)(2,1)S(1)}, bf16[32,256]{1,0:T(8,128)(2,1)S(1)}, u32[]{:S(2)}, u32[]{:S(2)}) collective-permute-start(bf16[32,256]{1,0:T(8,128)(2,1)S(1)} %get-tuple-element.172.q0), channel_id=1, source_target_pairs={{32,64},{96,128},{160,192},{224,0},{64,32},{128,96},{192,160},{0,2... | collective-permute-start | bytes 49160 | tf_op jit(solution)/shard_map/ppermute | solution.py:407
  30.9 3.1 %collective-permute-start.11 = (bf16[32,256]{1,0:T(8,128)(2,1)S(1)}, bf16[32,256]{1,0:T(8,128)(2,1)S(1)}, u32[]{:S(2)}, u32[]{:S(2)}) collective-permute-start(bf16[32,256]{1,0:T(8,128)(2,1)S(1)} %get-tuple-element.175.q3), channel_id=1, source_target_pairs={{0,1},{1,0},{2,3},{3,2},{4,5},{5,4},{6,7},{7,6},{8,9},{9,8},{10,11... | collective-permute-start | bytes 49160 | tf_op jit(solution)/shard_map/ppermute | solution.py:410
  34.1 1.5 %shard_map.176 = (bf16[128,256]{1,0:T(8,128)(2,1)S(1)}, f32[640,256]{1,0:T(8,128)S(1)}, f32[640,256]{1,0:T(8,128)S(1)}, f32[128,256]{1,0:T(8,128)S(1)}, f32[128,...) custom-call(bf16[128,256]{1,0:T(8,128)(2,1)S(1)} %get-tuple-element.163.h_ref.re, ...), custom_call_target="tpu_custom_call" | custom-call | tf_op jit(solution)/shard_map/pallas_call | solution.py:55
  36.8 2.6 %collective-permute-start.12 = (bf16[32,256]{1,0:T(8,128)(2,1)S(1)}, bf16[32,256]{1,0:T(8,128)(2,1)S(1)}, u32[]{:S(2)}, u32[]{:S(2)}) collective-permute-start(bf16[32,256]{1,0:T(8,128)(2,1)S(1)} %get-tuple-element.180), channel_id=1, source_target_pairs={{32,64},{96,128},{160,192},{224,0},{64,32},{128,96},{192,160},{0,2... | collective-permute-start | bytes 49160 | tf_op jit(solution)/shard_map/ppermute | solution.py:407
  40.2 3.3 %collective-permute-start.15 = (bf16[32,256]{1,0:T(8,128)(2,1)S(1)}, bf16[32,256]{1,0:T(8,128)(2,1)S(1)}, u32[]{:S(2)}, u32[]{:S(2)}) collective-permute-start(bf16[32,256]{1,0:T(8,128)(2,1)S(1)} %get-tuple-element.183), channel_id=1, source_target_pairs={{0,1},{1,0},{2,3},{3,2},{4,5},{5,4},{6,7},{7,6},{8,9},{9,8},{10,11... | collective-permute-start | bytes 49160 | tf_op jit(solution)/shard_map/ppermute | solution.py:410
  43.5 1.5 %shard_map.178 = (bf16[128,256]{1,0:T(8,128)(2,1)S(1)}, f32[640,256]{1,0:T(8,128)S(1)}, f32[640,256]{1,0:T(8,128)S(1)}, f32[128,256]{1,0:T(8,128)S(1)}, f32[128,...) custom-call(bf16[128,256]{1,0:T(8,128)(2,1)S(1)} %get-tuple-element.171.h_ref.re, ...), custom_call_target="tpu_custom_call" | custom-call | tf_op jit(solution)/shard_map/pallas_call | solution.py:55
  45.1 2.2 %shard_map.179 = (bf16[32,256]{1,0:T(8,128)(2,1)S(1)}, bf16[32,256]{1,0:T(8,128)(2,1)S(1)}, bf16[32,256]{1,0:T(8,128)(2,1)S(1)}, bf16[32,256]{1,0:T(8,128)(2,1)S...) custom-call(bf16[128,256]{1,0:T(8,128)(2,1)S(1)} %get-tuple-element., ...), custom_call_target="tpu_custom_call" | custom-call | tf_op jit(solution)/shard_map/pallas_call | solution.py:55
  47.3 4.9 %collective-permute-start.16 = (bf16[32,256]{1,0:T(8,128)(2,1)S(1)}, bf16[32,256]{1,0:T(8,128)(2,1)S(1)}, u32[]{:S(2)}, u32[]{:S(2)}) collective-permute-start(bf16[32,256]{1,0:T(8,128)(2,1)S(1)} %get-tuple-element.191), channel_id=1, source_target_pairs={{32,64},{96,128},{160,192},{224,0},{64,32},{128,96},{192,160},{0,2... | collective-permute-start | bytes 49160 | tf_op jit(solution)/shard_map/ppermute | solution.py:407
  52.2 3.4 %collective-permute-start.19 = (bf16[32,256]{1,0:T(8,128)(2,1)S(1)}, bf16[32,256]{1,0:T(8,128)(2,1)S(1)}, u32[]{:S(2)}, u32[]{:S(2)}) collective-permute-start(bf16[32,256]{1,0:T(8,128)(2,1)S(1)} %get-tuple-element.194), channel_id=1, source_target_pairs={{0,1},{1,0},{2,3},{3,2},{4,5},{5,4},{6,7},{7,6},{8,9},{9,8},{10,11... | collective-permute-start | bytes 49160 | tf_op jit(solution)/shard_map/ppermute | solution.py:410
  56.5 1.3 shard_map.181
  57.8 3.7 %collective-permute-start.20 = (bf16[32,256]{1,0:T(8,128)(2,1)S(1)}, bf16[32,256]{1,0:T(8,128)(2,1)S(1)}, u32[]{:S(2)}, u32[]{:S(2)}) collective-permute-start(bf16[32,256]{1,0:T(8,128)(2,1)S(1)} %get-tuple-element.202), channel_id=1, source_target_pairs={{32,64},{96,128},{160,192},{224,0},{64,32},{128,96},{192,160},{0,2... | collective-permute-start | bytes 49160 | tf_op jit(solution)/shard_map/ppermute | solution.py:407
  61.5 4.8 %collective-permute-start.23 = (bf16[32,256]{1,0:T(8,128)(2,1)S(1)}, bf16[32,256]{1,0:T(8,128)(2,1)S(1)}, u32[]{:S(2)}, u32[]{:S(2)}) collective-permute-start(bf16[32,256]{1,0:T(8,128)(2,1)S(1)} %get-tuple-element.205), channel_id=1, source_target_pairs={{0,1},{1,0},{2,3},{3,2},{4,5},{5,4},{6,7},{7,6},{8,9},{9,8},{10,11... | collective-permute-start | bytes 49160 | tf_op jit(solution)/shard_map/ppermute | solution.py:410
  67.1 1.3 shard_map.183
  68.4 3.2 %collective-permute-start.24 = (bf16[32,256]{1,0:T(8,128)(2,1)S(1)}, bf16[32,256]{1,0:T(8,128)(2,1)S(1)}, u32[]{:S(2)}, u32[]{:S(2)}) collective-permute-start(bf16[32,256]{1,0:T(8,128)(2,1)S(1)} %get-tuple-element.213), channel_id=1, source_target_pairs={{32,64},{96,128},{160,192},{224,0},{64,32},{128,96},{192,160},{0,2... | collective-permute-start | bytes 49160 | tf_op jit(solution)/shard_map/ppermute | solution.py:407
  71.9 5.0 %collective-permute-start.27 = (bf16[32,256]{1,0:T(8,128)(2,1)S(1)}, bf16[32,256]{1,0:T(8,128)(2,1)S(1)}, u32[]{:S(2)}, u32[]{:S(2)}) collective-permute-start(bf16[32,256]{1,0:T(8,128)(2,1)S(1)} %get-tuple-element.216), channel_id=1, source_target_pairs={{0,1},{1,0},{2,3},{3,2},{4,5},{5,4},{6,7},{7,6},{8,9},{9,8},{10,11... | collective-permute-start | bytes 49160 | tf_op jit(solution)/shard_map/ppermute | solution.py:410
  81.4 2.7 %collective-permute-start.28 = (bf16[1024,256]{1,0:T(8,128)(2,1)S(1)}, bf16[1024,256]{1,0:T(8,128)(2,1)S(1)}, u32[]{:S(2)}, u32[]{:S(2)}) collective-permute-start(bf16[1024,256]{1,0:T(8,128)(2,1)S(1)} %slice_bitcast_fusion), channel_id=1, source_target_pairs={{0,1},{1,0},{2,3},{3,2},{4,5},{5,4},{6,7},{7,6},{8,9},{9,8},{10,11... | collective-permute-start | bytes 1572872 | tf_op jit(solution)/shard_map/ppermute | solution.py:416
  84.1 1.5 %collective-permute-done.28 = bf16[1024,256]{1,0:T(8,128)(2,1)S(1)} collective-permute-done((bf16[1024,256]{1,0:T(8,128)(2,1)S(1)}, bf16[1024,256]{1,0:T(8,128)(2,1)S(1)}, u32[]{:S(2)}, u32[]{:S(2)}) %collective-permute-start.28) | collective-permute-done | bytes 524320 | tf_op jit(solution)/shard_map/ppermute | solution.py:416
  85.8 16.9 %all_to_all.15 = bf16[16,64,256]{2,1,0:T(8,128)(2,1)S(1)} all-to-all(bf16[16,64,256]{2,1,0:T(8,128)(2,1)S(1)} %bitcast.11), channel_id=1, replica_groups=mesh['x'=4,'yh'=2,'z'=8,'yl'=2,'c'=2] {'yl','yh','x'}, dimensions={0} | all-to-all | bytes 1048576 | tf_op jit(solution)/shard_map/all_to_all | solution.py:418
  103.5 4.9 %all-to-all-start.1 = ((bf16[8,64,256]{2,1,0:T(8,128)(2,1)}), bf16[8,64,256]{2,1,0:T(8,128)(2,1)S(1)}, u32[]{:S(2)}, u32[]{:S(2)}) async-start(bf16[8,64,256]{2,1,0:T(8,128)(2,1)} %broadcast_in_dim.4), calls=%async_computation.1 | async-start | bytes 524288 | tf_op jit(solution)/shard_map/all_to_all | solution.py:421
  109.7 2.1 %collective-permute-start.30 = (bf16[32,256]{1,0:T(8,128)(2,1)S(1)}, bf16[32,256]{1,0:T(8,128)(2,1)S(1)}, u32[]{:S(2)}, u32[]{:S(2)}) collective-permute-start(bf16[32,256]{1,0:T(8,128)(2,1)S(1)} %get-tuple-element.252), channel_id=1, source_target_pairs={{0,32},{32,0},{64,96},{96,64},{128,160},{160,128},{192,224},{224,1... | collective-permute-start | bytes 49160 | tf_op jit(solution)/shard_map/ppermute | solution.py:408
  111.8 2.1 %collective-permute-start.31 = (bf16[32,256]{1,0:T(8,128)(2,1)S(1)}, bf16[32,256]{1,0:T(8,128)(2,1)S(1)}, u32[]{:S(2)}, u32[]{:S(2)}) collective-permute-start(bf16[32,256]{1,0:T(8,128)(2,1)S(1)} %get-tuple-element.253), channel_id=1, source_target_pairs={{1,2},{3,4},{5,6},{7,8},{9,10},{11,12},{13,14},{15,16},{17,18},{19... | collective-permute-start | bytes 49160 | tf_op jit(solution)/shard_map/ppermute | solution.py:409
  116.7 1.4 %all-to-all-done.1 = bf16[8,64,256]{2,1,0:T(8,128)(2,1)S(1)} async-done(((bf16[8,64,256]{2,1,0:T(8,128)(2,1)}), bf16[8,64,256]{2,1,0:T(8,128)(2,1)S(1)}, u32[]{:S(2)}, u32[]{:S(2)}) %all-to-all-start.1) | async-done | bytes 262176 | tf_op jit(solution)/shard_map/all_to_all | solution.py:421
  118.2 15.0 %all_to_all.16 = bf16[16,64,256]{2,1,0:T(8,128)(2,1)S(1)} all-to-all(bf16[16,64,256]{2,1,0:T(8,128)(2,1)S(1)} %broadcast_in_dim.5), channel_id=1, replica_groups=mesh['x'=4,'yh'=2,'z'=8,'yl'=2,'c'=2] {'yl','yh','x'}, dimensions={0} | all-to-all | bytes 1048576 | tf_op jit(solution)/shard_map/all_to_all | solution.py:425
  133.1 2.2 %collective-permute-start.33 = (bf16[1024,256]{1,0:T(8,128)(2,1)S(1)}, bf16[1024,256]{1,0:T(8,128)(2,1)S(1)}, u32[]{:S(2)}, u32[]{:S(2)}) collective-permute-start(bf16[1024,256]{1,0:T(8,128)(2,1)S(1)} %bitcast.9), channel_id=1, source_target_pairs={{0,1},{1,0},{2,3},{3,2},{4,5},{5,4},{6,7},{7,6},{8,9},{9,8},{10,11... | collective-permute-start | bytes 1572872 | tf_op jit(solution)/shard_map/ppermute | solution.py:426
  (70 shorter events, 19.7 us)
Async XLA Ops:
  1.7 15.1 %collective-permute-start = (bf16[32,256]{1,0:T(8,128)(2,1)S(1)}, bf16[32,256]{1,0:T(8,128)(2,1)S(1)}, u32[]{:S(2)}, u32[]{:S(2)}) collective-permute-start(bf16[32,256]{1,0:T(8,128)(2,1)S(1)} %get-tuple-element.140.q0), channel_id=1, source_target_pairs={{32,64},{96,128},{160,192},{224,0},{64,32},{128,96},{192,160},{0,2... | collective-permute-start | bytes 49160 | tf_op jit(solution)/shard_map/ppermute | solution.py:407
  7.7 9.1 %collective-permute-start.1 = (bf16[32,256]{1,0:T(8,128)(2,1)S(1)}, bf16[32,256]{1,0:T(8,128)(2,1)S(1)}, u32[]{:S(2)}, u32[]{:S(2)}) collective-permute-start(bf16[32,256]{1,0:T(8,128)(2,1)S(1)} %get-tuple-element.141.q1), channel_id=1, source_target_pairs={{0,32},{32,0},{64,96},{96,64},{128,160},{160,128},{192,224},{224,1... | collective-permute-start | bytes 49160 | tf_op jit(solution)/shard_map/ppermute | solution.py:408
  7.7 9.1 %collective-permute-start.2 = (bf16[32,256]{1,0:T(8,128)(2,1)S(1)}, bf16[32,256]{1,0:T(8,128)(2,1)S(1)}, u32[]{:S(2)}, u32[]{:S(2)}) collective-permute-start(bf16[32,256]{1,0:T(8,128)(2,1)S(1)} %get-tuple-element.142.q2), channel_id=1, source_target_pairs={{1,2},{3,4},{5,6},{7,8},{9,10},{11,12},{13,14},{15,16},{17,18},{19... | collective-permute-start | bytes 49160 | tf_op jit(solution)/shard_map/ppermute | solution.py:409
  9.0 7.9 %collective-permute-start.3 = (bf16[32,256]{1,0:T(8,128)(2,1)S(1)}, bf16[32,256]{1,0:T(8,128)(2,1)S(1)}, u32[]{:S(2)}, u32[]{:S(2)}) collective-permute-start(bf16[32,256]{1,0:T(8,128)(2,1)S(1)} %get-tuple-element.143.q3), channel_id=1, source_target_pairs={{0,1},{1,0},{2,3},{3,2},{4,5},{5,4},{6,7},{7,6},{8,9},{9,8},{10,11... | collective-permute-start | bytes 49160 | tf_op jit(solution)/shard_map/ppermute | solution.py:410
  18.0 7.4 %collective-permute-start.4 = (bf16[32,256]{1,0:T(8,128)(2,1)S(1)}, bf16[32,256]{1,0:T(8,128)(2,1)S(1)}, u32[]{:S(2)}, u32[]{:S(2)}) collective-permute-start(bf16[32,256]{1,0:T(8,128)(2,1)S(1)} %get-tuple-element.164.q0), channel_id=1, source_target_pairs={{32,64},{96,128},{160,192},{224,0},{64,32},{128,96},{192,160},{0,2... | collective-permute-start | bytes 49160 | tf_op jit(solution)/shard_map/ppermute | solution.py:407
  22.0 4.1 %collective-permute-start.5 = (bf16[32,256]{1,0:T(8,128)(2,1)S(1)}, bf16[32,256]{1,0:T(8,128)(2,1)S(1)}, u32[]{:S(2)}, u32[]{:S(2)}) collective-permute-start(bf16[32,256]{1,0:T(8,128)(2,1)S(1)} %get-tuple-element.165.q1), channel_id=1, source_target_pairs={{0,32},{32,0},{64,96},{96,64},{128,160},{160,128},{192,224},{224,1... | collective-permute-start | bytes 49160 | tf_op jit(solution)/shard_map/ppermute | solution.py:408
  22.0 4.1 %collective-permute-start.6 = (bf16[32,256]{1,0:T(8,128)(2,1)S(1)}, bf16[32,256]{1,0:T(8,128)(2,1)S(1)}, u32[]{:S(2)}, u32[]{:S(2)}) collective-permute-start(bf16[32,256]{1,0:T(8,128)(2,1)S(1)} %get-tuple-element.166.q2), channel_id=1, source_target_pairs={{1,2},{3,4},{5,6},{7,8},{9,10},{11,12},{13,14},{15,16},{17,18},{19... | collective-permute-start | bytes 49160 | tf_op jit(solution)/shard_map/ppermute | solution.py:409
  22.0 4.1 %collective-permute-start.7 = (bf16[32,256]{1,0:T(8,128)(2,1)S(1)}, bf16[32,256]{1,0:T(8,128)(2,1)S(1)}, u32[]{:S(2)}, u32[]{:S(2)}) collective-permute-start(bf16[32,256]{1,0:T(8,128)(2,1)S(1)} %get-tuple-element.167.q3), channel_id=1, source_target_pairs={{0,1},{1,0},{2,3},{3,2},{4,5},{5,4},{6,7},{7,6},{8,9},{9,8},{10,11... | collective-permute-start | bytes 49160 | tf_op jit(solution)/shard_map/ppermute | solution.py:410
  27.2 8.3 %collective-permute-start.8 = (bf16[32,256]{1,0:T(8,128)(2,1)S(1)}, bf16[32,256]{1,0:T(8,128)(2,1)S(1)}, u32[]{:S(2)}, u32[]{:S(2)}) collective-permute-start(bf16[32,256]{1,0:T(8,128)(2,1)S(1)} %get-tuple-element.172.q0), channel_id=1, source_target_pairs={{32,64},{96,128},{160,192},{224,0},{64,32},{128,96},{192,160},{0,2... | collective-permute-start | bytes 49160 | tf_op jit(solution)/shard_map/ppermute | solution.py:407
  29.9 5.7 %collective-permute-start.9 = (bf16[32,256]{1,0:T(8,128)(2,1)S(1)}, bf16[32,256]{1,0:T(8,128)(2,1)S(1)}, u32[]{:S(2)}, u32[]{:S(2)}) collective-permute-start(bf16[32,256]{1,0:T(8,128)(2,1)S(1)} %get-tuple-element.173.q1), channel_id=1, source_target_pairs={{0,32},{32,0},{64,96},{96,64},{128,160},{160,128},{192,224},{224,1... | collective-permute-start | bytes 49160 | tf_op jit(solution)/shard_map/ppermute | solution.py:408
  30.9 4.7 %collective-permute-start.10 = (bf16[32,256]{1,0:T(8,128)(2,1)S(1)}, bf16[32,256]{1,0:T(8,128)(2,1)S(1)}, u32[]{:S(2)}, u32[]{:S(2)}) collective-permute-start(bf16[32,256]{1,0:T(8,128)(2,1)S(1)} %get-tuple-element.174.q2), channel_id=1, source_target_pairs={{1,2},{3,4},{5,6},{7,8},{9,10},{11,12},{13,14},{15,16},{17,18},{19... | collective-permute-start | bytes 49160 | tf_op jit(solution)/shard_map/ppermute | solution.py:409
  30.9 4.7 %collective-permute-start.11 = (bf16[32,256]{1,0:T(8,128)(2,1)S(1)}, bf16[32,256]{1,0:T(8,128)(2,1)S(1)}, u32[]{:S(2)}, u32[]{:S(2)}) collective-permute-start(bf16[32,256]{1,0:T(8,128)(2,1)S(1)} %get-tuple-element.175.q3), channel_id=1, source_target_pairs={{0,1},{1,0},{2,3},{3,2},{4,5},{5,4},{6,7},{7,6},{8,9},{9,8},{10,11... | collective-permute-start | bytes 49160 | tf_op jit(solution)/shard_map/ppermute | solution.py:410
  36.8 8.2 %collective-permute-start.12 = (bf16[32,256]{1,0:T(8,128)(2,1)S(1)}, bf16[32,256]{1,0:T(8,128)(2,1)S(1)}, u32[]{:S(2)}, u32[]{:S(2)}) collective-permute-start(bf16[32,256]{1,0:T(8,128)(2,1)S(1)} %get-tuple-element.180), channel_id=1, source_target_pairs={{32,64},{96,128},{160,192},{224,0},{64,32},{128,96},{192,160},{0,2... | collective-permute-start | bytes 49160 | tf_op jit(solution)/shard_map/ppermute | solution.py:407
  39.4 5.6 %collective-permute-start.13 = (bf16[32,256]{1,0:T(8,128)(2,1)S(1)}, bf16[32,256]{1,0:T(8,128)(2,1)S(1)}, u32[]{:S(2)}, u32[]{:S(2)}) collective-permute-start(bf16[32,256]{1,0:T(8,128)(2,1)S(1)} %get-tuple-element.181), channel_id=1, source_target_pairs={{0,32},{32,0},{64,96},{96,64},{128,160},{160,128},{192,224},{224,1... | collective-permute-start | bytes 49160 | tf_op jit(solution)/shard_map/ppermute | solution.py:408
  39.8 5.3 %collective-permute-start.14 = (bf16[32,256]{1,0:T(8,128)(2,1)S(1)}, bf16[32,256]{1,0:T(8,128)(2,1)S(1)}, u32[]{:S(2)}, u32[]{:S(2)}) collective-permute-start(bf16[32,256]{1,0:T(8,128)(2,1)S(1)} %get-tuple-element.182), channel_id=1, source_target_pairs={{1,2},{3,4},{5,6},{7,8},{9,10},{11,12},{13,14},{15,16},{17,18},{19... | collective-permute-start | bytes 49160 | tf_op jit(solution)/shard_map/ppermute | solution.py:409
  40.2 4.9 %collective-permute-start.15 = (bf16[32,256]{1,0:T(8,128)(2,1)S(1)}, bf16[32,256]{1,0:T(8,128)(2,1)S(1)}, u32[]{:S(2)}, u32[]{:S(2)}) collective-permute-start(bf16[32,256]{1,0:T(8,128)(2,1)S(1)} %get-tuple-element.183), channel_id=1, source_target_pairs={{0,1},{1,0},{2,3},{3,2},{4,5},{5,4},{6,7},{7,6},{8,9},{9,8},{10,11... | collective-permute-start | bytes 49160 | tf_op jit(solution)/shard_map/ppermute | solution.py:410
  47.3 8.6 %collective-permute-start.16 = (bf16[32,256]{1,0:T(8,128)(2,1)S(1)}, bf16[32,256]{1,0:T(8,128)(2,1)S(1)}, u32[]{:S(2)}, u32[]{:S(2)}) collective-permute-start(bf16[32,256]{1,0:T(8,128)(2,1)S(1)} %get-tuple-element.191), channel_id=1, source_target_pairs={{32,64},{96,128},{160,192},{224,0},{64,32},{128,96},{192,160},{0,2... | collective-permute-start | bytes 49160 | tf_op jit(solution)/shard_map/ppermute | solution.py:407
  52.2 4.1 %collective-permute-start.17 = (bf16[32,256]{1,0:T(8,128)(2,1)S(1)}, bf16[32,256]{1,0:T(8,128)(2,1)S(1)}, u32[]{:S(2)}, u32[]{:S(2)}) collective-permute-start(bf16[32,256]{1,0:T(8,128)(2,1)S(1)} %get-tuple-element.192), channel_id=1, source_target_pairs={{0,32},{32,0},{64,96},{96,64},{128,160},{160,128},{192,224},{224,1... | collective-permute-start | bytes 49160 | tf_op jit(solution)/shard_map/ppermute | solution.py:408
  52.2 4.1 %collective-permute-start.18 = (bf16[32,256]{1,0:T(8,128)(2,1)S(1)}, bf16[32,256]{1,0:T(8,128)(2,1)S(1)}, u32[]{:S(2)}, u32[]{:S(2)}) collective-permute-start(bf16[32,256]{1,0:T(8,128)(2,1)S(1)} %get-tuple-element.193), channel_id=1, source_target_pairs={{1,2},{3,4},{5,6},{7,8},{9,10},{11,12},{13,14},{15,16},{17,18},{19... | collective-permute-start | bytes 49160 | tf_op jit(solution)/shard_map/ppermute | solution.py:409
  52.2 4.3 %collective-permute-start.19 = (bf16[32,256]{1,0:T(8,128)(2,1)S(1)}, bf16[32,256]{1,0:T(8,128)(2,1)S(1)}, u32[]{:S(2)}, u32[]{:S(2)}) collective-permute-start(bf16[32,256]{1,0:T(8,128)(2,1)S(1)} %get-tuple-element.194), channel_id=1, source_target_pairs={{0,1},{1,0},{2,3},{3,2},{4,5},{5,4},{6,7},{7,6},{8,9},{9,8},{10,11... | collective-permute-start | bytes 49160 | tf_op jit(solution)/shard_map/ppermute | solution.py:410
  57.8 8.7 %collective-permute-start.20 = (bf16[32,256]{1,0:T(8,128)(2,1)S(1)}, bf16[32,256]{1,0:T(8,128)(2,1)S(1)}, u32[]{:S(2)}, u32[]{:S(2)}) collective-permute-start(bf16[32,256]{1,0:T(8,128)(2,1)S(1)} %get-tuple-element.202), channel_id=1, source_target_pairs={{32,64},{96,128},{160,192},{224,0},{64,32},{128,96},{192,160},{0,2... | collective-permute-start | bytes 49160 | tf_op jit(solution)/shard_map/ppermute | solution.py:407
  61.5 5.1 %collective-permute-start.21 = (bf16[32,256]{1,0:T(8,128)(2,1)S(1)}, bf16[32,256]{1,0:T(8,128)(2,1)S(1)}, u32[]{:S(2)}, u32[]{:S(2)}) collective-permute-start(bf16[32,256]{1,0:T(8,128)(2,1)S(1)} %get-tuple-element.203), channel_id=1, source_target_pairs={{0,32},{32,0},{64,96},{96,64},{128,160},{160,128},{192,224},{224,1... | collective-permute-start | bytes 49160 | tf_op jit(solution)/shard_map/ppermute | solution.py:408
  61.5 5.1 %collective-permute-start.22 = (bf16[32,256]{1,0:T(8,128)(2,1)S(1)}, bf16[32,256]{1,0:T(8,128)(2,1)S(1)}, u32[]{:S(2)}, u32[]{:S(2)}) collective-permute-start(bf16[32,256]{1,0:T(8,128)(2,1)S(1)} %get-tuple-element.204), channel_id=1, source_target_pairs={{1,2},{3,4},{5,6},{7,8},{9,10},{11,12},{13,14},{15,16},{17,18},{19... | collective-permute-start | bytes 49160 | tf_op jit(solution)/shard_map/ppermute | solution.py:409
  61.5 5.6 %collective-permute-start.23 = (bf16[32,256]{1,0:T(8,128)(2,1)S(1)}, bf16[32,256]{1,0:T(8,128)(2,1)S(1)}, u32[]{:S(2)}, u32[]{:S(2)}) collective-permute-start(bf16[32,256]{1,0:T(8,128)(2,1)S(1)} %get-tuple-element.205), channel_id=1, source_target_pairs={{0,1},{1,0},{2,3},{3,2},{4,5},{5,4},{6,7},{7,6},{8,9},{9,8},{10,11... | collective-permute-start | bytes 49160 | tf_op jit(solution)/shard_map/ppermute | solution.py:410
  68.4 11.1 %collective-permute-start.24 = (bf16[32,256]{1,0:T(8,128)(2,1)S(1)}, bf16[32,256]{1,0:T(8,128)(2,1)S(1)}, u32[]{:S(2)}, u32[]{:S(2)}) collective-permute-start(bf16[32,256]{1,0:T(8,128)(2,1)S(1)} %get-tuple-element.213), channel_id=1, source_target_pairs={{32,64},{96,128},{160,192},{224,0},{64,32},{128,96},{192,160},{0,2... | collective-permute-start | bytes 49160 | tf_op jit(solution)/shard_map/ppermute | solution.py:407
  71.5 8.0 %collective-permute-start.25 = (bf16[32,256]{1,0:T(8,128)(2,1)S(1)}, bf16[32,256]{1,0:T(8,128)(2,1)S(1)}, u32[]{:S(2)}, u32[]{:S(2)}) collective-permute-start(bf16[32,256]{1,0:T(8,128)(2,1)S(1)} %get-tuple-element.214), channel_id=1, source_target_pairs={{0,32},{32,0},{64,96},{96,64},{128,160},{160,128},{192,224},{224,1... | collective-permute-start | bytes 49160 | tf_op jit(solution)/shard_map/ppermute | solution.py:408
  71.9 7.6 %collective-permute-start.26 = (bf16[32,256]{1,0:T(8,128)(2,1)S(1)}, bf16[32,256]{1,0:T(8,128)(2,1)S(1)}, u32[]{:S(2)}, u32[]{:S(2)}) collective-permute-start(bf16[32,256]{1,0:T(8,128)(2,1)S(1)} %get-tuple-element.215), channel_id=1, source_target_pairs={{1,2},{3,4},{5,6},{7,8},{9,10},{11,12},{13,14},{15,16},{17,18},{19... | collective-permute-start | bytes 49160 | tf_op jit(solution)/shard_map/ppermute | solution.py:409
  71.9 7.6 %collective-permute-start.27 = (bf16[32,256]{1,0:T(8,128)(2,1)S(1)}, bf16[32,256]{1,0:T(8,128)(2,1)S(1)}, u32[]{:S(2)}, u32[]{:S(2)}) collective-permute-start(bf16[32,256]{1,0:T(8,128)(2,1)S(1)} %get-tuple-element.216), channel_id=1, source_target_pairs={{0,1},{1,0},{2,3},{3,2},{4,5},{5,4},{6,7},{7,6},{8,9},{9,8},{10,11... | collective-permute-start | bytes 49160 | tf_op jit(solution)/shard_map/ppermute | solution.py:410
  81.4 4.3 %collective-permute-start.28 = (bf16[1024,256]{1,0:T(8,128)(2,1)S(1)}, bf16[1024,256]{1,0:T(8,128)(2,1)S(1)}, u32[]{:S(2)}, u32[]{:S(2)}) collective-permute-start(bf16[1024,256]{1,0:T(8,128)(2,1)S(1)} %slice_bitcast_fusion), channel_id=1, source_target_pairs={{0,1},{1,0},{2,3},{3,2},{4,5},{5,4},{6,7},{7,6},{8,9},{9,8},{10,11... | collective-permute-start | bytes 1572872 | tf_op jit(solution)/shard_map/ppermute | solution.py:416
  103.5 14.6 %all-to-all-start.1 = ((bf16[8,64,256]{2,1,0:T(8,128)(2,1)}), bf16[8,64,256]{2,1,0:T(8,128)(2,1)S(1)}, u32[]{:S(2)}, u32[]{:S(2)}) async-start(bf16[8,64,256]{2,1,0:T(8,128)(2,1)} %broadcast_in_dim.4), calls=%async_computation.1 | async-start | bytes 524288 | tf_op jit(solution)/shard_map/all_to_all | solution.py:421
  108.8 6.9 %collective-permute-start.29 = (bf16[32,256]{1,0:T(8,128)(2,1)S(1)}, bf16[32,256]{1,0:T(8,128)(2,1)S(1)}, u32[]{:S(2)}, u32[]{:S(2)}) collective-permute-start(bf16[32,256]{1,0:T(8,128)(2,1)S(1)} %get-tuple-element.251), channel_id=1, source_target_pairs={{32,64},{96,128},{160,192},{224,0},{64,32},{128,96},{192,160},{0,2... | collective-permute-start | bytes 49160 | tf_op jit(solution)/shard_map/ppermute | solution.py:407
  109.7 5.9 %collective-permute-start.30 = (bf16[32,256]{1,0:T(8,128)(2,1)S(1)}, bf16[32,256]{1,0:T(8,128)(2,1)S(1)}, u32[]{:S(2)}, u32[]{:S(2)}) collective-permute-start(bf16[32,256]{1,0:T(8,128)(2,1)S(1)} %get-tuple-element.252), channel_id=1, source_target_pairs={{0,32},{32,0},{64,96},{96,64},{128,160},{160,128},{192,224},{224,1... | collective-permute-start | bytes 49160 | tf_op jit(solution)/shard_map/ppermute | solution.py:408
  (3 other events, 9.7 us)

commit v6 on v5

--- a/solution.py
+++ b/solution.py
@@ -492,6 +492,7 @@
     )
     for layer in reversed(range(STEPS - 1)):
         h, halo, (edge_slope, hidden_sum, node_slope, hidden_node, normed, inv_dev) = saved[layer]
+        back, totals = lax.optimization_barrier((back, totals))
         gpe, qr, gpn, gu, gain_term, up, *sends = call(
             backward_kernel, back_outs + own_out + (halo_outs if layer > 0 else []),
             own, *back, spread, edge_slope, node_slope, normed, inv_dev, gain, ss, ttst, w1t, back_w, n2t,

time: 138 us -> 138 us (level)
    ppermute x1, starting transfers between devices: 2.74 us -> 4.28 us  [reduce_all(): got = lax.ppermute(payload[1], 'c', [(0, 1), (1, 0)])]
  transfers between devices with their start and end apart: 35 -> 35, of which waited for: 8 -> 5; matrix products, arithmetic and copies ran while one was open for 0% -> 0% of each run, Pallas kernels for 9% -> 9%
where the time goes in v6:
time: 138 us
  starting transfers between devices  73.8 us (53%)
  blocking collectives  31.8 us (23%)
  Pallas kernels  25.1 us (18%)
  waiting for transfers between devices  4.43 us (3%)
  between operations  1.86 us (1%)
    ppermute x8, starting transfers between devices, exchange(): lax.ppermute(parts[0], REGION, odd_pairs(regions))  28 us
    ppermute x8, starting transfers between devices, exchange(): lax.ppermute(parts[3], SLAB, even_pairs(slabs))  26.7 us
    pallas_call x22, Pallas kernels, call(): pl.pallas_call(kernel, out_shape=[jax.ShapeDtypeStruct(s, d) for s, d in...  23.2 us
    all_to_all x1, blocking collectives, reduce_all(): part = lax.all_to_all(part, PLANE, 0, 0, tiled=True)  16.8 us
    all_to_all x1, blocking collectives, reduce_all(): lax.all_to_all(part, PLANE, 0, 0, tiled=True)  15 us
    all_to_all x1, starting transfers between devices, reduce_all(): lax.all_to_all(jnp.broadcast_to(part[None], (deep,) + part.shape), 'z', 0...  4.95 us
    ppermute x1, starting transfers between devices, reduce_all(): got = lax.ppermute(payload[1], 'c', [(0, 1), (1, 0)])  4.28 us
    ppermute x8, starting transfers between devices, exchange(): lax.ppermute(parts[1], REGION, even_pairs(regions))  3.97 us
  transfers between devices with their start and end apart: 35, of which 5 were waited for; matrix products, arithmetic and copies ran while one was open for 0% of the time, Pallas kernels for 9%

profile of v6, /device:TPU:1, one launch (start us, length us, event | category | flops | bytes accessed | tf_op | source)
XLA Modules:
  0.0 138.1 jit_solution(12360726199177656325)
XLA Ops:
  1.7 6.0 %collective-permute-start = (bf16[32,256]{1,0:T(8,128)(2,1)S(1)}, bf16[32,256]{1,0:T(8,128)(2,1)S(1)}, u32[]{:S(2)}, u32[]{:S(2)}) collective-permute-start(bf16[32,256]{1,0:T(8,128)(2,1)S(1)} %get-tuple-element.161.q0), channel_id=1, source_target_pairs={{32,64},{96,128},{160,192},{224,0},{64,32},{128,96},{192,160},{0,2... | collective-permute-start | bytes 49160 | tf_op jit(solution)/shard_map/ppermute | solution.py:407
  7.7 1.2 collective-permute-start.2
  9.0 4.8 %collective-permute-start.3 = (bf16[32,256]{1,0:T(8,128)(2,1)S(1)}, bf16[32,256]{1,0:T(8,128)(2,1)S(1)}, u32[]{:S(2)}, u32[]{:S(2)}) collective-permute-start(bf16[32,256]{1,0:T(8,128)(2,1)S(1)} %get-tuple-element.164.q3), channel_id=1, source_target_pairs={{0,1},{1,0},{2,3},{3,2},{4,5},{5,4},{6,7},{7,6},{8,9},{9,8},{10,11... | collective-permute-start | bytes 49160 | tf_op jit(solution)/shard_map/ppermute | solution.py:410
  14.5 2.3 %shard_map.172 = (bf16[640,512]{1,0:T(8,128)(2,1)S(1)}, bf16[640,256]{1,0:T(8,128)(2,1)S(1)}, bf16[640,256]{1,0:T(8,128)(2,1)S(1)}, bf16[384,640]{1,0:T(8,128)(2...) custom-call(s32[1,1]{1,0:T(1,128)S(6)} %copy.29.count_in, ...), custom_call_target="tpu_custom_call" | custom-call | tf_op jit(solution)/shard_map/pallas_call | solution.py:55
  18.0 3.9 %collective-permute-start.4 = (bf16[32,256]{1,0:T(8,128)(2,1)S(1)}, bf16[32,256]{1,0:T(8,128)(2,1)S(1)}, u32[]{:S(2)}, u32[]{:S(2)}) collective-permute-start(bf16[32,256]{1,0:T(8,128)(2,1)S(1)} %get-tuple-element.185.q0), channel_id=1, source_target_pairs={{32,64},{96,128},{160,192},{224,0},{64,32},{128,96},{192,160},{0,2... | collective-permute-start | bytes 49160 | tf_op jit(solution)/shard_map/ppermute | solution.py:407
  22.0 2.0 %collective-permute-start.7 = (bf16[32,256]{1,0:T(8,128)(2,1)S(1)}, bf16[32,256]{1,0:T(8,128)(2,1)S(1)}, u32[]{:S(2)}, u32[]{:S(2)}) collective-permute-start(bf16[32,256]{1,0:T(8,128)(2,1)S(1)} %get-tuple-element.188.q3), channel_id=1, source_target_pairs={{0,1},{1,0},{2,3},{3,2},{4,5},{5,4},{6,7},{7,6},{8,9},{9,8},{10,11... | collective-permute-start | bytes 49160 | tf_op jit(solution)/shard_map/ppermute | solution.py:410
  23.9 1.5 %shard_map.174 = (bf16[128,256]{1,0:T(8,128)(2,1)S(1)}, f32[640,256]{1,0:T(8,128)S(1)}, f32[640,256]{1,0:T(8,128)S(1)}, f32[128,256]{1,0:T(8,128)S(1)}, f32[128,...) custom-call(bf16[128,256]{1,0:T(8,128)(2,1)S(1)} %get-tuple-element.160.h_ref.re, ...), custom_call_target="tpu_custom_call" | custom-call | tf_op jit(solution)/shard_map/pallas_call | solution.py:55
  27.2 2.7 %collective-permute-start.8 = (bf16[32,256]{1,0:T(8,128)(2,1)S(1)}, bf16[32,256]{1,0:T(8,128)(2,1)S(1)}, u32[]{:S(2)}, u32[]{:S(2)}) collective-permute-start(bf16[32,256]{1,0:T(8,128)(2,1)S(1)} %get-tuple-element.193.q0), channel_id=1, source_target_pairs={{32,64},{96,128},{160,192},{224,0},{64,32},{128,96},{192,160},{0,2... | collective-permute-start | bytes 49160 | tf_op jit(solution)/shard_map/ppermute | solution.py:407
  30.9 3.1 %collective-permute-start.11 = (bf16[32,256]{1,0:T(8,128)(2,1)S(1)}, bf16[32,256]{1,0:T(8,128)(2,1)S(1)}, u32[]{:S(2)}, u32[]{:S(2)}) collective-permute-start(bf16[32,256]{1,0:T(8,128)(2,1)S(1)} %get-tuple-element.196.q3), channel_id=1, source_target_pairs={{0,1},{1,0},{2,3},{3,2},{4,5},{5,4},{6,7},{7,6},{8,9},{9,8},{10,11... | collective-permute-start | bytes 49160 | tf_op jit(solution)/shard_map/ppermute | solution.py:410
  34.1 1.5 %shard_map.176 = (bf16[128,256]{1,0:T(8,128)(2,1)S(1)}, f32[640,256]{1,0:T(8,128)S(1)}, f32[640,256]{1,0:T(8,128)S(1)}, f32[128,256]{1,0:T(8,128)S(1)}, f32[128,...) custom-call(bf16[128,256]{1,0:T(8,128)(2,1)S(1)} %get-tuple-element.184.h_ref.re, ...), custom_call_target="tpu_custom_call" | custom-call | tf_op jit(solution)/shard_map/pallas_call | solution.py:55
  35.6 1.2 shard_map.177
  36.8 2.6 %collective-permute-start.12 = (bf16[32,256]{1,0:T(8,128)(2,1)S(1)}, bf16[32,256]{1,0:T(8,128)(2,1)S(1)}, u32[]{:S(2)}, u32[]{:S(2)}) collective-permute-start(bf16[32,256]{1,0:T(8,128)(2,1)S(1)} %get-tuple-element.201), channel_id=1, source_target_pairs={{32,64},{96,128},{160,192},{224,0},{64,32},{128,96},{192,160},{0,2... | collective-permute-start | bytes 49160 | tf_op jit(solution)/shard_map/ppermute | solution.py:407
  40.2 3.3 %collective-permute-start.15 = (bf16[32,256]{1,0:T(8,128)(2,1)S(1)}, bf16[32,256]{1,0:T(8,128)(2,1)S(1)}, u32[]{:S(2)}, u32[]{:S(2)}) collective-permute-start(bf16[32,256]{1,0:T(8,128)(2,1)S(1)} %get-tuple-element.204), channel_id=1, source_target_pairs={{0,1},{1,0},{2,3},{3,2},{4,5},{5,4},{6,7},{7,6},{8,9},{9,8},{10,11... | collective-permute-start | bytes 49160 | tf_op jit(solution)/shard_map/ppermute | solution.py:410
  43.5 1.5 %shard_map.178 = (bf16[128,256]{1,0:T(8,128)(2,1)S(1)}, f32[640,256]{1,0:T(8,128)S(1)}, f32[640,256]{1,0:T(8,128)S(1)}, f32[128,256]{1,0:T(8,128)S(1)}, f32[128,...) custom-call(bf16[128,256]{1,0:T(8,128)(2,1)S(1)} %get-tuple-element.192.h_ref.re, ...), custom_call_target="tpu_custom_call" | custom-call | tf_op jit(solution)/shard_map/pallas_call | solution.py:55
  45.1 2.2 %shard_map.179 = (bf16[32,256]{1,0:T(8,128)(2,1)S(1)}, bf16[32,256]{1,0:T(8,128)(2,1)S(1)}, bf16[32,256]{1,0:T(8,128)(2,1)S(1)}, bf16[32,256]{1,0:T(8,128)(2,1)S...) custom-call(bf16[128,256]{1,0:T(8,128)(2,1)S(1)} %get-tuple-element., ...), custom_call_target="tpu_custom_call" | custom-call | tf_op jit(solution)/shard_map/pallas_call | solution.py:55
  47.3 4.9 %collective-permute-start.16 = (bf16[32,256]{1,0:T(8,128)(2,1)S(1)}, bf16[32,256]{1,0:T(8,128)(2,1)S(1)}, u32[]{:S(2)}, u32[]{:S(2)}) collective-permute-start(bf16[32,256]{1,0:T(8,128)(2,1)S(1)} %get-tuple-element.212), channel_id=1, source_target_pairs={{32,64},{96,128},{160,192},{224,0},{64,32},{128,96},{192,160},{0,2... | collective-permute-start | bytes 49160 | tf_op jit(solution)/shard_map/ppermute | solution.py:407
  52.2 3.5 %collective-permute-start.19 = (bf16[32,256]{1,0:T(8,128)(2,1)S(1)}, bf16[32,256]{1,0:T(8,128)(2,1)S(1)}, u32[]{:S(2)}, u32[]{:S(2)}) collective-permute-start(bf16[32,256]{1,0:T(8,128)(2,1)S(1)} %get-tuple-element.215), channel_id=1, source_target_pairs={{0,1},{1,0},{2,3},{3,2},{4,5},{5,4},{6,7},{7,6},{8,9},{9,8},{10,11... | collective-permute-start | bytes 49160 | tf_op jit(solution)/shard_map/ppermute | solution.py:410
  56.7 1.3 shard_map.182
  58.0 3.7 %collective-permute-start.20 = (bf16[32,256]{1,0:T(8,128)(2,1)S(1)}, bf16[32,256]{1,0:T(8,128)(2,1)S(1)}, u32[]{:S(2)}, u32[]{:S(2)}) collective-permute-start(bf16[32,256]{1,0:T(8,128)(2,1)S(1)} %get-tuple-element.235), channel_id=1, source_target_pairs={{32,64},{96,128},{160,192},{224,0},{64,32},{128,96},{192,160},{0,2... | collective-permute-start | bytes 49160 | tf_op jit(solution)/shard_map/ppermute | solution.py:407
  61.7 4.6 %collective-permute-start.23 = (bf16[32,256]{1,0:T(8,128)(2,1)S(1)}, bf16[32,256]{1,0:T(8,128)(2,1)S(1)}, u32[]{:S(2)}, u32[]{:S(2)}) collective-permute-start(bf16[32,256]{1,0:T(8,128)(2,1)S(1)} %get-tuple-element.238), channel_id=1, source_target_pairs={{0,1},{1,0},{2,3},{3,2},{4,5},{5,4},{6,7},{7,6},{8,9},{9,8},{10,11... | collective-permute-start | bytes 49160 | tf_op jit(solution)/shard_map/ppermute | solution.py:410
  67.3 1.3 shard_map.185
  68.6 3.1 %collective-permute-start.24 = (bf16[32,256]{1,0:T(8,128)(2,1)S(1)}, bf16[32,256]{1,0:T(8,128)(2,1)S(1)}, u32[]{:S(2)}, u32[]{:S(2)}) collective-permute-start(bf16[32,256]{1,0:T(8,128)(2,1)S(1)} %get-tuple-element.261), channel_id=1, source_target_pairs={{32,64},{96,128},{160,192},{224,0},{64,32},{128,96},{192,160},{0,2... | collective-permute-start | bytes 49160 | tf_op jit(solution)/shard_map/ppermute | solution.py:407
  72.3 4.8 %collective-permute-start.27 = (bf16[32,256]{1,0:T(8,128)(2,1)S(1)}, bf16[32,256]{1,0:T(8,128)(2,1)S(1)}, u32[]{:S(2)}, u32[]{:S(2)}) collective-permute-start(bf16[32,256]{1,0:T(8,128)(2,1)S(1)} %get-tuple-element.264), channel_id=1, source_target_pairs={{0,1},{1,0},{2,3},{3,2},{4,5},{5,4},{6,7},{7,6},{8,9},{9,8},{10,11... | collective-permute-start | bytes 49160 | tf_op jit(solution)/shard_map/ppermute | solution.py:410
  79.9 4.3 %collective-permute-start.28 = (bf16[1024,256]{1,0:T(8,128)(2,1)S(1)}, bf16[1024,256]{1,0:T(8,128)(2,1)S(1)}, u32[]{:S(2)}, u32[]{:S(2)}) collective-permute-start(bf16[1024,256]{1,0:T(8,128)(2,1)S(1)} %slice_bitcast_fusion), channel_id=1, source_target_pairs={{0,1},{1,0},{2,3},{3,2},{4,5},{5,4},{6,7},{7,6},{8,9},{9,8},{10,11... | collective-permute-start | bytes 1572872 | tf_op jit(solution)/shard_map/ppermute | solution.py:416
  84.2 1.5 %collective-permute-done.28 = bf16[1024,256]{1,0:T(8,128)(2,1)S(1)} collective-permute-done((bf16[1024,256]{1,0:T(8,128)(2,1)S(1)}, bf16[1024,256]{1,0:T(8,128)(2,1)S(1)}, u32[]{:S(2)}, u32[]{:S(2)}) %collective-permute-start.28) | collective-permute-done | bytes 524320 | tf_op jit(solution)/shard_map/ppermute | solution.py:416
  85.9 16.8 %all_to_all.15 = bf16[16,64,256]{2,1,0:T(8,128)(2,1)S(1)} all-to-all(bf16[16,64,256]{2,1,0:T(8,128)(2,1)S(1)} %bitcast.11), channel_id=1, replica_groups=mesh['x'=4,'yh'=2,'z'=8,'yl'=2,'c'=2] {'yl','yh','x'}, dimensions={0} | all-to-all | bytes 1048576 | tf_op jit(solution)/shard_map/all_to_all | solution.py:418
  103.5 4.9 %all-to-all-start.1 = ((bf16[8,64,256]{2,1,0:T(8,128)(2,1)}), bf16[8,64,256]{2,1,0:T(8,128)(2,1)S(1)}, u32[]{:S(2)}, u32[]{:S(2)}) async-start(bf16[8,64,256]{2,1,0:T(8,128)(2,1)} %broadcast_in_dim.4), calls=%async_computation.1 | async-start | bytes 524288 | tf_op jit(solution)/shard_map/all_to_all | solution.py:421
  109.7 2.1 %collective-permute-start.30 = (bf16[32,256]{1,0:T(8,128)(2,1)S(1)}, bf16[32,256]{1,0:T(8,128)(2,1)S(1)}, u32[]{:S(2)}, u32[]{:S(2)}) collective-permute-start(bf16[32,256]{1,0:T(8,128)(2,1)S(1)} %get-tuple-element.294), channel_id=1, source_target_pairs={{0,32},{32,0},{64,96},{96,64},{128,160},{160,128},{192,224},{224,1... | collective-permute-start | bytes 49160 | tf_op jit(solution)/shard_map/ppermute | solution.py:408
  111.9 2.1 %collective-permute-start.31 = (bf16[32,256]{1,0:T(8,128)(2,1)S(1)}, bf16[32,256]{1,0:T(8,128)(2,1)S(1)}, u32[]{:S(2)}, u32[]{:S(2)}) collective-permute-start(bf16[32,256]{1,0:T(8,128)(2,1)S(1)} %get-tuple-element.295), channel_id=1, source_target_pairs={{1,2},{3,4},{5,6},{7,8},{9,10},{11,12},{13,14},{15,16},{17,18},{19... | collective-permute-start | bytes 49160 | tf_op jit(solution)/shard_map/ppermute | solution.py:409
  116.7 1.4 %all-to-all-done.1 = bf16[8,64,256]{2,1,0:T(8,128)(2,1)S(1)} async-done(((bf16[8,64,256]{2,1,0:T(8,128)(2,1)}), bf16[8,64,256]{2,1,0:T(8,128)(2,1)S(1)}, u32[]{:S(2)}, u32[]{:S(2)}) %all-to-all-start.1) | async-done | bytes 262176 | tf_op jit(solution)/shard_map/all_to_all | solution.py:421
  118.2 15.0 %all_to_all.16 = bf16[16,64,256]{2,1,0:T(8,128)(2,1)S(1)} all-to-all(bf16[16,64,256]{2,1,0:T(8,128)(2,1)S(1)} %broadcast_in_dim.5), channel_id=1, replica_groups=mesh['x'=4,'yh'=2,'z'=8,'yl'=2,'c'=2] {'yl','yh','x'}, dimensions={0} | all-to-all | bytes 1048576 | tf_op jit(solution)/shard_map/all_to_all | solution.py:425
  133.1 2.2 %collective-permute-start.33 = (bf16[1024,256]{1,0:T(8,128)(2,1)S(1)}, bf16[1024,256]{1,0:T(8,128)(2,1)S(1)}, u32[]{:S(2)}, u32[]{:S(2)}) collective-permute-start(bf16[1024,256]{1,0:T(8,128)(2,1)S(1)} %bitcast.9), channel_id=1, source_target_pairs={{0,1},{1,0},{2,3},{3,2},{4,5},{5,4},{6,7},{7,6},{8,9},{9,8},{10,11... | collective-permute-start | bytes 1572872 | tf_op jit(solution)/shard_map/ppermute | solution.py:426
  (70 shorter events, 18.7 us)
Async XLA Ops:
  1.7 15.1 %collective-permute-start = (bf16[32,256]{1,0:T(8,128)(2,1)S(1)}, bf16[32,256]{1,0:T(8,128)(2,1)S(1)}, u32[]{:S(2)}, u32[]{:S(2)}) collective-permute-start(bf16[32,256]{1,0:T(8,128)(2,1)S(1)} %get-tuple-element.161.q0), channel_id=1, source_target_pairs={{32,64},{96,128},{160,192},{224,0},{64,32},{128,96},{192,160},{0,2... | collective-permute-start | bytes 49160 | tf_op jit(solution)/shard_map/ppermute | solution.py:407
  7.7 9.1 %collective-permute-start.1 = (bf16[32,256]{1,0:T(8,128)(2,1)S(1)}, bf16[32,256]{1,0:T(8,128)(2,1)S(1)}, u32[]{:S(2)}, u32[]{:S(2)}) collective-permute-start(bf16[32,256]{1,0:T(8,128)(2,1)S(1)} %get-tuple-element.162.q1), channel_id=1, source_target_pairs={{0,32},{32,0},{64,96},{96,64},{128,160},{160,128},{192,224},{224,1... | collective-permute-start | bytes 49160 | tf_op jit(solution)/shard_map/ppermute | solution.py:408
  7.7 9.1 %collective-permute-start.2 = (bf16[32,256]{1,0:T(8,128)(2,1)S(1)}, bf16[32,256]{1,0:T(8,128)(2,1)S(1)}, u32[]{:S(2)}, u32[]{:S(2)}) collective-permute-start(bf16[32,256]{1,0:T(8,128)(2,1)S(1)} %get-tuple-element.163.q2), channel_id=1, source_target_pairs={{1,2},{3,4},{5,6},{7,8},{9,10},{11,12},{13,14},{15,16},{17,18},{19... | collective-permute-start | bytes 49160 | tf_op jit(solution)/shard_map/ppermute | solution.py:409
  9.0 7.9 %collective-permute-start.3 = (bf16[32,256]{1,0:T(8,128)(2,1)S(1)}, bf16[32,256]{1,0:T(8,128)(2,1)S(1)}, u32[]{:S(2)}, u32[]{:S(2)}) collective-permute-start(bf16[32,256]{1,0:T(8,128)(2,1)S(1)} %get-tuple-element.164.q3), channel_id=1, source_target_pairs={{0,1},{1,0},{2,3},{3,2},{4,5},{5,4},{6,7},{7,6},{8,9},{9,8},{10,11... | collective-permute-start | bytes 49160 | tf_op jit(solution)/shard_map/ppermute | solution.py:410
  18.0 7.4 %collective-permute-start.4 = (bf16[32,256]{1,0:T(8,128)(2,1)S(1)}, bf16[32,256]{1,0:T(8,128)(2,1)S(1)}, u32[]{:S(2)}, u32[]{:S(2)}) collective-permute-start(bf16[32,256]{1,0:T(8,128)(2,1)S(1)} %get-tuple-element.185.q0), channel_id=1, source_target_pairs={{32,64},{96,128},{160,192},{224,0},{64,32},{128,96},{192,160},{0,2... | collective-permute-start | bytes 49160 | tf_op jit(solution)/shard_map/ppermute | solution.py:407
  22.0 4.1 %collective-permute-start.5 = (bf16[32,256]{1,0:T(8,128)(2,1)S(1)}, bf16[32,256]{1,0:T(8,128)(2,1)S(1)}, u32[]{:S(2)}, u32[]{:S(2)}) collective-permute-start(bf16[32,256]{1,0:T(8,128)(2,1)S(1)} %get-tuple-element.186.q1), channel_id=1, source_target_pairs={{0,32},{32,0},{64,96},{96,64},{128,160},{160,128},{192,224},{224,1... | collective-permute-start | bytes 49160 | tf_op jit(solution)/shard_map/ppermute | solution.py:408
  22.0 4.1 %collective-permute-start.6 = (bf16[32,256]{1,0:T(8,128)(2,1)S(1)}, bf16[32,256]{1,0:T(8,128)(2,1)S(1)}, u32[]{:S(2)}, u32[]{:S(2)}) collective-permute-start(bf16[32,256]{1,0:T(8,128)(2,1)S(1)} %get-tuple-element.187.q2), channel_id=1, source_target_pairs={{1,2},{3,4},{5,6},{7,8},{9,10},{11,12},{13,14},{15,16},{17,18},{19... | collective-permute-start | bytes 49160 | tf_op jit(solution)/shard_map/ppermute | solution.py:409
  22.0 4.1 %collective-permute-start.7 = (bf16[32,256]{1,0:T(8,128)(2,1)S(1)}, bf16[32,256]{1,0:T(8,128)(2,1)S(1)}, u32[]{:S(2)}, u32[]{:S(2)}) collective-permute-start(bf16[32,256]{1,0:T(8,128)(2,1)S(1)} %get-tuple-element.188.q3), channel_id=1, source_target_pairs={{0,1},{1,0},{2,3},{3,2},{4,5},{5,4},{6,7},{7,6},{8,9},{9,8},{10,11... | collective-permute-start | bytes 49160 | tf_op jit(solution)/shard_map/ppermute | solution.py:410
  27.2 8.3 %collective-permute-start.8 = (bf16[32,256]{1,0:T(8,128)(2,1)S(1)}, bf16[32,256]{1,0:T(8,128)(2,1)S(1)}, u32[]{:S(2)}, u32[]{:S(2)}) collective-permute-start(bf16[32,256]{1,0:T(8,128)(2,1)S(1)} %get-tuple-element.193.q0), channel_id=1, source_target_pairs={{32,64},{96,128},{160,192},{224,0},{64,32},{128,96},{192,160},{0,2... | collective-permute-start | bytes 49160 | tf_op jit(solution)/shard_map/ppermute | solution.py:407
  29.9 5.7 %collective-permute-start.9 = (bf16[32,256]{1,0:T(8,128)(2,1)S(1)}, bf16[32,256]{1,0:T(8,128)(2,1)S(1)}, u32[]{:S(2)}, u32[]{:S(2)}) collective-permute-start(bf16[32,256]{1,0:T(8,128)(2,1)S(1)} %get-tuple-element.194.q1), channel_id=1, source_target_pairs={{0,32},{32,0},{64,96},{96,64},{128,160},{160,128},{192,224},{224,1... | collective-permute-start | bytes 49160 | tf_op jit(solution)/shard_map/ppermute | solution.py:408
  30.9 4.7 %collective-permute-start.10 = (bf16[32,256]{1,0:T(8,128)(2,1)S(1)}, bf16[32,256]{1,0:T(8,128)(2,1)S(1)}, u32[]{:S(2)}, u32[]{:S(2)}) collective-permute-start(bf16[32,256]{1,0:T(8,128)(2,1)S(1)} %get-tuple-element.195.q2), channel_id=1, source_target_pairs={{1,2},{3,4},{5,6},{7,8},{9,10},{11,12},{13,14},{15,16},{17,18},{19... | collective-permute-start | bytes 49160 | tf_op jit(solution)/shard_map/ppermute | solution.py:409
  30.9 4.7 %collective-permute-start.11 = (bf16[32,256]{1,0:T(8,128)(2,1)S(1)}, bf16[32,256]{1,0:T(8,128)(2,1)S(1)}, u32[]{:S(2)}, u32[]{:S(2)}) collective-permute-start(bf16[32,256]{1,0:T(8,128)(2,1)S(1)} %get-tuple-element.196.q3), channel_id=1, source_target_pairs={{0,1},{1,0},{2,3},{3,2},{4,5},{5,4},{6,7},{7,6},{8,9},{9,8},{10,11... | collective-permute-start | bytes 49160 | tf_op jit(solution)/shard_map/ppermute | solution.py:410
  36.8 8.2 %collective-permute-start.12 = (bf16[32,256]{1,0:T(8,128)(2,1)S(1)}, bf16[32,256]{1,0:T(8,128)(2,1)S(1)}, u32[]{:S(2)}, u32[]{:S(2)}) collective-permute-start(bf16[32,256]{1,0:T(8,128)(2,1)S(1)} %get-tuple-element.201), channel_id=1, source_target_pairs={{32,64},{96,128},{160,192},{224,0},{64,32},{128,96},{192,160},{0,2... | collective-permute-start | bytes 49160 | tf_op jit(solution)/shard_map/ppermute | solution.py:407
  39.4 5.6 %collective-permute-start.13 = (bf16[32,256]{1,0:T(8,128)(2,1)S(1)}, bf16[32,256]{1,0:T(8,128)(2,1)S(1)}, u32[]{:S(2)}, u32[]{:S(2)}) collective-permute-start(bf16[32,256]{1,0:T(8,128)(2,1)S(1)} %get-tuple-element.202), channel_id=1, source_target_pairs={{0,32},{32,0},{64,96},{96,64},{128,160},{160,128},{192,224},{224,1... | collective-permute-start | bytes 49160 | tf_op jit(solution)/shard_map/ppermute | solution.py:408
  39.8 5.2 %collective-permute-start.14 = (bf16[32,256]{1,0:T(8,128)(2,1)S(1)}, bf16[32,256]{1,0:T(8,128)(2,1)S(1)}, u32[]{:S(2)}, u32[]{:S(2)}) collective-permute-start(bf16[32,256]{1,0:T(8,128)(2,1)S(1)} %get-tuple-element.203), channel_id=1, source_target_pairs={{1,2},{3,4},{5,6},{7,8},{9,10},{11,12},{13,14},{15,16},{17,18},{19... | collective-permute-start | bytes 49160 | tf_op jit(solution)/shard_map/ppermute | solution.py:409
  40.2 4.9 %collective-permute-start.15 = (bf16[32,256]{1,0:T(8,128)(2,1)S(1)}, bf16[32,256]{1,0:T(8,128)(2,1)S(1)}, u32[]{:S(2)}, u32[]{:S(2)}) collective-permute-start(bf16[32,256]{1,0:T(8,128)(2,1)S(1)} %get-tuple-element.204), channel_id=1, source_target_pairs={{0,1},{1,0},{2,3},{3,2},{4,5},{5,4},{6,7},{7,6},{8,9},{9,8},{10,11... | collective-permute-start | bytes 49160 | tf_op jit(solution)/shard_map/ppermute | solution.py:410
  47.3 9.4 %collective-permute-start.16 = (bf16[32,256]{1,0:T(8,128)(2,1)S(1)}, bf16[32,256]{1,0:T(8,128)(2,1)S(1)}, u32[]{:S(2)}, u32[]{:S(2)}) collective-permute-start(bf16[32,256]{1,0:T(8,128)(2,1)S(1)} %get-tuple-element.212), channel_id=1, source_target_pairs={{32,64},{96,128},{160,192},{224,0},{64,32},{128,96},{192,160},{0,2... | collective-permute-start | bytes 49160 | tf_op jit(solution)/shard_map/ppermute | solution.py:407
  52.2 4.5 %collective-permute-start.17 = (bf16[32,256]{1,0:T(8,128)(2,1)S(1)}, bf16[32,256]{1,0:T(8,128)(2,1)S(1)}, u32[]{:S(2)}, u32[]{:S(2)}) collective-permute-start(bf16[32,256]{1,0:T(8,128)(2,1)S(1)} %get-tuple-element.213), channel_id=1, source_target_pairs={{0,32},{32,0},{64,96},{96,64},{128,160},{160,128},{192,224},{224,1... | collective-permute-start | bytes 49160 | tf_op jit(solution)/shard_map/ppermute | solution.py:408
  52.2 4.5 %collective-permute-start.18 = (bf16[32,256]{1,0:T(8,128)(2,1)S(1)}, bf16[32,256]{1,0:T(8,128)(2,1)S(1)}, u32[]{:S(2)}, u32[]{:S(2)}) collective-permute-start(bf16[32,256]{1,0:T(8,128)(2,1)S(1)} %get-tuple-element.214), channel_id=1, source_target_pairs={{1,2},{3,4},{5,6},{7,8},{9,10},{11,12},{13,14},{15,16},{17,18},{19... | collective-permute-start | bytes 49160 | tf_op jit(solution)/shard_map/ppermute | solution.py:409
  52.2 4.5 %collective-permute-start.19 = (bf16[32,256]{1,0:T(8,128)(2,1)S(1)}, bf16[32,256]{1,0:T(8,128)(2,1)S(1)}, u32[]{:S(2)}, u32[]{:S(2)}) collective-permute-start(bf16[32,256]{1,0:T(8,128)(2,1)S(1)} %get-tuple-element.215), channel_id=1, source_target_pairs={{0,1},{1,0},{2,3},{3,2},{4,5},{5,4},{6,7},{7,6},{8,9},{9,8},{10,11... | collective-permute-start | bytes 49160 | tf_op jit(solution)/shard_map/ppermute | solution.py:410
  58.0 9.3 %collective-permute-start.20 = (bf16[32,256]{1,0:T(8,128)(2,1)S(1)}, bf16[32,256]{1,0:T(8,128)(2,1)S(1)}, u32[]{:S(2)}, u32[]{:S(2)}) collective-permute-start(bf16[32,256]{1,0:T(8,128)(2,1)S(1)} %get-tuple-element.235), channel_id=1, source_target_pairs={{32,64},{96,128},{160,192},{224,0},{64,32},{128,96},{192,160},{0,2... | collective-permute-start | bytes 49160 | tf_op jit(solution)/shard_map/ppermute | solution.py:407
  61.7 5.6 %collective-permute-start.21 = (bf16[32,256]{1,0:T(8,128)(2,1)S(1)}, bf16[32,256]{1,0:T(8,128)(2,1)S(1)}, u32[]{:S(2)}, u32[]{:S(2)}) collective-permute-start(bf16[32,256]{1,0:T(8,128)(2,1)S(1)} %get-tuple-element.236), channel_id=1, source_target_pairs={{0,32},{32,0},{64,96},{96,64},{128,160},{160,128},{192,224},{224,1... | collective-permute-start | bytes 49160 | tf_op jit(solution)/shard_map/ppermute | solution.py:408
  61.7 5.7 %collective-permute-start.22 = (bf16[32,256]{1,0:T(8,128)(2,1)S(1)}, bf16[32,256]{1,0:T(8,128)(2,1)S(1)}, u32[]{:S(2)}, u32[]{:S(2)}) collective-permute-start(bf16[32,256]{1,0:T(8,128)(2,1)S(1)} %get-tuple-element.237), channel_id=1, source_target_pairs={{1,2},{3,4},{5,6},{7,8},{9,10},{11,12},{13,14},{15,16},{17,18},{19... | collective-permute-start | bytes 49160 | tf_op jit(solution)/shard_map/ppermute | solution.py:409
  61.7 5.7 %collective-permute-start.23 = (bf16[32,256]{1,0:T(8,128)(2,1)S(1)}, bf16[32,256]{1,0:T(8,128)(2,1)S(1)}, u32[]{:S(2)}, u32[]{:S(2)}) collective-permute-start(bf16[32,256]{1,0:T(8,128)(2,1)S(1)} %get-tuple-element.238), channel_id=1, source_target_pairs={{0,1},{1,0},{2,3},{3,2},{4,5},{5,4},{6,7},{7,6},{8,9},{9,8},{10,11... | collective-permute-start | bytes 49160 | tf_op jit(solution)/shard_map/ppermute | solution.py:410
  68.6 9.4 %collective-permute-start.24 = (bf16[32,256]{1,0:T(8,128)(2,1)S(1)}, bf16[32,256]{1,0:T(8,128)(2,1)S(1)}, u32[]{:S(2)}, u32[]{:S(2)}) collective-permute-start(bf16[32,256]{1,0:T(8,128)(2,1)S(1)} %get-tuple-element.261), channel_id=1, source_target_pairs={{32,64},{96,128},{160,192},{224,0},{64,32},{128,96},{192,160},{0,2... | collective-permute-start | bytes 49160 | tf_op jit(solution)/shard_map/ppermute | solution.py:407
  71.8 6.3 %collective-permute-start.25 = (bf16[32,256]{1,0:T(8,128)(2,1)S(1)}, bf16[32,256]{1,0:T(8,128)(2,1)S(1)}, u32[]{:S(2)}, u32[]{:S(2)}) collective-permute-start(bf16[32,256]{1,0:T(8,128)(2,1)S(1)} %get-tuple-element.262), channel_id=1, source_target_pairs={{0,32},{32,0},{64,96},{96,64},{128,160},{160,128},{192,224},{224,1... | collective-permute-start | bytes 49160 | tf_op jit(solution)/shard_map/ppermute | solution.py:408
  72.3 5.8 %collective-permute-start.26 = (bf16[32,256]{1,0:T(8,128)(2,1)S(1)}, bf16[32,256]{1,0:T(8,128)(2,1)S(1)}, u32[]{:S(2)}, u32[]{:S(2)}) collective-permute-start(bf16[32,256]{1,0:T(8,128)(2,1)S(1)} %get-tuple-element.263), channel_id=1, source_target_pairs={{1,2},{3,4},{5,6},{7,8},{9,10},{11,12},{13,14},{15,16},{17,18},{19... | collective-permute-start | bytes 49160 | tf_op jit(solution)/shard_map/ppermute | solution.py:409
  72.3 5.8 %collective-permute-start.27 = (bf16[32,256]{1,0:T(8,128)(2,1)S(1)}, bf16[32,256]{1,0:T(8,128)(2,1)S(1)}, u32[]{:S(2)}, u32[]{:S(2)}) collective-permute-start(bf16[32,256]{1,0:T(8,128)(2,1)S(1)} %get-tuple-element.264), channel_id=1, source_target_pairs={{0,1},{1,0},{2,3},{3,2},{4,5},{5,4},{6,7},{7,6},{8,9},{9,8},{10,11... | collective-permute-start | bytes 49160 | tf_op jit(solution)/shard_map/ppermute | solution.py:410
  79.9 5.8 %collective-permute-start.28 = (bf16[1024,256]{1,0:T(8,128)(2,1)S(1)}, bf16[1024,256]{1,0:T(8,128)(2,1)S(1)}, u32[]{:S(2)}, u32[]{:S(2)}) collective-permute-start(bf16[1024,256]{1,0:T(8,128)(2,1)S(1)} %slice_bitcast_fusion), channel_id=1, source_target_pairs={{0,1},{1,0},{2,3},{3,2},{4,5},{5,4},{6,7},{7,6},{8,9},{9,8},{10,11... | collective-permute-start | bytes 1572872 | tf_op jit(solution)/shard_map/ppermute | solution.py:416
  103.5 14.6 %all-to-all-start.1 = ((bf16[8,64,256]{2,1,0:T(8,128)(2,1)}), bf16[8,64,256]{2,1,0:T(8,128)(2,1)S(1)}, u32[]{:S(2)}, u32[]{:S(2)}) async-start(bf16[8,64,256]{2,1,0:T(8,128)(2,1)} %broadcast_in_dim.4), calls=%async_computation.1 | async-start | bytes 524288 | tf_op jit(solution)/shard_map/all_to_all | solution.py:421
  108.8 6.9 %collective-permute-start.29 = (bf16[32,256]{1,0:T(8,128)(2,1)S(1)}, bf16[32,256]{1,0:T(8,128)(2,1)S(1)}, u32[]{:S(2)}, u32[]{:S(2)}) collective-permute-start(bf16[32,256]{1,0:T(8,128)(2,1)S(1)} %get-tuple-element.293), channel_id=1, source_target_pairs={{32,64},{96,128},{160,192},{224,0},{64,32},{128,96},{192,160},{0,2... | collective-permute-start | bytes 49160 | tf_op jit(solution)/shard_map/ppermute | solution.py:407
  109.7 5.9 %collective-permute-start.30 = (bf16[32,256]{1,0:T(8,128)(2,1)S(1)}, bf16[32,256]{1,0:T(8,128)(2,1)S(1)}, u32[]{:S(2)}, u32[]{:S(2)}) collective-permute-start(bf16[32,256]{1,0:T(8,128)(2,1)S(1)} %get-tuple-element.294), channel_id=1, source_target_pairs={{0,32},{32,0},{64,96},{96,64},{128,160},{160,128},{192,224},{224,1... | collective-permute-start | bytes 49160 | tf_op jit(solution)/shard_map/ppermute | solution.py:408
  (3 other events, 9.7 us)

commit v7 on v6

--- a/solution.py
+++ b/solution.py
@@ -229,11 +229,10 @@
     gu_o[...] = gu
     gpn_o[...] = gpn
     gh = mm(gpn, back[:, 2 * L : 3 * L]) + mm(gpn, back[:, 3 * L :])
-    high, low = split(gh)
-    pair = jnp.concatenate([high, low], axis=0)
+    gh = gh.astype(BF16)
     gpe = []
     for lo in range(0, edge_slope.shape[0], CHUNK):
-        part = (mm(ss[lo : lo + CHUNK], pair) * edge_slope[lo : lo + CHUNK]).astype(BF16)
+        part = (mm(ss[lo : lo + CHUNK, :OWN], gh) * edge_slope[lo : lo + CHUNK]).astype(BF16)
         gpe_o[lo : lo + CHUNK] = part
         gpe.append(part)
     qr = mm(ttst[...], jnp.concatenate(gpe, axis=0))
@@ -243,9 +242,7 @@
 
 
 def halo_grads(qr, w1t, sends):
-    q_high, q_low = split(qr[OWN : 2 * OWN])
-    far = w1t[:, :L]
-    ge = mm(q_high, far) + mm(q_low, far)
+    ge = mm(qr[OWN : 2 * OWN].astype(BF16), w1t[:, :L])
     for i, out in enumerate(sends):
         out[...] = ge[i * HALO : (i + 1) * HALO].astype(BF16)
 

time: 138 us -> 138 us (level)
  no operation moved by 1% of the time
where the time goes in v7:
time: 138 us
  starting transfers between devices  73.8 us (53%)
  blocking collectives  31.8 us (23%)
  Pallas kernels  25 us (18%)
  waiting for transfers between devices  4.45 us (3%)
  between operations  1.85 us (1%)
    ppermute x8, starting transfers between devices, exchange(): lax.ppermute(parts[0], REGION, odd_pairs(regions))  28.1 us
    ppermute x8, starting transfers between devices, exchange(): lax.ppermute(parts[3], SLAB, even_pairs(slabs))  26.7 us
    pallas_call x22, Pallas kernels, call(): pl.pallas_call(kernel, out_shape=[jax.ShapeDtypeStruct(s, d) for s, d in...  23.1 us
    all_to_all x1, blocking collectives, reduce_all(): part = lax.all_to_all(part, PLANE, 0, 0, tiled=True)  16.8 us
    all_to_all x1, blocking collectives, reduce_all(): lax.all_to_all(part, PLANE, 0, 0, tiled=True)  14.9 us
    all_to_all x1, starting transfers between devices, reduce_all(): lax.all_to_all(jnp.broadcast_to(part[None], (deep,) + part.shape), 'z', 0...  4.95 us
    ppermute x1, starting transfers between devices, reduce_all(): got = lax.ppermute(payload[1], 'c', [(0, 1), (1, 0)])  4.28 us
    ppermute x8, starting transfers between devices, exchange(): lax.ppermute(parts[1], REGION, even_pairs(regions))  3.87 us
  transfers between devices with their start and end apart: 35, of which 5 were waited for; matrix products, arithmetic and copies ran while one was open for 0% of the time, Pallas kernels for 9%

profile of v7, /device:TPU:1, one launch (start us, length us, event | category | flops | bytes accessed | tf_op | source)
XLA Modules:
  0.0 138.0 jit_solution(11796869722166063640)
XLA Ops:
  1.7 6.0 %collective-permute-start = (bf16[32,256]{1,0:T(8,128)(2,1)S(1)}, bf16[32,256]{1,0:T(8,128)(2,1)S(1)}, u32[]{:S(2)}, u32[]{:S(2)}) collective-permute-start(bf16[32,256]{1,0:T(8,128)(2,1)S(1)} %get-tuple-element.161.q0), channel_id=1, source_target_pairs={{32,64},{96,128},{160,192},{224,0},{64,32},{128,96},{192,160},{0,2... | collective-permute-start | bytes 49160 | tf_op jit(solution)/shard_map/ppermute | solution.py:404
  7.7 1.2 collective-permute-start.2
  9.0 4.8 %collective-permute-start.3 = (bf16[32,256]{1,0:T(8,128)(2,1)S(1)}, bf16[32,256]{1,0:T(8,128)(2,1)S(1)}, u32[]{:S(2)}, u32[]{:S(2)}) collective-permute-start(bf16[32,256]{1,0:T(8,128)(2,1)S(1)} %get-tuple-element.164.q3), channel_id=1, source_target_pairs={{0,1},{1,0},{2,3},{3,2},{4,5},{5,4},{6,7},{7,6},{8,9},{9,8},{10,11... | collective-permute-start | bytes 49160 | tf_op jit(solution)/shard_map/ppermute | solution.py:407
  14.5 2.3 %shard_map.172 = (bf16[640,512]{1,0:T(8,128)(2,1)S(1)}, bf16[640,256]{1,0:T(8,128)(2,1)S(1)}, bf16[640,256]{1,0:T(8,128)(2,1)S(1)}, bf16[384,640]{1,0:T(8,128)(2...) custom-call(s32[1,1]{1,0:T(1,128)S(6)} %copy.29.count_in, ...), custom_call_target="tpu_custom_call" | custom-call | tf_op jit(solution)/shard_map/pallas_call | solution.py:55
  18.0 3.9 %collective-permute-start.4 = (bf16[32,256]{1,0:T(8,128)(2,1)S(1)}, bf16[32,256]{1,0:T(8,128)(2,1)S(1)}, u32[]{:S(2)}, u32[]{:S(2)}) collective-permute-start(bf16[32,256]{1,0:T(8,128)(2,1)S(1)} %get-tuple-element.185.q0), channel_id=1, source_target_pairs={{32,64},{96,128},{160,192},{224,0},{64,32},{128,96},{192,160},{0,2... | collective-permute-start | bytes 49160 | tf_op jit(solution)/shard_map/ppermute | solution.py:404
  22.0 2.0 %collective-permute-start.7 = (bf16[32,256]{1,0:T(8,128)(2,1)S(1)}, bf16[32,256]{1,0:T(8,128)(2,1)S(1)}, u32[]{:S(2)}, u32[]{:S(2)}) collective-permute-start(bf16[32,256]{1,0:T(8,128)(2,1)S(1)} %get-tuple-element.188.q3), channel_id=1, source_target_pairs={{0,1},{1,0},{2,3},{3,2},{4,5},{5,4},{6,7},{7,6},{8,9},{9,8},{10,11... | collective-permute-start | bytes 49160 | tf_op jit(solution)/shard_map/ppermute | solution.py:407
  23.9 1.5 %shard_map.174 = (bf16[128,256]{1,0:T(8,128)(2,1)S(1)}, f32[640,256]{1,0:T(8,128)S(1)}, f32[640,256]{1,0:T(8,128)S(1)}, f32[128,256]{1,0:T(8,128)S(1)}, f32[128,...) custom-call(bf16[128,256]{1,0:T(8,128)(2,1)S(1)} %get-tuple-element.160.h_ref.re, ...), custom_call_target="tpu_custom_call" | custom-call | tf_op jit(solution)/shard_map/pallas_call | solution.py:55
  27.2 2.7 %collective-permute-start.8 = (bf16[32,256]{1,0:T(8,128)(2,1)S(1)}, bf16[32,256]{1,0:T(8,128)(2,1)S(1)}, u32[]{:S(2)}, u32[]{:S(2)}) collective-permute-start(bf16[32,256]{1,0:T(8,128)(2,1)S(1)} %get-tuple-element.193.q0), channel_id=1, source_target_pairs={{32,64},{96,128},{160,192},{224,0},{64,32},{128,96},{192,160},{0,2... | collective-permute-start | bytes 49160 | tf_op jit(solution)/shard_map/ppermute | solution.py:404
  30.9 3.1 %collective-permute-start.11 = (bf16[32,256]{1,0:T(8,128)(2,1)S(1)}, bf16[32,256]{1,0:T(8,128)(2,1)S(1)}, u32[]{:S(2)}, u32[]{:S(2)}) collective-permute-start(bf16[32,256]{1,0:T(8,128)(2,1)S(1)} %get-tuple-element.196.q3), channel_id=1, source_target_pairs={{0,1},{1,0},{2,3},{3,2},{4,5},{5,4},{6,7},{7,6},{8,9},{9,8},{10,11... | collective-permute-start | bytes 49160 | tf_op jit(solution)/shard_map/ppermute | solution.py:407
  34.1 1.5 %shard_map.176 = (bf16[128,256]{1,0:T(8,128)(2,1)S(1)}, f32[640,256]{1,0:T(8,128)S(1)}, f32[640,256]{1,0:T(8,128)S(1)}, f32[128,256]{1,0:T(8,128)S(1)}, f32[128,...) custom-call(bf16[128,256]{1,0:T(8,128)(2,1)S(1)} %get-tuple-element.184.h_ref.re, ...), custom_call_target="tpu_custom_call" | custom-call | tf_op jit(solution)/shard_map/pallas_call | solution.py:55
  35.6 1.2 shard_map.177
  36.8 2.6 %collective-permute-start.12 = (bf16[32,256]{1,0:T(8,128)(2,1)S(1)}, bf16[32,256]{1,0:T(8,128)(2,1)S(1)}, u32[]{:S(2)}, u32[]{:S(2)}) collective-permute-start(bf16[32,256]{1,0:T(8,128)(2,1)S(1)} %get-tuple-element.201), channel_id=1, source_target_pairs={{32,64},{96,128},{160,192},{224,0},{64,32},{128,96},{192,160},{0,2... | collective-permute-start | bytes 49160 | tf_op jit(solution)/shard_map/ppermute | solution.py:404
  40.2 3.3 %collective-permute-start.15 = (bf16[32,256]{1,0:T(8,128)(2,1)S(1)}, bf16[32,256]{1,0:T(8,128)(2,1)S(1)}, u32[]{:S(2)}, u32[]{:S(2)}) collective-permute-start(bf16[32,256]{1,0:T(8,128)(2,1)S(1)} %get-tuple-element.204), channel_id=1, source_target_pairs={{0,1},{1,0},{2,3},{3,2},{4,5},{5,4},{6,7},{7,6},{8,9},{9,8},{10,11... | collective-permute-start | bytes 49160 | tf_op jit(solution)/shard_map/ppermute | solution.py:407
  43.5 1.5 %shard_map.178 = (bf16[128,256]{1,0:T(8,128)(2,1)S(1)}, f32[640,256]{1,0:T(8,128)S(1)}, f32[640,256]{1,0:T(8,128)S(1)}, f32[128,256]{1,0:T(8,128)S(1)}, f32[128,...) custom-call(bf16[128,256]{1,0:T(8,128)(2,1)S(1)} %get-tuple-element.192.h_ref.re, ...), custom_call_target="tpu_custom_call" | custom-call | tf_op jit(solution)/shard_map/pallas_call | solution.py:55
  45.1 2.2 %shard_map.179 = (bf16[32,256]{1,0:T(8,128)(2,1)S(1)}, bf16[32,256]{1,0:T(8,128)(2,1)S(1)}, bf16[32,256]{1,0:T(8,128)(2,1)S(1)}, bf16[32,256]{1,0:T(8,128)(2,1)S...) custom-call(bf16[128,256]{1,0:T(8,128)(2,1)S(1)} %get-tuple-element., ...), custom_call_target="tpu_custom_call" | custom-call | tf_op jit(solution)/shard_map/pallas_call | solution.py:55
  47.3 4.9 %collective-permute-start.16 = (bf16[32,256]{1,0:T(8,128)(2,1)S(1)}, bf16[32,256]{1,0:T(8,128)(2,1)S(1)}, u32[]{:S(2)}, u32[]{:S(2)}) collective-permute-start(bf16[32,256]{1,0:T(8,128)(2,1)S(1)} %get-tuple-element.212), channel_id=1, source_target_pairs={{32,64},{96,128},{160,192},{224,0},{64,32},{128,96},{192,160},{0,2... | collective-permute-start | bytes 49160 | tf_op jit(solution)/shard_map/ppermute | solution.py:404
  52.2 3.5 %collective-permute-start.19 = (bf16[32,256]{1,0:T(8,128)(2,1)S(1)}, bf16[32,256]{1,0:T(8,128)(2,1)S(1)}, u32[]{:S(2)}, u32[]{:S(2)}) collective-permute-start(bf16[32,256]{1,0:T(8,128)(2,1)S(1)} %get-tuple-element.215), channel_id=1, source_target_pairs={{0,1},{1,0},{2,3},{3,2},{4,5},{5,4},{6,7},{7,6},{8,9},{9,8},{10,11... | collective-permute-start | bytes 49160 | tf_op jit(solution)/shard_map/ppermute | solution.py:407
  56.7 1.2 shard_map.182
  57.9 3.7 %collective-permute-start.20 = (bf16[32,256]{1,0:T(8,128)(2,1)S(1)}, bf16[32,256]{1,0:T(8,128)(2,1)S(1)}, u32[]{:S(2)}, u32[]{:S(2)}) collective-permute-start(bf16[32,256]{1,0:T(8,128)(2,1)S(1)} %get-tuple-element.235), channel_id=1, source_target_pairs={{32,64},{96,128},{160,192},{224,0},{64,32},{128,96},{192,160},{0,2... | collective-permute-start | bytes 49160 | tf_op jit(solution)/shard_map/ppermute | solution.py:404
  61.6 4.6 %collective-permute-start.23 = (bf16[32,256]{1,0:T(8,128)(2,1)S(1)}, bf16[32,256]{1,0:T(8,128)(2,1)S(1)}, u32[]{:S(2)}, u32[]{:S(2)}) collective-permute-start(bf16[32,256]{1,0:T(8,128)(2,1)S(1)} %get-tuple-element.238), channel_id=1, source_target_pairs={{0,1},{1,0},{2,3},{3,2},{4,5},{5,4},{6,7},{7,6},{8,9},{9,8},{10,11... | collective-permute-start | bytes 49160 | tf_op jit(solution)/shard_map/ppermute | solution.py:407
  67.2 1.2 shard_map.185
  68.5 3.2 %collective-permute-start.24 = (bf16[32,256]{1,0:T(8,128)(2,1)S(1)}, bf16[32,256]{1,0:T(8,128)(2,1)S(1)}, u32[]{:S(2)}, u32[]{:S(2)}) collective-permute-start(bf16[32,256]{1,0:T(8,128)(2,1)S(1)} %get-tuple-element.261), channel_id=1, source_target_pairs={{32,64},{96,128},{160,192},{224,0},{64,32},{128,96},{192,160},{0,2... | collective-permute-start | bytes 49160 | tf_op jit(solution)/shard_map/ppermute | solution.py:404
  72.1 4.8 %collective-permute-start.27 = (bf16[32,256]{1,0:T(8,128)(2,1)S(1)}, bf16[32,256]{1,0:T(8,128)(2,1)S(1)}, u32[]{:S(2)}, u32[]{:S(2)}) collective-permute-start(bf16[32,256]{1,0:T(8,128)(2,1)S(1)} %get-tuple-element.264), channel_id=1, source_target_pairs={{0,1},{1,0},{2,3},{3,2},{4,5},{5,4},{6,7},{7,6},{8,9},{9,8},{10,11... | collective-permute-start | bytes 49160 | tf_op jit(solution)/shard_map/ppermute | solution.py:407
  79.8 4.3 %collective-permute-start.28 = (bf16[1024,256]{1,0:T(8,128)(2,1)S(1)}, bf16[1024,256]{1,0:T(8,128)(2,1)S(1)}, u32[]{:S(2)}, u32[]{:S(2)}) collective-permute-start(bf16[1024,256]{1,0:T(8,128)(2,1)S(1)} %slice_bitcast_fusion), channel_id=1, source_target_pairs={{0,1},{1,0},{2,3},{3,2},{4,5},{5,4},{6,7},{7,6},{8,9},{9,8},{10,11... | collective-permute-start | bytes 1572872 | tf_op jit(solution)/shard_map/ppermute | solution.py:413
  84.1 1.5 %collective-permute-done.28 = bf16[1024,256]{1,0:T(8,128)(2,1)S(1)} collective-permute-done((bf16[1024,256]{1,0:T(8,128)(2,1)S(1)}, bf16[1024,256]{1,0:T(8,128)(2,1)S(1)}, u32[]{:S(2)}, u32[]{:S(2)}) %collective-permute-start.28) | collective-permute-done | bytes 524320 | tf_op jit(solution)/shard_map/ppermute | solution.py:413
  85.8 16.8 %all_to_all.15 = bf16[16,64,256]{2,1,0:T(8,128)(2,1)S(1)} all-to-all(bf16[16,64,256]{2,1,0:T(8,128)(2,1)S(1)} %bitcast.11), channel_id=1, replica_groups=mesh['x'=4,'yh'=2,'z'=8,'yl'=2,'c'=2] {'yl','yh','x'}, dimensions={0} | all-to-all | bytes 1048576 | tf_op jit(solution)/shard_map/all_to_all | solution.py:415
  103.4 5.0 %all-to-all-start.1 = ((bf16[8,64,256]{2,1,0:T(8,128)(2,1)}), bf16[8,64,256]{2,1,0:T(8,128)(2,1)S(1)}, u32[]{:S(2)}, u32[]{:S(2)}) async-start(bf16[8,64,256]{2,1,0:T(8,128)(2,1)} %broadcast_in_dim.4), calls=%async_computation.1 | async-start | bytes 524288 | tf_op jit(solution)/shard_map/all_to_all | solution.py:418
  109.6 2.1 %collective-permute-start.30 = (bf16[32,256]{1,0:T(8,128)(2,1)S(1)}, bf16[32,256]{1,0:T(8,128)(2,1)S(1)}, u32[]{:S(2)}, u32[]{:S(2)}) collective-permute-start(bf16[32,256]{1,0:T(8,128)(2,1)S(1)} %get-tuple-element.294), channel_id=1, source_target_pairs={{0,32},{32,0},{64,96},{96,64},{128,160},{160,128},{192,224},{224,1... | collective-permute-start | bytes 49160 | tf_op jit(solution)/shard_map/ppermute | solution.py:405
  111.7 2.1 %collective-permute-start.31 = (bf16[32,256]{1,0:T(8,128)(2,1)S(1)}, bf16[32,256]{1,0:T(8,128)(2,1)S(1)}, u32[]{:S(2)}, u32[]{:S(2)}) collective-permute-start(bf16[32,256]{1,0:T(8,128)(2,1)S(1)} %get-tuple-element.295), channel_id=1, source_target_pairs={{1,2},{3,4},{5,6},{7,8},{9,10},{11,12},{13,14},{15,16},{17,18},{19... | collective-permute-start | bytes 49160 | tf_op jit(solution)/shard_map/ppermute | solution.py:406
  116.6 1.4 %all-to-all-done.1 = bf16[8,64,256]{2,1,0:T(8,128)(2,1)S(1)} async-done(((bf16[8,64,256]{2,1,0:T(8,128)(2,1)}), bf16[8,64,256]{2,1,0:T(8,128)(2,1)S(1)}, u32[]{:S(2)}, u32[]{:S(2)}) %all-to-all-start.1) | async-done | bytes 262176 | tf_op jit(solution)/shard_map/all_to_all | solution.py:418
  118.1 14.9 %all_to_all.16 = bf16[16,64,256]{2,1,0:T(8,128)(2,1)S(1)} all-to-all(bf16[16,64,256]{2,1,0:T(8,128)(2,1)S(1)} %broadcast_in_dim.5), channel_id=1, replica_groups=mesh['x'=4,'yh'=2,'z'=8,'yl'=2,'c'=2] {'yl','yh','x'}, dimensions={0} | all-to-all | bytes 1048576 | tf_op jit(solution)/shard_map/all_to_all | solution.py:422
  133.0 2.2 %collective-permute-start.33 = (bf16[1024,256]{1,0:T(8,128)(2,1)S(1)}, bf16[1024,256]{1,0:T(8,128)(2,1)S(1)}, u32[]{:S(2)}, u32[]{:S(2)}) collective-permute-start(bf16[1024,256]{1,0:T(8,128)(2,1)S(1)} %bitcast.9), channel_id=1, source_target_pairs={{0,1},{1,0},{2,3},{3,2},{4,5},{5,4},{6,7},{7,6},{8,9},{9,8},{10,11... | collective-permute-start | bytes 1572872 | tf_op jit(solution)/shard_map/ppermute | solution.py:423
  (70 shorter events, 18.6 us)
Async XLA Ops:
  1.7 15.1 %collective-permute-start = (bf16[32,256]{1,0:T(8,128)(2,1)S(1)}, bf16[32,256]{1,0:T(8,128)(2,1)S(1)}, u32[]{:S(2)}, u32[]{:S(2)}) collective-permute-start(bf16[32,256]{1,0:T(8,128)(2,1)S(1)} %get-tuple-element.161.q0), channel_id=1, source_target_pairs={{32,64},{96,128},{160,192},{224,0},{64,32},{128,96},{192,160},{0,2... | collective-permute-start | bytes 49160 | tf_op jit(solution)/shard_map/ppermute | solution.py:404
  7.7 9.1 %collective-permute-start.1 = (bf16[32,256]{1,0:T(8,128)(2,1)S(1)}, bf16[32,256]{1,0:T(8,128)(2,1)S(1)}, u32[]{:S(2)}, u32[]{:S(2)}) collective-permute-start(bf16[32,256]{1,0:T(8,128)(2,1)S(1)} %get-tuple-element.162.q1), channel_id=1, source_target_pairs={{0,32},{32,0},{64,96},{96,64},{128,160},{160,128},{192,224},{224,1... | collective-permute-start | bytes 49160 | tf_op jit(solution)/shard_map/ppermute | solution.py:405
  7.7 9.1 %collective-permute-start.2 = (bf16[32,256]{1,0:T(8,128)(2,1)S(1)}, bf16[32,256]{1,0:T(8,128)(2,1)S(1)}, u32[]{:S(2)}, u32[]{:S(2)}) collective-permute-start(bf16[32,256]{1,0:T(8,128)(2,1)S(1)} %get-tuple-element.163.q2), channel_id=1, source_target_pairs={{1,2},{3,4},{5,6},{7,8},{9,10},{11,12},{13,14},{15,16},{17,18},{19... | collective-permute-start | bytes 49160 | tf_op jit(solution)/shard_map/ppermute | solution.py:406
  9.0 7.9 %collective-permute-start.3 = (bf16[32,256]{1,0:T(8,128)(2,1)S(1)}, bf16[32,256]{1,0:T(8,128)(2,1)S(1)}, u32[]{:S(2)}, u32[]{:S(2)}) collective-permute-start(bf16[32,256]{1,0:T(8,128)(2,1)S(1)} %get-tuple-element.164.q3), channel_id=1, source_target_pairs={{0,1},{1,0},{2,3},{3,2},{4,5},{5,4},{6,7},{7,6},{8,9},{9,8},{10,11... | collective-permute-start | bytes 49160 | tf_op jit(solution)/shard_map/ppermute | solution.py:407
  18.0 7.4 %collective-permute-start.4 = (bf16[32,256]{1,0:T(8,128)(2,1)S(1)}, bf16[32,256]{1,0:T(8,128)(2,1)S(1)}, u32[]{:S(2)}, u32[]{:S(2)}) collective-permute-start(bf16[32,256]{1,0:T(8,128)(2,1)S(1)} %get-tuple-element.185.q0), channel_id=1, source_target_pairs={{32,64},{96,128},{160,192},{224,0},{64,32},{128,96},{192,160},{0,2... | collective-permute-start | bytes 49160 | tf_op jit(solution)/shard_map/ppermute | solution.py:404
  22.0 4.1 %collective-permute-start.5 = (bf16[32,256]{1,0:T(8,128)(2,1)S(1)}, bf16[32,256]{1,0:T(8,128)(2,1)S(1)}, u32[]{:S(2)}, u32[]{:S(2)}) collective-permute-start(bf16[32,256]{1,0:T(8,128)(2,1)S(1)} %get-tuple-element.186.q1), channel_id=1, source_target_pairs={{0,32},{32,0},{64,96},{96,64},{128,160},{160,128},{192,224},{224,1... | collective-permute-start | bytes 49160 | tf_op jit(solution)/shard_map/ppermute | solution.py:405
  22.0 4.1 %collective-permute-start.6 = (bf16[32,256]{1,0:T(8,128)(2,1)S(1)}, bf16[32,256]{1,0:T(8,128)(2,1)S(1)}, u32[]{:S(2)}, u32[]{:S(2)}) collective-permute-start(bf16[32,256]{1,0:T(8,128)(2,1)S(1)} %get-tuple-element.187.q2), channel_id=1, source_target_pairs={{1,2},{3,4},{5,6},{7,8},{9,10},{11,12},{13,14},{15,16},{17,18},{19... | collective-permute-start | bytes 49160 | tf_op jit(solution)/shard_map/ppermute | solution.py:406
  22.0 4.1 %collective-permute-start.7 = (bf16[32,256]{1,0:T(8,128)(2,1)S(1)}, bf16[32,256]{1,0:T(8,128)(2,1)S(1)}, u32[]{:S(2)}, u32[]{:S(2)}) collective-permute-start(bf16[32,256]{1,0:T(8,128)(2,1)S(1)} %get-tuple-element.188.q3), channel_id=1, source_target_pairs={{0,1},{1,0},{2,3},{3,2},{4,5},{5,4},{6,7},{7,6},{8,9},{9,8},{10,11... | collective-permute-start | bytes 49160 | tf_op jit(solution)/shard_map/ppermute | solution.py:407
  27.2 8.3 %collective-permute-start.8 = (bf16[32,256]{1,0:T(8,128)(2,1)S(1)}, bf16[32,256]{1,0:T(8,128)(2,1)S(1)}, u32[]{:S(2)}, u32[]{:S(2)}) collective-permute-start(bf16[32,256]{1,0:T(8,128)(2,1)S(1)} %get-tuple-element.193.q0), channel_id=1, source_target_pairs={{32,64},{96,128},{160,192},{224,0},{64,32},{128,96},{192,160},{0,2... | collective-permute-start | bytes 49160 | tf_op jit(solution)/shard_map/ppermute | solution.py:404
  29.9 5.7 %collective-permute-start.9 = (bf16[32,256]{1,0:T(8,128)(2,1)S(1)}, bf16[32,256]{1,0:T(8,128)(2,1)S(1)}, u32[]{:S(2)}, u32[]{:S(2)}) collective-permute-start(bf16[32,256]{1,0:T(8,128)(2,1)S(1)} %get-tuple-element.194.q1), channel_id=1, source_target_pairs={{0,32},{32,0},{64,96},{96,64},{128,160},{160,128},{192,224},{224,1... | collective-permute-start | bytes 49160 | tf_op jit(solution)/shard_map/ppermute | solution.py:405
  30.9 4.7 %collective-permute-start.10 = (bf16[32,256]{1,0:T(8,128)(2,1)S(1)}, bf16[32,256]{1,0:T(8,128)(2,1)S(1)}, u32[]{:S(2)}, u32[]{:S(2)}) collective-permute-start(bf16[32,256]{1,0:T(8,128)(2,1)S(1)} %get-tuple-element.195.q2), channel_id=1, source_target_pairs={{1,2},{3,4},{5,6},{7,8},{9,10},{11,12},{13,14},{15,16},{17,18},{19... | collective-permute-start | bytes 49160 | tf_op jit(solution)/shard_map/ppermute | solution.py:406
  30.9 4.7 %collective-permute-start.11 = (bf16[32,256]{1,0:T(8,128)(2,1)S(1)}, bf16[32,256]{1,0:T(8,128)(2,1)S(1)}, u32[]{:S(2)}, u32[]{:S(2)}) collective-permute-start(bf16[32,256]{1,0:T(8,128)(2,1)S(1)} %get-tuple-element.196.q3), channel_id=1, source_target_pairs={{0,1},{1,0},{2,3},{3,2},{4,5},{5,4},{6,7},{7,6},{8,9},{9,8},{10,11... | collective-permute-start | bytes 49160 | tf_op jit(solution)/shard_map/ppermute | solution.py:407
  36.8 8.2 %collective-permute-start.12 = (bf16[32,256]{1,0:T(8,128)(2,1)S(1)}, bf16[32,256]{1,0:T(8,128)(2,1)S(1)}, u32[]{:S(2)}, u32[]{:S(2)}) collective-permute-start(bf16[32,256]{1,0:T(8,128)(2,1)S(1)} %get-tuple-element.201), channel_id=1, source_target_pairs={{32,64},{96,128},{160,192},{224,0},{64,32},{128,96},{192,160},{0,2... | collective-permute-start | bytes 49160 | tf_op jit(solution)/shard_map/ppermute | solution.py:404
  39.4 5.6 %collective-permute-start.13 = (bf16[32,256]{1,0:T(8,128)(2,1)S(1)}, bf16[32,256]{1,0:T(8,128)(2,1)S(1)}, u32[]{:S(2)}, u32[]{:S(2)}) collective-permute-start(bf16[32,256]{1,0:T(8,128)(2,1)S(1)} %get-tuple-element.202), channel_id=1, source_target_pairs={{0,32},{32,0},{64,96},{96,64},{128,160},{160,128},{192,224},{224,1... | collective-permute-start | bytes 49160 | tf_op jit(solution)/shard_map/ppermute | solution.py:405
  39.8 5.2 %collective-permute-start.14 = (bf16[32,256]{1,0:T(8,128)(2,1)S(1)}, bf16[32,256]{1,0:T(8,128)(2,1)S(1)}, u32[]{:S(2)}, u32[]{:S(2)}) collective-permute-start(bf16[32,256]{1,0:T(8,128)(2,1)S(1)} %get-tuple-element.203), channel_id=1, source_target_pairs={{1,2},{3,4},{5,6},{7,8},{9,10},{11,12},{13,14},{15,16},{17,18},{19... | collective-permute-start | bytes 49160 | tf_op jit(solution)/shard_map/ppermute | solution.py:406
  40.2 4.9 %collective-permute-start.15 = (bf16[32,256]{1,0:T(8,128)(2,1)S(1)}, bf16[32,256]{1,0:T(8,128)(2,1)S(1)}, u32[]{:S(2)}, u32[]{:S(2)}) collective-permute-start(bf16[32,256]{1,0:T(8,128)(2,1)S(1)} %get-tuple-element.204), channel_id=1, source_target_pairs={{0,1},{1,0},{2,3},{3,2},{4,5},{5,4},{6,7},{7,6},{8,9},{9,8},{10,11... | collective-permute-start | bytes 49160 | tf_op jit(solution)/shard_map/ppermute | solution.py:407
  47.3 9.4 %collective-permute-start.16 = (bf16[32,256]{1,0:T(8,128)(2,1)S(1)}, bf16[32,256]{1,0:T(8,128)(2,1)S(1)}, u32[]{:S(2)}, u32[]{:S(2)}) collective-permute-start(bf16[32,256]{1,0:T(8,128)(2,1)S(1)} %get-tuple-element.212), channel_id=1, source_target_pairs={{32,64},{96,128},{160,192},{224,0},{64,32},{128,96},{192,160},{0,2... | collective-permute-start | bytes 49160 | tf_op jit(solution)/shard_map/ppermute | solution.py:404
  52.1 4.5 %collective-permute-start.17 = (bf16[32,256]{1,0:T(8,128)(2,1)S(1)}, bf16[32,256]{1,0:T(8,128)(2,1)S(1)}, u32[]{:S(2)}, u32[]{:S(2)}) collective-permute-start(bf16[32,256]{1,0:T(8,128)(2,1)S(1)} %get-tuple-element.213), channel_id=1, source_target_pairs={{0,32},{32,0},{64,96},{96,64},{128,160},{160,128},{192,224},{224,1... | collective-permute-start | bytes 49160 | tf_op jit(solution)/shard_map/ppermute | solution.py:405
  52.2 4.5 %collective-permute-start.18 = (bf16[32,256]{1,0:T(8,128)(2,1)S(1)}, bf16[32,256]{1,0:T(8,128)(2,1)S(1)}, u32[]{:S(2)}, u32[]{:S(2)}) collective-permute-start(bf16[32,256]{1,0:T(8,128)(2,1)S(1)} %get-tuple-element.214), channel_id=1, source_target_pairs={{1,2},{3,4},{5,6},{7,8},{9,10},{11,12},{13,14},{15,16},{17,18},{19... | collective-permute-start | bytes 49160 | tf_op jit(solution)/shard_map/ppermute | solution.py:406
  52.2 4.5 %collective-permute-start.19 = (bf16[32,256]{1,0:T(8,128)(2,1)S(1)}, bf16[32,256]{1,0:T(8,128)(2,1)S(1)}, u32[]{:S(2)}, u32[]{:S(2)}) collective-permute-start(bf16[32,256]{1,0:T(8,128)(2,1)S(1)} %get-tuple-element.215), channel_id=1, source_target_pairs={{0,1},{1,0},{2,3},{3,2},{4,5},{5,4},{6,7},{7,6},{8,9},{9,8},{10,11... | collective-permute-start | bytes 49160 | tf_op jit(solution)/shard_map/ppermute | solution.py:407
  57.9 9.3 %collective-permute-start.20 = (bf16[32,256]{1,0:T(8,128)(2,1)S(1)}, bf16[32,256]{1,0:T(8,128)(2,1)S(1)}, u32[]{:S(2)}, u32[]{:S(2)}) collective-permute-start(bf16[32,256]{1,0:T(8,128)(2,1)S(1)} %get-tuple-element.235), channel_id=1, source_target_pairs={{32,64},{96,128},{160,192},{224,0},{64,32},{128,96},{192,160},{0,2... | collective-permute-start | bytes 49160 | tf_op jit(solution)/shard_map/ppermute | solution.py:404
  61.6 5.6 %collective-permute-start.21 = (bf16[32,256]{1,0:T(8,128)(2,1)S(1)}, bf16[32,256]{1,0:T(8,128)(2,1)S(1)}, u32[]{:S(2)}, u32[]{:S(2)}) collective-permute-start(bf16[32,256]{1,0:T(8,128)(2,1)S(1)} %get-tuple-element.236), channel_id=1, source_target_pairs={{0,32},{32,0},{64,96},{96,64},{128,160},{160,128},{192,224},{224,1... | collective-permute-start | bytes 49160 | tf_op jit(solution)/shard_map/ppermute | solution.py:405
  61.6 5.6 %collective-permute-start.22 = (bf16[32,256]{1,0:T(8,128)(2,1)S(1)}, bf16[32,256]{1,0:T(8,128)(2,1)S(1)}, u32[]{:S(2)}, u32[]{:S(2)}) collective-permute-start(bf16[32,256]{1,0:T(8,128)(2,1)S(1)} %get-tuple-element.237), channel_id=1, source_target_pairs={{1,2},{3,4},{5,6},{7,8},{9,10},{11,12},{13,14},{15,16},{17,18},{19... | collective-permute-start | bytes 49160 | tf_op jit(solution)/shard_map/ppermute | solution.py:406
  61.6 5.7 %collective-permute-start.23 = (bf16[32,256]{1,0:T(8,128)(2,1)S(1)}, bf16[32,256]{1,0:T(8,128)(2,1)S(1)}, u32[]{:S(2)}, u32[]{:S(2)}) collective-permute-start(bf16[32,256]{1,0:T(8,128)(2,1)S(1)} %get-tuple-element.238), channel_id=1, source_target_pairs={{0,1},{1,0},{2,3},{3,2},{4,5},{5,4},{6,7},{7,6},{8,9},{9,8},{10,11... | collective-permute-start | bytes 49160 | tf_op jit(solution)/shard_map/ppermute | solution.py:407
  68.5 9.4 %collective-permute-start.24 = (bf16[32,256]{1,0:T(8,128)(2,1)S(1)}, bf16[32,256]{1,0:T(8,128)(2,1)S(1)}, u32[]{:S(2)}, u32[]{:S(2)}) collective-permute-start(bf16[32,256]{1,0:T(8,128)(2,1)S(1)} %get-tuple-element.261), channel_id=1, source_target_pairs={{32,64},{96,128},{160,192},{224,0},{64,32},{128,96},{192,160},{0,2... | collective-permute-start | bytes 49160 | tf_op jit(solution)/shard_map/ppermute | solution.py:404
  71.7 6.2 %collective-permute-start.25 = (bf16[32,256]{1,0:T(8,128)(2,1)S(1)}, bf16[32,256]{1,0:T(8,128)(2,1)S(1)}, u32[]{:S(2)}, u32[]{:S(2)}) collective-permute-start(bf16[32,256]{1,0:T(8,128)(2,1)S(1)} %get-tuple-element.262), channel_id=1, source_target_pairs={{0,32},{32,0},{64,96},{96,64},{128,160},{160,128},{192,224},{224,1... | collective-permute-start | bytes 49160 | tf_op jit(solution)/shard_map/ppermute | solution.py:405
  72.1 5.8 %collective-permute-start.26 = (bf16[32,256]{1,0:T(8,128)(2,1)S(1)}, bf16[32,256]{1,0:T(8,128)(2,1)S(1)}, u32[]{:S(2)}, u32[]{:S(2)}) collective-permute-start(bf16[32,256]{1,0:T(8,128)(2,1)S(1)} %get-tuple-element.263), channel_id=1, source_target_pairs={{1,2},{3,4},{5,6},{7,8},{9,10},{11,12},{13,14},{15,16},{17,18},{19... | collective-permute-start | bytes 49160 | tf_op jit(solution)/shard_map/ppermute | solution.py:406
  72.1 5.8 %collective-permute-start.27 = (bf16[32,256]{1,0:T(8,128)(2,1)S(1)}, bf16[32,256]{1,0:T(8,128)(2,1)S(1)}, u32[]{:S(2)}, u32[]{:S(2)}) collective-permute-start(bf16[32,256]{1,0:T(8,128)(2,1)S(1)} %get-tuple-element.264), channel_id=1, source_target_pairs={{0,1},{1,0},{2,3},{3,2},{4,5},{5,4},{6,7},{7,6},{8,9},{9,8},{10,11... | collective-permute-start | bytes 49160 | tf_op jit(solution)/shard_map/ppermute | solution.py:407
  79.8 5.8 %collective-permute-start.28 = (bf16[1024,256]{1,0:T(8,128)(2,1)S(1)}, bf16[1024,256]{1,0:T(8,128)(2,1)S(1)}, u32[]{:S(2)}, u32[]{:S(2)}) collective-permute-start(bf16[1024,256]{1,0:T(8,128)(2,1)S(1)} %slice_bitcast_fusion), channel_id=1, source_target_pairs={{0,1},{1,0},{2,3},{3,2},{4,5},{5,4},{6,7},{7,6},{8,9},{9,8},{10,11... | collective-permute-start | bytes 1572872 | tf_op jit(solution)/shard_map/ppermute | solution.py:413
  103.4 14.6 %all-to-all-start.1 = ((bf16[8,64,256]{2,1,0:T(8,128)(2,1)}), bf16[8,64,256]{2,1,0:T(8,128)(2,1)S(1)}, u32[]{:S(2)}, u32[]{:S(2)}) async-start(bf16[8,64,256]{2,1,0:T(8,128)(2,1)} %broadcast_in_dim.4), calls=%async_computation.1 | async-start | bytes 524288 | tf_op jit(solution)/shard_map/all_to_all | solution.py:418
  108.6 6.9 %collective-permute-start.29 = (bf16[32,256]{1,0:T(8,128)(2,1)S(1)}, bf16[32,256]{1,0:T(8,128)(2,1)S(1)}, u32[]{:S(2)}, u32[]{:S(2)}) collective-permute-start(bf16[32,256]{1,0:T(8,128)(2,1)S(1)} %get-tuple-element.293), channel_id=1, source_target_pairs={{32,64},{96,128},{160,192},{224,0},{64,32},{128,96},{192,160},{0,2... | collective-permute-start | bytes 49160 | tf_op jit(solution)/shard_map/ppermute | solution.py:404
  109.6 5.9 %collective-permute-start.30 = (bf16[32,256]{1,0:T(8,128)(2,1)S(1)}, bf16[32,256]{1,0:T(8,128)(2,1)S(1)}, u32[]{:S(2)}, u32[]{:S(2)}) collective-permute-start(bf16[32,256]{1,0:T(8,128)(2,1)S(1)} %get-tuple-element.294), channel_id=1, source_target_pairs={{0,32},{32,0},{64,96},{96,64},{128,160},{160,128},{192,224},{224,1... | collective-permute-start | bytes 49160 | tf_op jit(solution)/shard_map/ppermute | solution.py:405
  (3 other events, 9.7 us)
